TPU v7x, 32 devices: a whole 2x2x4 slice. The times are simulated.
32 devices in a mesh: batch: 4 (over y, x), seq: 8 (over z, core).
Axes of the slice: x: 2, y: 2, z: 4, core: 2. Of those that a mesh axis runs over, the one named last changes fastest.
Arguments:
- hidden_in: bfloat16 [16, 1024, 768], P('batch', 'seq'), may hold values from -6 to 6
- positions: int32 [16, 1024], P('batch', 'seq'), may hold values from 0 to 1534, as said below
- cotangent: bfloat16 [16, 1024, 768], P('batch', 'seq'), may hold values from -6 to 6
- norm_gains: float32 [2, 2, 768], replicated, may hold values from 0.5 to 1.5
- norm_biases: float32 [2, 2, 768], replicated, may hold values from -2 to 2
- w_qkv: bfloat16 [768, 896], replicated, may hold values from -0.21875 to 0.21875
- b_qkv: float32 [896], replicated, may hold values from -2 to 2
- w_q2: bfloat16 [768, 768], replicated, may hold values from -0.21875 to 0.21875
- b_q2: float32 [768], replicated, may hold values from -2 to 2
- w_out: bfloat16 [2, 768, 768], replicated, may hold values from -3 to 3
- w_up: bfloat16 [2, 768, 3072], replicated, may hold values from -0.21875 to 0.21875
- b_up: float32 [2, 3072], replicated, may hold values from -2 to 2
- w_down: bfloat16 [2, 3072, 768], replicated, may hold values from -0.109375 to 0.109375
- out_bias: float32 [2, 768], replicated, may hold values from -2 to 2
Outputs:
- hidden_out: bfloat16 [16, 1024, 768], P('batch', 'seq')
- grad_input: float32 [16, 1024, 768], P('batch', 'seq')
- grad_gains: float32 [2, 2, 768], replicated
- grad_biases: float32 [2, 2, 768], replicated
- grad_qkv: float32 [768, 896], replicated
- grad_qkv_bias: float32 [896], replicated
- grad_q2: float32 [768, 768], replicated
- grad_q2_bias: float32 [768], replicated
- grad_out: float32 [2, 768, 768], replicated
- grad_up: float32 [2, 768, 3072], replicated
- grad_up_bias: float32 [2, 3072], replicated
- grad_down: float32 [2, 3072, 768], replicated
- grad_out_bias: float32 [2, 768], replicated
Inputs may be any that keep to these rules, and one draw needn't show every extreme that they name: `positions`: in each sequence the first position is 0 and each next one exceeds the one before by 1 or 2, by 2 exactly (1023) // 2 times.
All inputs are finite; a program needn't handle non-finite values.
Results may differ from a plain program's by a relative error of at most 0.025.
Values may be sent and summed in bfloat16 or wider, within the bound.
No kernel may reach another device: no remote copies, remote signals or barrier semaphores. Data moves between devices by JAX's collectives and lax.ppermute only.
A program may use at most 256 MiB of HBM per device.

v0:
```python
from functools import partial

import jax
import jax.numpy as jnp
from jax import lax
from jax.sharding import PartitionSpec as P

ROT = 16


EPSILON = 1e-05
SCALE = 0.125
NEGATIVE = -1e30
BASE = 10000.0


def normalize(values, gain_row, offset):
    center = values - jnp.mean(values, axis=-1, keepdims=True)
    spread = jnp.mean(center * center, axis=-1, keepdims=True)
    return center * lax.rsqrt(spread + EPSILON) * gain_row + offset


def both_norms(values, gains, offsets):
    return (normalize(values, gains[0], offsets[0]), normalize(values, gains[1], offsets[1]))


def rotary_tables(positions):
    half_rot = ROT // 2
    inverse = BASE ** (-(jnp.arange(half_rot, dtype=jnp.float32) * 2.0 / ROT))
    angles = positions.astype(jnp.float32)[..., None] * inverse
    return (jnp.cos(angles), jnp.sin(angles))


def rotate(values, cosine_table, sine_table):
    half_rot = ROT // 2
    first_half = values[..., :half_rot]
    second_half = values[..., half_rot:ROT]
    return jnp.concatenate(
        [
            first_half * cosine_table - second_half * sine_table,
            second_half * cosine_table + first_half * sine_table,
            values[..., ROT:],
        ],
        axis=-1,
    )


def rotate_back(values, grads, cosine_table, sine_table):
    pullback = jax.vjp(partial(rotate, cosine_table=cosine_table, sine_table=sine_table), values)[1]
    return pullback(grads)[0]


def exact_gelu(values):
    return jax.nn.gelu(values, approximate=False)


def attend(queries, shared, first):
    seq_count, group_len, head_count, head_size = queries.shape
    length = shared.shape[1]
    key_block = min(512, length)
    block_count = (first + group_len - 1) // key_block + 1
    query_rows = first + jnp.arange(group_len, dtype=jnp.int32)

    def step(block_index, carry):
        row_top, row_total, summed = carry
        key_start = block_index * key_block
        keys_vals = lax.dynamic_slice_in_dim(shared, key_start, key_block, 1)
        scores = (
            jnp.einsum(
                "schd,skd->shck",
                queries,
                keys_vals[..., :head_size],
                preferred_element_type=jnp.float32,
            )
            * SCALE
        )
        allowed = key_start + jnp.arange(key_block, dtype=jnp.int32)[None, :] <= query_rows[:, None]
        scores = jnp.where(allowed, scores, NEGATIVE)
        new_top = jnp.maximum(row_top, jnp.max(scores, axis=-1))
        weights = jnp.exp(scores - new_top[..., None])
        factor = jnp.exp(row_top - new_top)
        row_total = row_total * factor + jnp.sum(weights, axis=-1)
        summed = summed * factor[..., None] + jnp.einsum(
            "shck,skd->shcd",
            weights.astype(jnp.bfloat16),
            keys_vals[..., head_size:],
            preferred_element_type=jnp.float32,
        )
        return (new_top, row_total, summed)

    state_shape = (seq_count, head_count, group_len)
    start_state = (
        jnp.full(state_shape, NEGATIVE, jnp.float32),
        jnp.zeros(state_shape, jnp.float32),
        jnp.zeros(state_shape + (head_size,), jnp.float32),
    )
    row_top, row_total, summed = lax.fori_loop(0, block_count, step, start_state)
    attended = jnp.transpose(summed / row_total[..., None], (0, 2, 1, 3))
    return (attended, row_top + jnp.log(row_total))


def attend_back(queries, shared, attended, log_total, grad_attended, first, buffer):
    seq_count, group_len, head_count, head_size = queries.shape
    length = shared.shape[1]
    key_block = min(512, length)
    block_count = (first + group_len - 1) // key_block + 1
    query_rows = first + jnp.arange(group_len, dtype=jnp.int32)
    row_delta = jnp.transpose(
        jnp.sum(grad_attended.astype(jnp.float32) * attended, axis=-1), (0, 2, 1)
    )

    def step(block_index, carry):
        grad_queries, buffer = carry
        key_start = block_index * key_block
        keys_vals = lax.dynamic_slice_in_dim(shared, key_start, key_block, 1)
        keys = keys_vals[..., :head_size]
        scores = (
            jnp.einsum("schd,skd->shck", queries, keys, preferred_element_type=jnp.float32) * SCALE
        )
        allowed = key_start + jnp.arange(key_block, dtype=jnp.int32)[None, :] <= query_rows[:, None]
        probs = jnp.where(allowed, jnp.exp(scores - log_total[..., None]), 0.0)
        grad_probs = jnp.einsum(
            "schd,skd->shck",
            grad_attended,
            keys_vals[..., head_size:],
            preferred_element_type=jnp.float32,
        )
        grad_scores = (probs * (grad_probs - row_delta[..., None])).astype(jnp.bfloat16)
        grad_queries = (
            grad_queries
            + jnp.einsum("shck,skd->schd", grad_scores, keys, preferred_element_type=jnp.float32)
            * SCALE
        )
        grad_keys = (
            jnp.einsum("shck,schd->skd", grad_scores, queries, preferred_element_type=jnp.float32)
            * SCALE
        )
        grad_values = jnp.einsum(
            "shck,schd->skd",
            probs.astype(jnp.bfloat16),
            grad_attended,
            preferred_element_type=jnp.float32,
        )
        previous = lax.dynamic_slice_in_dim(buffer, key_start, key_block, 1)
        buffer = lax.dynamic_update_slice_in_dim(
            buffer, previous + jnp.concatenate([grad_keys, grad_values], axis=-1), key_start, 1
        )
        return (grad_queries, buffer)

    start_state = (jnp.zeros(queries.shape, jnp.float32), buffer)
    return lax.fori_loop(0, block_count, step, start_state)


def branches(layer_in, mlp_in, queries, shared, first, w_o, w_u, b_u, w_d, bias_out):
    seq_count, group_len, width = layer_in.shape
    attended, log_total = attend(queries, shared, first)
    attended_low = attended.reshape(seq_count, group_len, width).astype(jnp.bfloat16)
    mixed_out = jnp.einsum("scd,de->sce", attended_low, w_o, preferred_element_type=jnp.float32)
    lifted = jnp.einsum("scd,df->scf", mlp_in, w_u, preferred_element_type=jnp.float32) + b_u
    active = exact_gelu(lifted).astype(jnp.bfloat16)
    down_out = jnp.einsum("scf,fd->scd", active, w_d, preferred_element_type=jnp.float32)
    return (
        layer_in + mixed_out + down_out + bias_out,
        (attended, attended_low, log_total, lifted, active),
    )


def branches_back(grad_layer, kept_state, mlp_in, queries, shared, first, w_o, w_u, w_d, buffer):
    attended, attended_low, log_total, lifted, active = kept_state
    grad_low = grad_layer.astype(jnp.bfloat16)
    grad_wout = jnp.einsum(
        "scd,sce->de", attended_low, grad_low, preferred_element_type=jnp.float32
    )
    grad_wdown = jnp.einsum("scf,sce->fe", active, grad_low, preferred_element_type=jnp.float32)
    grad_bias = jnp.sum(grad_layer, axis=(0, 1))
    grad_attended = jnp.einsum(
        "sce,de->scd", grad_low, w_o, preferred_element_type=jnp.float32
    ).astype(jnp.bfloat16)
    grad_attended = grad_attended.reshape(queries.shape)
    grad_active = jnp.einsum("sce,fe->scf", grad_low, w_d, preferred_element_type=jnp.float32)
    grad_lifted = jax.vjp(exact_gelu, lifted)[1](grad_active)[0].astype(jnp.bfloat16)
    grad_wup = jnp.einsum("scd,scf->df", mlp_in, grad_lifted, preferred_element_type=jnp.float32)
    grad_bup = jnp.sum(grad_lifted.astype(jnp.float32), axis=(0, 1))
    grad_mlp_in = jnp.einsum("scf,df->scd", grad_lifted, w_u, preferred_element_type=jnp.float32)
    grad_queries, buffer = attend_back(
        queries, shared, attended, log_total, grad_attended, first, buffer
    )
    return (
        (grad_wout, grad_wup, grad_bup, grad_wdown, grad_bias),
        grad_mlp_in,
        grad_queries,
        buffer,
    )


def reduce_grads(
    proj_weight,
    proj_bias,
    out_weight,
    up_weight,
    up_bias,
    down_weight,
    gain_grad,
    offset_grad,
    bias_grad,
):
    (
        proj_weight,
        proj_bias,
        out_weight,
        up_weight,
        up_bias,
        down_weight,
        gain_grad,
        offset_grad,
        bias_grad,
    ) = (
        lax.psum_scatter(
            proj_weight.astype(jnp.bfloat16), "seq", scatter_dimension=0, tiled=True
        ).astype(jnp.float32),
        lax.psum_scatter(
            proj_bias.astype(jnp.bfloat16), "seq", scatter_dimension=0, tiled=True
        ).astype(jnp.float32),
        lax.psum_scatter(
            out_weight.astype(jnp.bfloat16), "seq", scatter_dimension=0, tiled=True
        ).astype(jnp.float32),
        lax.psum_scatter(
            up_weight.astype(jnp.bfloat16), "seq", scatter_dimension=0, tiled=True
        ).astype(jnp.float32),
        lax.psum_scatter(
            up_bias.astype(jnp.bfloat16), "seq", scatter_dimension=0, tiled=True
        ).astype(jnp.float32),
        lax.psum_scatter(
            down_weight.astype(jnp.bfloat16), "seq", scatter_dimension=0, tiled=True
        ).astype(jnp.float32),
        lax.psum_scatter(
            gain_grad.astype(jnp.bfloat16), "seq", scatter_dimension=1, tiled=True
        ).astype(jnp.float32),
        lax.psum_scatter(
            offset_grad.astype(jnp.bfloat16), "seq", scatter_dimension=1, tiled=True
        ).astype(jnp.float32),
        lax.psum_scatter(
            bias_grad.astype(jnp.bfloat16), "seq", scatter_dimension=0, tiled=True
        ).astype(jnp.float32),
    )
    (
        proj_weight,
        proj_bias,
        out_weight,
        up_weight,
        up_bias,
        down_weight,
        gain_grad,
        offset_grad,
        bias_grad,
    ) = (
        lax.psum(proj_weight.astype(jnp.bfloat16), "batch").astype(jnp.float32),
        lax.psum(proj_bias.astype(jnp.bfloat16), "batch").astype(jnp.float32),
        lax.psum(out_weight.astype(jnp.bfloat16), "batch").astype(jnp.float32),
        lax.psum(up_weight.astype(jnp.bfloat16), "batch").astype(jnp.float32),
        lax.psum(up_bias.astype(jnp.bfloat16), "batch").astype(jnp.float32),
        lax.psum(down_weight.astype(jnp.bfloat16), "batch").astype(jnp.float32),
        lax.psum(gain_grad.astype(jnp.bfloat16), "batch").astype(jnp.float32),
        lax.psum(offset_grad.astype(jnp.bfloat16), "batch").astype(jnp.float32),
        lax.psum(bias_grad.astype(jnp.bfloat16), "batch").astype(jnp.float32),
    )
    return (
        lax.all_gather(proj_weight.astype(jnp.bfloat16), "seq", axis=0, tiled=True).astype(
            proj_weight.dtype
        ),
        lax.all_gather(proj_bias.astype(jnp.bfloat16), "seq", axis=0, tiled=True).astype(
            proj_bias.dtype
        ),
        lax.all_gather(out_weight.astype(jnp.bfloat16), "seq", axis=0, tiled=True).astype(
            out_weight.dtype
        ),
        lax.all_gather(up_weight.astype(jnp.bfloat16), "seq", axis=0, tiled=True).astype(
            up_weight.dtype
        ),
        lax.all_gather(up_bias.astype(jnp.bfloat16), "seq", axis=0, tiled=True).astype(
            up_bias.dtype
        ),
        lax.all_gather(down_weight.astype(jnp.bfloat16), "seq", axis=0, tiled=True).astype(
            down_weight.dtype
        ),
        lax.all_gather(gain_grad.astype(jnp.bfloat16), "seq", axis=1, tiled=True).astype(
            gain_grad.dtype
        ),
        lax.all_gather(offset_grad.astype(jnp.bfloat16), "seq", axis=1, tiled=True).astype(
            offset_grad.dtype
        ),
        lax.all_gather(bias_grad.astype(jnp.bfloat16), "seq", axis=0, tiled=True).astype(
            bias_grad.dtype
        ),
    )


def local(
    hidden_in,
    positions,
    cotangent,
    norm_gains,
    norm_biases,
    w_qkv,
    b_qkv,
    w_q2,
    b_q2,
    w_out,
    w_up,
    b_up,
    w_down,
    out_bias,
):
    seq_count, group_len, width = hidden_in.shape
    head_size = (w_qkv.shape[1] - width) // 2
    head_count = width // head_size
    first = lax.axis_index("seq") * group_len
    cosine_table, sine_table = rotary_tables(positions)
    head_cosine = cosine_table[:, :, None, :]
    head_sine = sine_table[:, :, None, :]
    first_in = hidden_in.astype(jnp.float32)
    attn_norm1, mlp_norm1 = both_norms(first_in, norm_gains[0], norm_biases[0])
    attn_low1 = attn_norm1.astype(jnp.bfloat16)
    mlp_low1 = mlp_norm1.astype(jnp.bfloat16)
    projected1 = (
        jnp.einsum("scd,de->sce", attn_low1, w_qkv, preferred_element_type=jnp.float32) + b_qkv
    )
    query_lin1 = projected1[..., :width].reshape(seq_count, group_len, head_count, head_size)
    key_lin = projected1[..., width : width + head_size]
    queries1 = rotate(query_lin1, head_cosine, head_sine).astype(jnp.bfloat16)
    local_kv = jnp.concatenate(
        [rotate(key_lin, cosine_table, sine_table), projected1[..., width + head_size :]], axis=-1
    ).astype(jnp.bfloat16)
    shared = lax.all_gather(local_kv, "seq", axis=1, tiled=True)
    first_out, kept_first = branches(
        first_in,
        mlp_low1,
        queries1,
        shared,
        first,
        w_out[0],
        w_up[0],
        b_up[0],
        w_down[0],
        out_bias[0],
    )
    second_in = first_out.astype(jnp.bfloat16).astype(jnp.float32)
    attn_norm2, mlp_norm2 = both_norms(second_in, norm_gains[1], norm_biases[1])
    attn_low2 = attn_norm2.astype(jnp.bfloat16)
    mlp_low2 = mlp_norm2.astype(jnp.bfloat16)
    query_lin2 = (
        jnp.einsum("scd,de->sce", attn_low2, w_q2, preferred_element_type=jnp.float32) + b_q2
    ).reshape(seq_count, group_len, head_count, head_size)
    queries2 = rotate(query_lin2, head_cosine, head_sine).astype(jnp.bfloat16)
    second_out, kept_second = branches(
        second_in,
        mlp_low2,
        queries2,
        shared,
        first,
        w_out[1],
        w_up[1],
        b_up[1],
        w_down[1],
        out_bias[1],
    )
    hidden_out = second_out.astype(jnp.bfloat16)
    grad_second = cotangent.astype(jnp.float32)
    buffer = jnp.zeros((seq_count, shared.shape[1], 2 * head_size), jnp.float32)
    grads_two, grad_mlp2, grad_q2_rot, buffer = branches_back(
        grad_second,
        kept_second,
        mlp_low2,
        queries2,
        shared,
        first,
        w_out[1],
        w_up[1],
        w_down[1],
        buffer,
    )
    grad_q2_lin = (
        rotate_back(query_lin2, grad_q2_rot, head_cosine, head_sine)
        .reshape(seq_count, group_len, width)
        .astype(jnp.bfloat16)
    )
    grad_wq2 = jnp.einsum("scd,sce->de", attn_low2, grad_q2_lin, preferred_element_type=jnp.float32)
    grad_bq2 = jnp.sum(grad_q2_lin.astype(jnp.float32), axis=(0, 1))
    grad_attn2 = jnp.einsum("sce,de->scd", grad_q2_lin, w_q2, preferred_element_type=jnp.float32)
    norm_pull2 = jax.vjp(both_norms, second_in, norm_gains[1], norm_biases[1])[1]
    grad_in2, grad_gain2, grad_offset2 = norm_pull2((grad_attn2, grad_mlp2))
    grad_in2 = grad_in2 + grad_second
    summed_two = reduce_grads(
        grad_wq2,
        grad_bq2,
        grads_two[0],
        grads_two[1],
        grads_two[2],
        grads_two[3],
        grad_gain2,
        grad_offset2,
        grads_two[4],
    )
    grad_first = grad_in2.astype(jnp.bfloat16).astype(jnp.float32)
    grads_one, grad_mlp1, grad_q1_rot, buffer = branches_back(
        grad_first,
        kept_first,
        mlp_low1,
        queries1,
        shared,
        first,
        w_out[0],
        w_up[0],
        w_down[0],
        buffer,
    )
    grad_kv = lax.psum_scatter(
        buffer.astype(jnp.bfloat16), "seq", scatter_dimension=1, tiled=True
    ).astype(jnp.float32)
    grad_q1_lin = rotate_back(query_lin1, grad_q1_rot, head_cosine, head_sine).reshape(
        seq_count, group_len, width
    )
    grad_key_lin = rotate_back(key_lin, grad_kv[..., :head_size], cosine_table, sine_table)
    grad_proj1 = jnp.concatenate(
        [grad_q1_lin, grad_key_lin, grad_kv[..., head_size:]], axis=-1
    ).astype(jnp.bfloat16)
    grad_wqkv = jnp.einsum("scd,sce->de", attn_low1, grad_proj1, preferred_element_type=jnp.float32)
    grad_bqkv = jnp.sum(grad_proj1.astype(jnp.float32), axis=(0, 1))
    grad_attn1 = jnp.einsum("sce,de->scd", grad_proj1, w_qkv, preferred_element_type=jnp.float32)
    norm_pull1 = jax.vjp(both_norms, first_in, norm_gains[0], norm_biases[0])[1]
    grad_in1, grad_gain1, grad_offset1 = norm_pull1((grad_attn1, grad_mlp1))
    grad_input = grad_in1 + grad_first
    summed_one = reduce_grads(
        grad_wqkv,
        grad_bqkv,
        grads_one[0],
        grads_one[1],
        grads_one[2],
        grads_one[3],
        grad_gain1,
        grad_offset1,
        grads_one[4],
    )
    grad_gains = jnp.stack([summed_one[6], summed_two[6]])
    grad_biases = jnp.stack([summed_one[7], summed_two[7]])
    grad_out = jnp.stack([summed_one[2], summed_two[2]])
    grad_up = jnp.stack([summed_one[3], summed_two[3]])
    grad_up_bias = jnp.stack([summed_one[4], summed_two[4]])
    grad_down = jnp.stack([summed_one[5], summed_two[5]])
    grad_out_bias = jnp.stack([summed_one[8], summed_two[8]])
    return (
        hidden_out,
        grad_input,
        grad_gains,
        grad_biases,
        summed_one[0],
        summed_one[1],
        summed_two[0],
        summed_two[1],
        grad_out,
        grad_up,
        grad_up_bias,
        grad_down,
        grad_out_bias,
    )


def solution(mesh):
    return jax.shard_map(
        local,
        mesh=mesh,
        in_specs=(
            P("batch", "seq", None),
            P("batch", "seq"),
            P("batch", "seq", None),
            P(),
            P(),
            P(),
            P(),
            P(),
            P(),
            P(),
            P(),
            P(),
            P(),
            P(),
        ),
        out_specs=(
            P("batch", "seq", None),
            P("batch", "seq", None),
            P(),
            P(),
            P(),
            P(),
            P(),
            P(),
            P(),
            P(),
            P(),
            P(),
            P(),
        ),
        check_vma=False,
    )
```

profile of v0, /device:TPU:0, one launch (start us, length us, event | category | flops | bytes accessed | tf_op | source)
XLA Modules:
  0.0 1260.2 jit_solution(4374170989422659431)
XLA Ops:
  24.6 15.5 %multiply_convert_fusion.1 = (bf16[4,128,3072]{2,1,0:T(8,128)(2,1)}, f32[4,128,3072]{2,1,0:T(8,128)}) fusion(f32[4,128,3072]{2,1,0:T(8,128)S(1)} %get-tuple-element.632, f32[3072]{0:T(1024)S(1)} %bitcast.436, u8[128,3072]{1,0:T(8,128)(4,1)S(1)} %get-tuple-element.456, u8[128,3072]{1,0:T(8,128)(4,1)S(1)} %get-tuple-element.455), kind=kLoop, calls=%fused_computation.130 | loop fusion | flops 111673344 | bytes 16527360 | tf_op jit(solution)/shard_map/convert_element_type | solution.py:160
  58.2 17.1 %while.56 = (s32[]{:T(128)}, f32[4,12,128]{2,1,0:T(8,128)S(1)}, f32[4,12,128]{2,1,0:T(8,128)S(1)}, f32[4,12,128,64]{2,3,1,0:T(8,128)}, s32[]{:T(128)}, /*index=5...) while((s32[]{:T(128)}, f32[4,12,128]{2,1,0:T(8,128)S(1)}, ...), condition=%wide.region_5.6_spmd.clone, body=%wide.region_2.5_spmd.clone.sunk | while | flops 840774272 | bytes 93197544 | solution.py:97
  87.9 16.2 %while.57 = (s32[]{:T(128)}, f32[4,12,128]{2,1,0:T(8,128)S(1)}, f32[4,12,128]{2,1,0:T(8,128)S(1)}, f32[4,12,128,64]{2,3,1,0:T(8,128)}, s32[]{:T(128)}, /*index=5...) while((s32[]{:T(128)}, f32[4,12,128]{2,1,0:T(8,128)S(1)}, ...), condition=%wide.region_11.12_spmd.clone, body=%wide.region_8.11_spmd.clone.sunk | while | flops 840774272 | bytes 93213928 | solution.py:97
  109.0 32.0 %while.58 = (s32[]{:T(128)}, f32[4,128,12,64]{1,3,2,0:T(8,128)}, f32[4,1024,128]{1,2,0:T(8,128)}, s32[]{:T(128)}, bf16[4,1024,128]{1,2,0:T(8,128)(2,1)S(1)}, /*i...) while((s32[]{:T(128)}, f32[4,128,12,64]{1,3,2,0:T(8,128)}, ...), condition=%wide.region_16.17_spmd.clone, body=%wide.region_15.16_spmd.clone.sunk | while | flops 2046231168 | bytes 143684912 | solution.py:151
  150.4 15.7 %multiply_convert_fusion = (bf16[4,128,3072]{2,1,0:T(8,128)(2,1)}, f32[4,128,3072]{2,1,0:T(8,128)S(1)}) fusion(f32[4,128,3072]{2,1,0:T(8,128)S(1)} %get-tuple-element.635, f32[3072]{0:T(1024)S(1)} %bitcast.439, u8[128,3072]{1,0:T(8,128)(4,1)S(1)} %get-tuple-element.454, u8[128,3072]{1,0:T(8,128)(4,1)S(1)} %get-tuple-element.453), kind=kLoop, calls=%fused_computation.117 | loop fusion | flops 111673344 | bytes 16527360 | tf_op jit(solution)/shard_map/convert_element_type | solution.py:160
  194.3 32.0 %while.59 = (s32[]{:T(128)}, f32[4,128,12,64]{1,3,2,0:T(8,128)}, f32[4,1024,128]{1,2,0:T(8,128)}, s32[]{:T(128)}, bf16[4,1024,128]{1,2,0:T(8,128)(2,1)S(1)}, /*i...) while((s32[]{:T(128)}, f32[4,128,12,64]{1,3,2,0:T(8,128)}, ...), condition=%wide.region_23.24_spmd.clone, body=%wide.region_22.23_spmd.clone.sunk | while | flops 2046231168 | bytes 143684912 | solution.py:151
  248.0 113.7 %reduce-scatter.40.cloned.1.call-done = bf16[128,512]{1,0:T(8,128)(2,1)} async-done(((bf16[1024,512]{1,0:T(8,128)(2,1)}), bf16[128,512]{1,0:T(8,128)(2,1)}) %reduce-scatter.40.cloned.1.call-update) | async-done | bytes 131088
  404.0 24.7 %reduce-scatter.26.cloned.1.call-done = bf16[96,768]{1,0:T(8,128)(2,1)} async-done(((bf16[768,768]{1,0:T(8,128)(2,1)}), bf16[96,768]{1,0:T(8,128)(2,1)}) %reduce-scatter.26.cloned.1.call-update) | async-done | bytes 147472 | tf_op jit(solution)/shard_map/reduce_scatter | solution.py:218
  428.7 33.2 %reduce-scatter.30.cloned.1.call-done = bf16[96,768]{1,0:T(8,128)(2,1)} async-done(((bf16[768,768]{1,0:T(8,128)(2,1)}), bf16[96,768]{1,0:T(8,128)(2,1)}) %reduce-scatter.30.cloned.1.call-update) | async-done | bytes 147472 | tf_op jit(solution)/shard_map/reduce_scatter | solution.py:224
  461.9 34.4 %reduce-scatter.24.cloned.1.call-done = bf16[96,896]{1,0:T(8,128)(2,1)} async-done(((bf16[768,896]{1,0:T(8,128)(2,1)}), bf16[96,896]{1,0:T(8,128)(2,1)}) %reduce-scatter.24.cloned.1.call-update) | async-done | bytes 172048 | tf_op jit(solution)/shard_map/reduce_scatter | solution.py:218
  496.3 56.3 %reduce-scatter.34.cloned.1.call-done = bf16[96,3072]{1,0:T(8,128)(2,1)} async-done(((bf16[768,3072]{1,0:T(8,128)(2,1)}), bf16[96,3072]{1,0:T(8,128)(2,1)}) %reduce-scatter.34.cloned.1.call-update) | async-done | bytes 589840 | tf_op jit(solution)/shard_map/reduce_scatter | solution.py:227
  552.6 55.8 %reduce-scatter.36.cloned.1.call-done = bf16[384,768]{1,0:T(8,128)(2,1)} async-done(((bf16[3072,768]{1,0:T(8,128)(2,1)}), bf16[384,768]{1,0:T(8,128)(2,1)}) %reduce-scatter.36.cloned.1.call-update) | async-done | bytes 589840 | tf_op jit(solution)/shard_map/reduce_scatter | solution.py:233
  608.4 56.3 %reduce-scatter.32.cloned.1.call-done = bf16[96,3072]{1,0:T(8,128)(2,1)} async-done(((bf16[768,3072]{1,0:T(8,128)(2,1)}), bf16[96,3072]{1,0:T(8,128)(2,1)}) %reduce-scatter.32.cloned.1.call-update) | async-done | bytes 589840 | tf_op jit(solution)/shard_map/reduce_scatter | solution.py:227
  664.7 56.2 %reduce-scatter.38.cloned.1.call-done = bf16[384,768]{1,0:T(8,128)(2,1)} async-done(((bf16[3072,768]{1,0:T(8,128)(2,1)}), bf16[384,768]{1,0:T(8,128)(2,1)}) %reduce-scatter.38.cloned.1.call-update) | async-done | bytes 589840 | tf_op jit(solution)/shard_map/reduce_scatter | solution.py:233
  736.6 73.0 %all-reduce.34.cloned.1.call-done = (bf16[96,896]{1,0:T(8,128)(2,1)}, bf16[96,768]{1,0:T(8,128)(2,1)}, bf16[96,768]{1,0:T(8,128)(2,1)}, bf16[96,768]{1,0:T(8,128...) async-done(((bf16[96,896]{1,0:T(8,128)(2,1)}, bf16[96,768]{1,0:T(8,128)(2,1)}, ...) | async-done | bytes 2973712 | tf_op jit(solution)/shard_map/psum | solution.py:257
  826.2 16.6 %reduce-scatter.48.cloned.1.call-done = bf16[96,2]{1,0:T(8,128)(2,1)} async-done(((bf16[768,2]{1,0:T(8,128)(2,1)}), bf16[96,2]{1,0:T(8,128)(2,1)}) %reduce-scatter.48.cloned.1.call-update) | async-done | bytes 400
  843.6 30.4 %reduce-scatter.44.cloned.1.call-done = bf16[96,2]{1,0:T(8,128)(2,1)} async-done(((bf16[768,2]{1,0:T(8,128)(2,1)}), bf16[96,2]{1,0:T(8,128)(2,1)}) %reduce-scatter.44.cloned.1.call-update) | async-done | bytes 400
  876.2 14.0 %all-reduce.28 = (bf16[896]{0:T(1024)(128)(2,1)S(1)}, bf16[768]{0:T(1024)(128)(2,1)S(1)}, bf16[768]{0:T(1024)(128)(2,1)S(1)}, bf16[768]{0:T(1024)(128)(2,1)S(1)}) all-reduce(bf16[896]{0:T(1024)(128)(2,1)S(1)} %fusion.204, bf16[768]{0:T(1024)(128)(2,1)S(1)} %reduce_sum.340, ...), channel_id=8, replica_groups=mesh['batch'=4,'seq'=8] {'seq'}, use_global_device_ids=true, to_apply=%region_46.47.clone | all-reduce | flops 3200 | bytes 12800
  890.5 10.1 all-reduce.30
  901.4 26.0 %all-reduce.27 = (bf16[896]{0:T(1024)(128)(2,1)S(1)}, bf16[768]{0:T(1024)(128)(2,1)S(1)}, bf16[3072]{0:T(1024)(128)(2,1)S(1)}, bf16[3072]{0:T(1024)(128)(2,1)S(1...) all-reduce(bf16[896]{0:T(1024)(128)(2,1)S(1)} %dynamic-update-slice, ...), channel_id=1, replica_groups=mesh['batch'=4,'seq'=8] {'seq'}, use_global_device_ids=true, to_apply=%add.17 | all-reduce | flops 9344 | bytes 37376
  936.7 9.8 all-reduce.29
  955.0 10.3 all-gather.3
  974.1 10.1 all-gather.1
  984.4 12.7 %all-gather.4 = bf16[8,1,384]{2,1,0:T(2,128)(2,1)S(1)} all-gather(bf16[1,1,384]{2,1,0:T(2,128)(2,1)S(1)} %reshape.242), channel_id=1, replica_groups=mesh['batch'=4,'seq'=8] {'seq'}, dimensions={0}, use_global_device_ids=true | all-gather | bytes 6912 | tf_op jit(solution)/shard_map/all_gather | solution.py:280
  997.1 12.7 %all-gather.5 = bf16[8,1,384]{2,1,0:T(2,128)(2,1)S(1)} all-gather(bf16[1,1,384]{2,1,0:T(2,128)(2,1)S(1)} %reshape.244), channel_id=1, replica_groups=mesh['batch'=4,'seq'=8] {'seq'}, dimensions={0}, use_global_device_ids=true | all-gather | bytes 6912 | tf_op jit(solution)/shard_map/all_gather | solution.py:280
  1018.6 13.3 %all-gather.18.cloned.1.call-done = bf16[768,896]{1,0:T(8,128)(2,1)} async-done(((bf16[96,896]{1,0:T(8,128)(2,1)}), bf16[768,896]{1,0:T(8,128)(2,1)}) %all-gather.18.cloned.1.call-update) | async-done | bytes 1376272 | tf_op jit(solution)/shard_map/all_gather | solution.py:268
  1035.0 49.5 %all-gather.30.cloned.1.call-done = bf16[3072,768]{1,0:T(8,128)(2,1)} async-done(((bf16[384,768]{1,0:T(8,128)(2,1)}), bf16[3072,768]{1,0:T(8,128)(2,1)}) %all-gather.30.cloned.1.call-update) | async-done | bytes 4718608 | tf_op jit(solution)/shard_map/all_gather | solution.py:283
  1084.5 52.3 %all-gather.32.cloned.1.call-done = bf16[3072,768]{1,0:T(8,128)(2,1)} async-done(((bf16[384,768]{1,0:T(8,128)(2,1)}), bf16[3072,768]{1,0:T(8,128)(2,1)}) %all-gather.32.cloned.1.call-update) | async-done | bytes 4718608 | tf_op jit(solution)/shard_map/all_gather | solution.py:283
  1136.8 12.0 maximum_convert_fusion.1
  1148.8 40.3 %all-gather.26.cloned.1.call-done = bf16[768,3072]{1,0:T(8,128)(2,1)} async-done(((bf16[96,3072]{1,0:T(8,128)(2,1)}), bf16[768,3072]{1,0:T(8,128)(2,1)}) %all-gather.26.cloned.1.call-update) | async-done | bytes 4718608 | tf_op jit(solution)/shard_map/all_gather | solution.py:277
  1189.1 52.3 %all-gather.28.cloned.1.call-done = bf16[768,3072]{1,0:T(8,128)(2,1)} async-done(((bf16[96,3072]{1,0:T(8,128)(2,1)}), bf16[768,3072]{1,0:T(8,128)(2,1)}) %all-gather.28.cloned.1.call-update) | async-done | bytes 4718608 | tf_op jit(solution)/shard_map/all_gather | solution.py:277
  1241.4 11.8 maximum_convert_fusion
  (426 shorter events, 321.0 us)
Async XLA Ops:
  7.2 49.7 %all-gather.16.cloned.1.call-start = ((), (), s32[]{:S(2)}) async-start(), calls=%async_computation.13 | async-start | bytes 1179648 | tf_op jit(solution)/shard_map/all_gather | solution.py:334
  16.9 344.7 %reduce-scatter.40.cloned.1.call-start = ((), (), s32[]{:S(2)}) async-start(), calls=%async_computation.30 | async-start | bytes 1179648
  230.1 173.9 %reduce-scatter.28.cloned.1.call-start = ((), (), s32[]{:S(2)}) async-start(), calls=%async_computation.18 | async-start | bytes 1327104 | tf_op jit(solution)/shard_map/reduce_scatter | solution.py:224
  233.1 195.6 %reduce-scatter.26.cloned.1.call-start = ((), (), s32[]{:S(2)}) async-start(), calls=%async_computation.16 | async-start | bytes 1327104 | tf_op jit(solution)/shard_map/reduce_scatter | solution.py:218
  236.4 225.5 %reduce-scatter.30.cloned.1.call-start = ((), (), s32[]{:S(2)}) async-start(), calls=%async_computation.20 | async-start | bytes 1327104 | tf_op jit(solution)/shard_map/reduce_scatter | solution.py:224
  242.0 254.3 %reduce-scatter.24.cloned.1.call-start = ((), (), s32[]{:S(2)}) async-start(), calls=%async_computation.14 | async-start | bytes 1548288 | tf_op jit(solution)/shard_map/reduce_scatter | solution.py:218
  243.5 119.5 %copy-start.65 = (f32[4,128]{1,0:T(4,128)S(1)}, f32[4,128]{1,0:T(4,128)}, u32[]{:S(2)}) copy-start(f32[4,128]{1,0:T(4,128)} %copy-done.64) | copy-start | bytes 6148
  243.5 119.5 %copy-start.85 = (f32[8]{0:T(128)S(1)}, f32[8]{0:T(128)}, u32[]{:S(2)}) copy-start(f32[8]{0:T(128)} %copy-done.84) | copy-start | bytes 100
  244.6 118.7 %copy-start.11 = (bf16[4,128,768]{2,1,0:T(8,128)(2,1)S(1)}, bf16[4,128,768]{2,1,0:T(8,128)(2,1)}, u32[]{:S(2)}) copy-start(bf16[4,128,768]{2,1,0:T(8,128)(2,1)} %param.22) | copy-start | bytes 2359300
  244.6 118.7 %copy-start.45 = (f32[768]{0:T(1024)S(1)}, f32[768]{0:T(1024)}, u32[]{:S(2)}) copy-start(f32[768]{0:T(1024)} %copy-done.44) | copy-start | bytes 9220
  244.6 118.7 %copy-start.52 = (f32[4,128]{1,0:T(4,128)S(1)}, f32[4,128]{1,0:T(4,128)}, u32[]{:S(2)}) copy-start(f32[4,128]{1,0:T(4,128)} %copy-done.51) | copy-start | bytes 6148
  366.8 185.9 %reduce-scatter.34.cloned.1.call-start = ((), (), s32[]{:S(2)}) async-start(), calls=%async_computation.24 | async-start | bytes 5308416 | tf_op jit(solution)/shard_map/reduce_scatter | solution.py:227
  373.4 235.0 %reduce-scatter.36.cloned.1.call-start = ((), (), s32[]{:S(2)}) async-start(), calls=%async_computation.26 | async-start | bytes 5308416 | tf_op jit(solution)/shard_map/reduce_scatter | solution.py:233
  380.5 284.3 %reduce-scatter.32.cloned.1.call-start = ((), (), s32[]{:S(2)}) async-start(), calls=%async_computation.22 | async-start | bytes 5308416 | tf_op jit(solution)/shard_map/reduce_scatter | solution.py:227
  396.9 324.0 %reduce-scatter.38.cloned.1.call-start = ((), (), s32[]{:S(2)}) async-start(), calls=%async_computation.28 | async-start | bytes 5308416 | tf_op jit(solution)/shard_map/reduce_scatter | solution.py:233
  403.9 317.1 %copy-start.83 = (f32[768]{0:T(1024)S(1)}, f32[768]{0:T(1024)}, u32[]{:S(2)}) copy-start(f32[768]{0:T(1024)} %get-tuple-element.616) | copy-start | bytes 9220
  403.9 317.2 %copy-start.82 = (f32[768]{0:T(1024)S(1)}, f32[768]{0:T(1024)}, u32[]{:S(2)}) copy-start(f32[768]{0:T(1024)} %get-tuple-element.471) | copy-start | bytes 9220
  403.9 318.0 %copy-start.67 = (f32[768]{0:T(1024)S(1)}, f32[768]{0:T(1024)}, u32[]{:S(2)}) copy-start(f32[768]{0:T(1024)} %get-tuple-element.461) | copy-start | bytes 9220
  403.9 318.0 %copy-start.66 = (f32[768]{0:T(1024)S(1)}, f32[768]{0:T(1024)}, u32[]{:S(2)}) copy-start(f32[768]{0:T(1024)} %get-tuple-element.476) | copy-start | bytes 9220
  403.9 405.7 %all-reduce.34.cloned.1.call-start = ((), (), s32[]{:S(2)}) async-start(), calls=%async_computation.35 | async-start | bytes 5947392 | tf_op jit(solution)/shard_map/psum | solution.py:257
  720.9 121.8 %reduce-scatter.48.cloned.1.call-start = ((), (), s32[]{:S(2)}) async-start(), calls=%async_computation.34 | async-start | bytes 221184
  729.0 145.0 %reduce-scatter.44.cloned.1.call-start = ((), (), s32[]{:S(2)}) async-start(), calls=%async_computation.32 | async-start | bytes 221184
  730.0 202.9 %reduce-scatter.46.cloned.1.call-start = ((), (), s32[]{:S(2)}) async-start(), calls=%async_computation.33 | async-start | bytes 221184
  735.6 200.3 %reduce-scatter.42.cloned.1.call-start = ((), (), s32[]{:S(2)}) async-start(), calls=%async_computation.31 | async-start | bytes 221184
  736.5 275.1 %all-gather.20.cloned.1.call-start = ((), (), s32[]{:S(2)}) async-start(), calls=%async_computation.17 | async-start | bytes 1327104 | tf_op jit(solution)/shard_map/all_gather | solution.py:268
  809.7 204.8 %all-gather.22.cloned.1.call-start = ((), (), s32[]{:S(2)}) async-start(), calls=%async_computation.19 | async-start | bytes 1327104 | tf_op jit(solution)/shard_map/all_gather | solution.py:274
  810.2 204.2 %all-gather.24.cloned.1.call-start = ((), (), s32[]{:S(2)}) async-start(), calls=%async_computation.21 | async-start | bytes 1327104 | tf_op jit(solution)/shard_map/all_gather | solution.py:274
  810.8 221.1 %all-gather.18.cloned.1.call-start = ((), (), s32[]{:S(2)}) async-start(), calls=%async_computation.15 | async-start | bytes 1548288 | tf_op jit(solution)/shard_map/all_gather | solution.py:268
  811.6 272.9 %all-gather.30.cloned.1.call-start = ((), (), s32[]{:S(2)}) async-start(), calls=%async_computation.27 | async-start | bytes 5308416 | tf_op jit(solution)/shard_map/all_gather | solution.py:283
  812.2 324.6 %all-gather.32.cloned.1.call-start = ((), (), s32[]{:S(2)}) async-start(), calls=%async_computation.29 | async-start | bytes 5308416 | tf_op jit(solution)/shard_map/all_gather | solution.py:283
  812.9 376.2 %all-gather.26.cloned.1.call-start = ((), (), s32[]{:S(2)}) async-start(), calls=%async_computation.23 | async-start | bytes 5308416 | tf_op jit(solution)/shard_map/all_gather | solution.py:277
  813.6 427.7 %all-gather.28.cloned.1.call-start = ((), (), s32[]{:S(2)}) async-start(), calls=%async_computation.25 | async-start | bytes 5308416 | tf_op jit(solution)/shard_map/all_gather | solution.py:277
  (83 other events, 1262.5 us)
Sparse Core Ops, SparseCore 0:
  17.1 26.6 all-gather.15
  230.2 131.4 reduce-scatter.39
  364.0 30.8 reduce-scatter.27
  397.6 31.0 reduce-scatter.25
  430.8 31.0 reduce-scatter.29
  464.7 31.6 reduce-scatter.23
  499.3 53.3 reduce-scatter.33
  555.1 53.3 reduce-scatter.35
  611.4 53.3 reduce-scatter.31
  667.6 53.3 reduce-scatter.37
  725.4 84.1 all-reduce.33
  812.4 30.3 reduce-scatter.47
  845.6 28.3 reduce-scatter.43
  876.2 28.4 reduce-scatter.45
  907.4 28.4 reduce-scatter.41
  937.5 20.8 all-gather.19
  960.0 22.2 all-gather.21
  983.8 22.4 all-gather.23
  1008.1 23.8 all-gather.17
  1033.5 50.9 all-gather.29
  1086.2 50.5 all-gather.31
  1138.5 50.5 all-gather.25
  1190.8 50.5 all-gather.27
where the time goes:
time: 1270 us; the launch traced here: 1260 us
  waiting for transfers between devices  765 us (60%)
  matrix products  187 us (15%)
  blocking collectives  123 us (10%)
  other arithmetic  113 us (9%)
  local copies, waits for them, and re-layouts  51.4 us (4%)
  between operations  19 us (1%)
    unnamed x28, waiting for transfers between devices  167 us
    reduce_scatter x2, waiting for transfers between devices, reduce_grads(): lax.psum_scatter(up_weight.astype(jnp.bfloat16), 'seq', scatter_dimension...  113 us
    reduce_scatter x2, waiting for transfers between devices, reduce_grads(): lax.psum_scatter(down_weight.astype(jnp.bfloat16), 'seq', scatter_dimensi...  112 us
    all_gather x2, waiting for transfers between devices, reduce_grads(): lax.all_gather(down_weight.astype(jnp.bfloat16), 'seq', axis=0, tiled=True)  102 us
    all_gather x2, waiting for transfers between devices, reduce_grads(): lax.all_gather(up_weight.astype(jnp.bfloat16), 'seq', axis=0, tiled=True)  92.6 us
    psum x1, waiting for transfers between devices, reduce_grads(): lax.psum(proj_weight.astype(jnp.bfloat16), 'batch').astype(jnp.float32)  73 us
    reduce_scatter x2, waiting for transfers between devices, reduce_grads(): lax.psum_scatter(proj_weight.astype(jnp.bfloat16), 'seq', scatter_dimensi...  59.1 us
    unnamed x2, blocking collectives  40 us
  transfers between devices with their start and end apart: 23, of which 17 were waited for; matrix products, arithmetic and copies ran while one was open for 12% of the time, Pallas kernels for 0%

commit v1 on v0

v1 whole, which is shorter than its diff:
```python
from functools import partial

import jax
import jax.numpy as jnp
from jax import lax
from jax.experimental import pallas as pl
from jax.experimental.pallas import tpu as pltpu
from jax.sharding import PartitionSpec as P

ROT = 16
EPSILON = 1e-05
SCALE = 0.125
NEGATIVE = -1e30
BASE = 10000.0

B = ("b0", "b1")
Z = "z"
C = "c"
TILE = 768
UNIT = 96
KB = 256

f32 = jnp.float32
bf16 = jnp.bfloat16


def dot_nn(a, b):
    return lax.dot_general(a, b, (((1,), (0,)), ((), ())), preferred_element_type=f32)


def dot_nt(a, b):
    return lax.dot_general(a, b, (((1,), (1,)), ((), ())), preferred_element_type=f32)


def dot_tn(a, b):
    return lax.dot_general(a, b, (((0,), (0,)), ((), ())), preferred_element_type=f32)


def params(limit=50):
    return pltpu.CompilerParams(vmem_limit_bytes=limit << 20)


def cost(flops, moved, transcendentals=0):
    return pl.CostEstimate(
        flops=int(flops), bytes_accessed=int(moved), transcendentals=int(transcendentals)
    )


def vmem(count):
    return [pl.BlockSpec(memory_space=pltpu.VMEM)] * count


def unit_rows(values):
    center = values - jnp.mean(values, axis=-1, keepdims=True)
    spread = jnp.mean(center * center, axis=-1, keepdims=True)
    inverse = lax.rsqrt(spread + EPSILON)
    return center * inverse, inverse


def turn(values, cos_tab, sin_low, sin_high):
    return (
        values * cos_tab
        + pltpu.roll(values, 120, 1) * sin_low
        + pltpu.roll(values, 8, 1) * sin_high
    )


def pairs_down(values):
    return jnp.concatenate(
        [values[:, p * 128 : (p + 1) * 128] for p in range(values.shape[1] // 128)], axis=0
    )


def gelu_parts(lifted):
    cdf = 0.5 * (1.0 + lax.erf(lifted * 0.7071067811865476))
    slope = cdf + lifted * (0.3989422804014327 * jnp.exp(-0.5 * lifted * lifted))
    return lifted * cdf, slope


def first_kernel(x_ref, gain_ref, off_ref, w_ref, b_ref, tab_ref, na_ref, nm_ref, q_ref, kv_ref):
    tokens, width = x_ref.shape
    unit = unit_rows(x_ref[...].astype(f32))[0]
    norm_a = (unit * gain_ref[0:1] + off_ref[0:1]).astype(bf16)
    na_ref[...] = norm_a
    nm_ref[...] = (unit * gain_ref[1:2] + off_ref[1:2]).astype(bf16)
    cos_tab, sin_low, sin_high = tab_ref[0], tab_ref[1], tab_ref[2]
    kv = dot_nn(norm_a, w_ref[:, width:]) + b_ref[:, width:]
    low_half = lax.broadcasted_iota(jnp.int32, kv.shape, 1) < 64
    kv = jnp.where(low_half, turn(kv, cos_tab, sin_low, sin_high), kv).astype(bf16)
    group = kv_ref.shape[0]
    for s in range(tokens // group):
        kv_ref[:, s * 128 : (s + 1) * 128] = kv[s * group : (s + 1) * group]
    proj = dot_nn(norm_a, w_ref[:, :width]) + b_ref[:, :width]
    for p in range(width // 128):
        cols = slice(p * 128, (p + 1) * 128)
        q_ref[:, cols] = (turn(proj[:, cols], cos_tab, sin_low, sin_high) * SCALE).astype(bf16)


def first_call(x, gains, offs, w_qkv, b_qkv, tab, group):
    tokens, width = x.shape
    shape = lambda *s: jax.ShapeDtypeStruct(s, bf16)
    return pl.pallas_call(
        first_kernel,
        out_shape=[
            shape(tokens, width),
            shape(tokens, width),
            shape(tokens, width),
            shape(group, tokens // group * 128),
        ],
        in_specs=vmem(6),
        out_specs=vmem(4),
        compiler_params=params(),
        cost_estimate=cost(2 * tokens * width * (width + 128), 6 << 20),
        name="first",
    )(x, gains, offs, w_qkv, b_qkv.reshape(1, -1), tab)


def mlp_fwd_kernel(nm_ref, up_ref, bup_ref, down_ref, y_ref, act_ref, slope_ref):
    lifted = dot_nn(nm_ref[...], up_ref[0]) + bup_ref[...]
    active, slope = gelu_parts(lifted)
    active = active.astype(bf16)
    act_ref[...] = active
    slope_ref[...] = slope.astype(bf16)

    @pl.when(pl.program_id(0) == 0)
    def _():
        y_ref[...] = jnp.zeros_like(y_ref)

    y_ref[...] += dot_nn(active, down_ref[0])


def mlp_fwd_call(nm, w_up, b_up, w_down, layer):
    tokens, width = nm.shape
    hidden = w_up.shape[2]
    return pl.pallas_call(
        mlp_fwd_kernel,
        grid=(hidden // TILE,),
        in_specs=[
            pl.BlockSpec((tokens, width), lambda t: (0, 0)),
            pl.BlockSpec((1, width, TILE), lambda t: (layer, 0, t)),
            pl.BlockSpec((1, TILE), lambda t: (0, t)),
            pl.BlockSpec((1, TILE, width), lambda t: (layer, t, 0)),
        ],
        out_specs=[
            pl.BlockSpec((tokens, width), lambda t: (0, 0)),
            pl.BlockSpec((tokens, TILE), lambda t: (0, t)),
            pl.BlockSpec((tokens, TILE), lambda t: (0, t)),
        ],
        out_shape=[
            jax.ShapeDtypeStruct((tokens, width), f32),
            jax.ShapeDtypeStruct((tokens, hidden), bf16),
            jax.ShapeDtypeStruct((tokens, hidden), bf16),
        ],
        compiler_params=params(),
        cost_estimate=cost(4 * tokens * width * hidden, 20 << 20, tokens * hidden),
        name="mlp_fwd",
    )(nm, w_up, b_up[layer : layer + 1], w_down)


def mlp_grads(active, slope, nm, grad, up, down, refs, core):
    grad_norm_ref, send_ref, keep_ref, bias_ref = refs
    step = pl.program_id(0)
    half = pl.num_programs(0) // 2
    grad_active = dot_nt(grad, down)
    grad_lifted_wide = grad_active * slope
    grad_lifted = grad_lifted_wide.astype(bf16)
    bias_ref[...] = jnp.sum(grad_lifted.astype(f32), axis=0, keepdims=True)

    @pl.when(step == 0)
    def _():
        grad_norm_ref[...] = jnp.zeros_like(grad_norm_ref)

    grad_norm_ref[...] += dot_nt(grad_lifted, up)
    grad_down = dot_tn(active, grad).astype(bf16)
    grad_up = dot_tn(nm, grad_lifted).astype(bf16)

    def put(ref):
        for j in range(TILE // UNIT):
            rows = slice(j * UNIT, (j + 1) * UNIT)
            ref[0, 2 * j * UNIT : (2 * j + 1) * UNIT] = grad_down[rows]
            ref[0, (2 * j + 1) * UNIT : (2 * j + 2) * UNIT] = grad_up[rows]

    @pl.when(step < half)
    def _():
        put(send_ref)

    @pl.when(step >= half)
    def _():
        put(keep_ref)


def mlp_both_kernel(
    core_ref, nm_ref, g_ref, up_ref, bup_ref, down_ref, y_ref, grad_norm_ref, send_ref, keep_ref, bias_ref
):
    nm, up, down = nm_ref[...], up_ref[0], down_ref[0]
    lifted = dot_nn(nm, up) + bup_ref[...]
    active, slope = gelu_parts(lifted)
    active = active.astype(bf16)

    @pl.when(pl.program_id(0) == 0)
    def _():
        y_ref[...] = jnp.zeros_like(y_ref)

    y_ref[...] += dot_nn(active, down)
    mlp_grads(
        active, slope, nm, g_ref[...], up, down, (grad_norm_ref, send_ref, keep_ref, bias_ref), core_ref
    )


def mlp_back_kernel(
    core_ref, nm_ref, g_ref, up_ref, down_ref, act_ref, slope_ref, grad_norm_ref, send_ref, keep_ref, bias_ref
):
    mlp_grads(
        act_ref[...],
        slope_ref[...].astype(f32),
        nm_ref[...],
        g_ref[...],
        up_ref[0],
        down_ref[0],
        (grad_norm_ref, send_ref, keep_ref, bias_ref),
        core_ref,
    )


def mlp_back_call(core, nm, grad, w_up, w_down, layer, b_up=None, kept=None):
    tokens, width = nm.shape
    hidden = w_up.shape[2]
    tiles = hidden // TILE
    half = tiles // 2

    def tile(t, core_ref):
        c = core_ref[0]
        return jnp.where(t < half, (1 - c) * half + t, c * half + t - half)

    whole = pl.BlockSpec((tokens, width), lambda t, c: (0, 0))
    up_spec = pl.BlockSpec((1, width, TILE), lambda t, c: (layer, 0, tile(t, c)))
    down_spec = pl.BlockSpec((1, TILE, width), lambda t, c: (layer, tile(t, c), 0))
    bias_spec = pl.BlockSpec((1, TILE), lambda t, c: (0, tile(t, c)))
    cols_spec = pl.BlockSpec((tokens, TILE), lambda t, c: (0, tile(t, c)))
    out_specs = [
        whole,
        pl.BlockSpec((1, 2 * TILE, width), lambda t, c: (jnp.minimum(t, half - 1), 0, 0)),
        pl.BlockSpec((1, 2 * TILE, width), lambda t, c: (jnp.maximum(t - half, 0), 0, 0)),
        bias_spec,
    ]
    out_shape = [
        jax.ShapeDtypeStruct((tokens, width), f32),
        jax.ShapeDtypeStruct((half, 2 * TILE, width), bf16),
        jax.ShapeDtypeStruct((half, 2 * TILE, width), bf16),
        jax.ShapeDtypeStruct((1, hidden), f32),
    ]
    if kept is None:
        kernel = mlp_both_kernel
        in_specs = [whole, whole, up_spec, bias_spec, down_spec]
        operands = (nm, grad, w_up, b_up[layer : layer + 1], w_down)
        out_specs = [whole] + out_specs
        out_shape = [jax.ShapeDtypeStruct((tokens, width), f32)] + out_shape
    else:
        kernel = mlp_back_kernel
        in_specs = [whole, whole, up_spec, down_spec, cols_spec, cols_spec]
        operands = (nm, grad, w_up, w_down) + kept
    return pl.pallas_call(
        kernel,
        grid_spec=pltpu.PrefetchScalarGridSpec(
            num_scalar_prefetch=1, grid=(tiles,), in_specs=in_specs, out_specs=out_specs
        ),
        out_shape=out_shape,
        compiler_params=params(),
        cost_estimate=cost((12 if kept is None else 8) * tokens * width * hidden, 25 << 20),
        name="mlp_both" if kept is None else "mlp_back",
    )(core, *operands)


def spread_kv(kv_ref, k0, k1, v0, v1):
    kv = kv_ref[...].astype(f32)
    swapped = pltpu.roll(kv, 64, 1)
    low_half = lax.broadcasted_iota(jnp.int32, kv.shape, 1) < 64
    zero = jnp.zeros_like(kv)
    k0[...] = jnp.where(low_half, kv, zero).astype(bf16)
    k1[...] = jnp.where(low_half, zero, swapped).astype(bf16)
    v0[...] = jnp.where(low_half, swapped, zero).astype(bf16)
    v1[...] = jnp.where(low_half, zero, kv).astype(bf16)


def block_rows(index):
    return pl.ds(pl.multiple_of(index * KB, KB), KB)


def forward_part(first, q6, keys, vals, group):
    full = first // KB

    def scores_of(kb):
        return dot_nt(q6, keys[block_rows(kb), :])

    scores = scores_of(full)
    row = lax.broadcasted_iota(jnp.int32, scores.shape, 0) % group
    col = lax.broadcasted_iota(jnp.int32, scores.shape, 1)
    scores = jnp.where(col - row <= first - full * KB, scores, NEGATIVE)
    top = jnp.max(scores, axis=1, keepdims=True)
    weights = jnp.exp(scores - top)
    total = jnp.sum(weights, axis=1, keepdims=True)
    summed = dot_nn(weights.astype(bf16), vals[block_rows(full), :])

    def step(kb, carry):
        top, total, summed = carry
        scores = scores_of(kb)
        new_top = jnp.maximum(top, jnp.max(scores, axis=1, keepdims=True))
        weights = jnp.exp(scores - new_top)
        factor = jnp.exp(top - new_top)
        total = total * factor + jnp.sum(weights, axis=1, keepdims=True)
        summed = summed * factor + dot_nn(weights.astype(bf16), vals[block_rows(kb), :])
        return new_top, total, summed

    top, total, summed = lax.fori_loop(0, full, step, (top, total, summed))
    return summed / total, top + jnp.log(total)


def attend_kernel(first_ref, q_ref, kv_ref, o_ref, lse_ref, k0, k1, v0, v1):
    first = first_ref[0]
    group = q_ref.shape[0]
    spread_kv(kv_ref, k0, k1, v0, v1)
    q6 = pairs_down(q_ref[...])
    even, even_log = forward_part(first, q6, k0, v0, group)
    odd, odd_log = forward_part(first, q6, k1, v1, group)
    both = (even + odd).astype(bf16)
    for p in range(q_ref.shape[1] // 128):
        o_ref[:, p * 128 : (p + 1) * 128] = both[p * group : (p + 1) * group]
    low_half = lax.broadcasted_iota(jnp.int32, even.shape, 1) < 64
    logs = jnp.where(low_half, even_log, odd_log).T
    lse_ref[0, 0] = logs[0:8]
    lse_ref[0, 1] = logs[64:72]


def attend_call(first, q, kv):
    tokens, width = q.shape
    length = kv.shape[0]
    seqs = kv.shape[1] // 128
    group = tokens // seqs
    rows = group * width // 128
    return pl.pallas_call(
        attend_kernel,
        grid_spec=pltpu.PrefetchScalarGridSpec(
            num_scalar_prefetch=1,
            grid=(seqs,),
            in_specs=[
                pl.BlockSpec((group, width), lambda s, f: (s, 0)),
                pl.BlockSpec((length, 128), lambda s, f: (0, s)),
            ],
            out_specs=[
                pl.BlockSpec((group, width), lambda s, f: (s, 0)),
                pl.BlockSpec((1, 2, 8, rows), lambda s, f: (s, 0, 0, 0)),
            ],
            scratch_shapes=[pltpu.VMEM((length, 128), bf16)] * 4,
        ),
        out_shape=[
            jax.ShapeDtypeStruct((tokens, width), bf16),
            jax.ShapeDtypeStruct((seqs, 2, 8, rows), f32),
        ],
        compiler_params=params(),
        cost_estimate=cost(8 * tokens * width * length, 4 << 20, tokens * 12 * length),
        name="attend",
    )(first, q, kv)


def backward_part(first, high, q6, do6, keys, vals, lse, delta, dkv_ref, group, dq_ref):
    full = first // KB
    low_half = lax.broadcasted_iota(jnp.int32, (KB, 128), 1) < 64

    def block(kb, masked):
        rows = block_rows(kb)
        key = keys[rows, :]
        probs = jnp.exp(dot_nt(key, q6) - lse)
        if masked:
            row = lax.broadcasted_iota(jnp.int32, probs.shape, 0)
            col = lax.broadcasted_iota(jnp.int32, probs.shape, 1) % group
            probs = jnp.where(row - col <= first - full * KB, probs, 0.0)
        grad_probs = dot_nt(vals[rows, :], do6)
        grad_scores = (probs * (grad_probs - delta)).astype(bf16)
        grad_key = dot_nn(grad_scores, q6)
        grad_val = dot_nn(probs.astype(bf16), do6)
        if high:
            part = jnp.where(low_half, pltpu.roll(grad_key, 64, 1), grad_val)
        else:
            part = jnp.where(low_half, grad_key, pltpu.roll(grad_val, 64, 1))
        dkv_ref[rows, :] += part
        dq_ref[...] += dot_tn(grad_scores, key)

    block(full, True)

    def step(kb, carry):
        block(kb, False)
        return carry

    lax.fori_loop(0, full, step, 0)


def attend_back_kernel(has_start, first_ref, *refs):
    if has_start:
        q_ref, kv_ref, o_ref, do_ref, lse_ref, tab_ref, start_ref, dq_out, dkv_ref, k0, k1, v0, v1, dq_ref = refs
        dkv_ref[...] = start_ref[...]
    else:
        q_ref, kv_ref, o_ref, do_ref, lse_ref, tab_ref, dq_out, dkv_ref, k0, k1, v0, v1, dq_ref = refs
        dkv_ref[...] = jnp.zeros_like(dkv_ref)
    first = first_ref[0]
    group = q_ref.shape[0]
    spread_kv(kv_ref, k0, k1, v0, v1)
    q6 = pairs_down(q_ref[...])
    do6 = pairs_down(do_ref[...])
    deltas = (do6.astype(f32) * pairs_down(o_ref[...]).astype(f32)).T
    even_delta = jnp.sum(deltas[:64], axis=0, keepdims=True)
    odd_delta = jnp.sum(deltas[64:], axis=0, keepdims=True)
    dq_ref[...] = jnp.zeros_like(dq_ref)
    backward_part(first, False, q6, do6, k0, v0, lse_ref[0, 0, 0:1], even_delta, dkv_ref, group, dq_ref)
    backward_part(first, True, q6, do6, k1, v1, lse_ref[0, 1, 0:1], odd_delta, dkv_ref, group, dq_ref)
    cos_tab, sin_low, sin_high = tab_ref[0], -tab_ref[1], -tab_ref[2]
    for p in range(q_ref.shape[1] // 128):
        part = dq_ref[p * group : (p + 1) * group] * SCALE
        dq_out[:, p * 128 : (p + 1) * 128] = turn(part, cos_tab, sin_low, sin_high).astype(bf16)


def attend_back_call(first, q, kv, attended, grad, lse, tab, start=None):
    tokens, width = q.shape
    length = kv.shape[0]
    seqs = kv.shape[1] // 128
    group = tokens // seqs
    rows = group * width // 128
    tok_spec = pl.BlockSpec((group, width), lambda s, f: (s, 0))
    len_spec = pl.BlockSpec((length, 128), lambda s, f: (0, s))
    in_specs = [
        tok_spec,
        len_spec,
        tok_spec,
        tok_spec,
        pl.BlockSpec((1, 2, 8, rows), lambda s, f: (s, 0, 0, 0)),
        pl.BlockSpec((3, group, 128), lambda s, f: (0, s, 0)),
    ]
    operands = [q, kv, attended, grad, lse, tab]
    if start is not None:
        in_specs.append(len_spec)
        operands.append(start)
    return pl.pallas_call(
        partial(attend_back_kernel, start is not None),
        grid_spec=pltpu.PrefetchScalarGridSpec(
            num_scalar_prefetch=1,
            grid=(seqs,),
            in_specs=in_specs,
            out_specs=[tok_spec, len_spec],
            scratch_shapes=[pltpu.VMEM((length, 128), bf16)] * 4 + [pltpu.VMEM((rows, 128), f32)],
        ),
        out_shape=[
            jax.ShapeDtypeStruct((tokens, width), bf16),
            jax.ShapeDtypeStruct((length, seqs * 128), f32),
        ],
        compiler_params=params(),
        cost_estimate=cost(20 * tokens * width * length, 8 << 20, tokens * 12 * length),
        name="attend_back",
    )(first, *operands)


def middle_kernel(
    att_ref, x_ref, y_ref, wo_ref, bias_ref, gain_ref, off_ref, wq_ref, bq_ref, tab_ref,
    x2_ref, na_ref, nm_ref, q_ref,
):
    second = (
        x_ref[...].astype(f32) + dot_nn(att_ref[...], wo_ref[0]) + y_ref[...] + bias_ref[...]
    ).astype(bf16)
    x2_ref[...] = second
    unit = unit_rows(second.astype(f32))[0]
    norm_a = (unit * gain_ref[0:1] + off_ref[0:1]).astype(bf16)
    na_ref[...] = norm_a
    nm_ref[...] = (unit * gain_ref[1:2] + off_ref[1:2]).astype(bf16)
    proj = dot_nn(norm_a, wq_ref[...]) + bq_ref[...]
    cos_tab, sin_low, sin_high = tab_ref[0], tab_ref[1], tab_ref[2]
    for p in range(proj.shape[1] // 128):
        cols = slice(p * 128, (p + 1) * 128)
        q_ref[:, cols] = (turn(proj[:, cols], cos_tab, sin_low, sin_high) * SCALE).astype(bf16)


def layer_spec(shape, layer):
    return pl.BlockSpec((1,) + shape, lambda i: (layer,) + (0,) * len(shape))


def full_spec(shape):
    return pl.BlockSpec(shape, lambda i: (0,) * len(shape))


def middle_call(att, x, y, w_out, bias, gains, offs, w_q2, b_q2, tab):
    tokens, width = x.shape
    operands = (att, x, y, w_out, bias, gains, offs, w_q2, b_q2.reshape(1, -1), tab)
    specs = [full_spec(v.shape) for v in operands]
    specs[3] = layer_spec((width, width), 0)
    return pl.pallas_call(
        middle_kernel,
        grid=(1,),
        in_specs=specs,
        out_specs=[full_spec((tokens, width))] * 4,
        out_shape=[jax.ShapeDtypeStruct((tokens, width), bf16)] * 4,
        compiler_params=params(),
        cost_estimate=cost(4 * tokens * width * width, 10 << 20),
        name="middle",
    )(*operands)


def norm_back(values, grad_a, grad_m, gain_ref, small_ref, row):
    unit, inverse = unit_rows(values)
    small_ref[row : row + 1] = jnp.sum(grad_a * unit, axis=0, keepdims=True)
    small_ref[row + 1 : row + 2] = jnp.sum(grad_m * unit, axis=0, keepdims=True)
    small_ref[row + 2 : row + 3] = jnp.sum(grad_a, axis=0, keepdims=True)
    small_ref[row + 3 : row + 4] = jnp.sum(grad_m, axis=0, keepdims=True)
    grad_unit = grad_a * gain_ref[0:1] + grad_m * gain_ref[1:2]
    return inverse * (
        grad_unit
        - jnp.mean(grad_unit, axis=-1, keepdims=True)
        - unit * jnp.mean(grad_unit * unit, axis=-1, keepdims=True)
    )


def turn_kernel(
    x2_ref, y_ref, att2_ref, att1_ref, g_ref, na_ref, dq_ref, dnm_ref, wo1_ref, wo2_ref, wq_ref, bias_ref, gain_ref,
    hidden_ref, grads_ref, g1_ref, do1_ref, small_ref,
):
    width = x2_ref.shape[1]
    second = x2_ref[...].astype(f32)
    att2, grad, dq = att2_ref[...], g_ref[...], dq_ref[...]
    wide = grad.astype(f32)
    small_ref[...] = jnp.zeros_like(small_ref)
    grad_a = dot_nt(dq, wq_ref[...])
    g1 = (norm_back(second, grad_a, dnm_ref[...], gain_ref, small_ref, 0) + wide).astype(bf16)
    g1_ref[...] = g1
    do1_ref[...] = dot_nt(g1, wo1_ref[0]).astype(bf16)
    small_ref[4:5] = jnp.sum(wide, axis=0, keepdims=True)
    small_ref[5:6] = jnp.sum(dq.astype(f32), axis=0, keepdims=True)
    small_ref[6:7] = jnp.sum(g1.astype(f32), axis=0, keepdims=True)
    grads_ref[0:width] = dot_tn(att2, grad).astype(bf16)
    grads_ref[width : 2 * width] = dot_tn(na_ref[...], dq).astype(bf16)
    grads_ref[2 * width : 3 * width] = dot_tn(att1_ref[...], g1).astype(bf16)
    hidden_ref[...] = (second + dot_nn(att2, wo2_ref[0]) + y_ref[...] + bias_ref[...]).astype(bf16)


def turn_call(x2, y2, att2, att1, g, na2, dq2, dnm2, w_out, w_q2, bias, gains):
    tokens, width = x2.shape
    operands = (x2, y2, att2, att1, g, na2, dq2, dnm2, w_out, w_out, w_q2, bias, gains)
    specs = [full_spec(v.shape) for v in operands]
    specs[8] = layer_spec((width, width), 0)
    specs[9] = layer_spec((width, width), 1)
    tok = full_spec((tokens, width))
    tok_shape = jax.ShapeDtypeStruct((tokens, width), bf16)
    return pl.pallas_call(
        turn_kernel,
        grid=(1,),
        in_specs=specs,
        out_specs=[tok, full_spec((3 * width, width)), tok, tok, full_spec((8, width))],
        out_shape=[
            tok_shape,
            jax.ShapeDtypeStruct((3 * width, width), bf16),
            tok_shape,
            tok_shape,
            jax.ShapeDtypeStruct((8, width), f32),
        ],
        compiler_params=params(),
        cost_estimate=cost(12 * tokens * width * width, 20 << 20),
        name="turn",
    )(*operands)


def last_kernel(
    x_ref, g1_ref, na_ref, dq_ref, dkv_ref, dnm_ref, w_ref, gain_ref, tab_ref, grad_ref, grads_ref, small_ref
):
    tokens, width = x_ref.shape
    group = dkv_ref.shape[0]
    dkv = jnp.concatenate(
        [dkv_ref[:, s * 128 : (s + 1) * 128] for s in range(tokens // group)], axis=0
    ).astype(f32)
    low_half = lax.broadcasted_iota(jnp.int32, dkv.shape, 1) < 64
    dkv = jnp.where(low_half, turn(dkv, tab_ref[0], -tab_ref[1], -tab_ref[2]), dkv).astype(bf16)
    dq, norm_a = dq_ref[...], na_ref[...]
    small_ref[...] = jnp.zeros_like(small_ref)
    small_ref[4:5] = jnp.sum(dq.astype(f32), axis=0, keepdims=True)
    small_ref[5:6, 0:128] = jnp.sum(dkv.astype(f32), axis=0, keepdims=True)
    grads_ref[0:width] = dot_tn(norm_a, dq).astype(bf16)
    grads_ref[width : width + 128] = dot_tn(dkv, norm_a).astype(bf16)
    grad_a = dot_nt(dq, w_ref[:, :width]) + dot_nt(dkv, w_ref[:, width:])
    grad_ref[...] = g1_ref[...].astype(f32) + norm_back(
        x_ref[...].astype(f32), grad_a, dnm_ref[...], gain_ref, small_ref, 0
    )


def last_call(x, g1, na1, dq1, dkv, dnm1, w_qkv, gains, tab):
    tokens, width = x.shape
    return pl.pallas_call(
        last_kernel,
        in_specs=vmem(9),
        out_specs=vmem(3),
        out_shape=[
            jax.ShapeDtypeStruct((tokens, width), f32),
            jax.ShapeDtypeStruct((width + 128, width), bf16),
            jax.ShapeDtypeStruct((8, width), f32),
        ],
        compiler_params=params(),
        cost_estimate=cost(4 * tokens * width * (width + 128), 10 << 20),
        name="last",
    )(x, g1, na1, dq1, dkv, dnm1, w_qkv, gains, tab)


def swap_cores(values):
    return lax.ppermute(values, C, [(0, 1), (1, 0)])


def reduce_parts(send, keep):
    part = (swap_cores(send).astype(f32) + keep.astype(f32)).astype(bf16)
    part = lax.psum_scatter(part, B, scatter_dimension=0, tiled=True)
    return lax.psum_scatter(part, Z, scatter_dimension=0, tiled=True)


def gather_parts(part):
    return lax.all_gather(part, (C,) + B + (Z,), axis=0, tiled=True)


def halves(rows, core):
    half = rows.shape[0] // 2
    send = lax.dynamic_slice_in_dim(rows, (1 - core) * half, half, 0)
    keep = lax.dynamic_slice_in_dim(rows, core * half, half, 0)
    return send, keep


def place_kernel(in_ref, *refs):
    down_ref, up_ref = refs[-2:]
    for j in range(in_ref.shape[0] // (2 * UNIT)):
        rows = slice(j * UNIT, (j + 1) * UNIT)
        down_ref[0, rows] = in_ref[2 * j * UNIT : (2 * j + 1) * UNIT].astype(f32)
        up_ref[0, rows] = in_ref[(2 * j + 1) * UNIT : (2 * j + 2) * UNIT].astype(f32)


def place_call(rows, layer, before=None):
    width = rows.shape[1]
    hidden = rows.shape[0] // 2
    step_rows = TILE // 2
    in_specs = [pl.BlockSpec((TILE, width), lambda i: (i, 0))]
    operands = [rows]
    aliases = {}
    if before is not None:
        in_specs += [pl.BlockSpec(memory_space=pl.ANY)] * 2
        operands += list(before)
        aliases = {1: 0, 2: 1}
    return pl.pallas_call(
        place_kernel,
        grid=(hidden // step_rows,),
        in_specs=in_specs,
        out_specs=[
            pl.BlockSpec((1, step_rows, width), lambda i: (layer, i, 0)),
            pl.BlockSpec((1, step_rows, TILE), lambda i: (layer, i % 2, i // 2)),
        ],
        out_shape=[
            jax.ShapeDtypeStruct((2, hidden, width), f32),
            jax.ShapeDtypeStruct((2, width, hidden), f32),
        ],
        input_output_aliases=aliases,
        compiler_params=params(),
        cost_estimate=cost(0, rows.size * 6),
        name="place",
    )(*operands)


def rotary_tables(positions):
    half_rot = ROT // 2
    inverse = BASE ** (-(jnp.arange(half_rot, dtype=f32) * 2.0 / ROT))
    angles = positions.astype(f32).reshape(-1, 1) * inverse
    cos, sin = jnp.cos(angles), jnp.sin(angles)
    zero = jnp.zeros_like(sin)
    rest = jnp.zeros((cos.shape[0], 64 - ROT), f32)
    head = [
        jnp.concatenate([cos, cos, rest + 1.0], axis=-1),
        jnp.concatenate([-sin, zero, rest], axis=-1),
        jnp.concatenate([zero, sin, rest], axis=-1),
    ]
    return jnp.stack([jnp.concatenate([h, h], axis=-1) for h in head])


def local(
    hidden_in,
    positions,
    cotangent,
    norm_gains,
    norm_biases,
    w_qkv,
    b_qkv,
    w_q2,
    b_q2,
    w_out,
    w_up,
    b_up,
    w_down,
    out_bias,
):
    seqs, group, width = hidden_in.shape
    tokens = seqs * group
    hidden = w_up.shape[2]
    core = lax.axis_index(C)
    core_row = core.reshape(1).astype(jnp.int32)
    first = ((lax.axis_index(Z) * 2 + core) * group).reshape(1).astype(jnp.int32)
    x1 = hidden_in.reshape(tokens, width)
    g2 = cotangent.reshape(tokens, width)
    tab = rotary_tables(positions)

    na1, nm1, q1, kv_own = first_call(x1, norm_gains[0], norm_biases[0], w_qkv, b_qkv, tab, group)
    kv = lax.all_gather(kv_own, (Z, C), axis=0, tiled=True)
    y1, act1, slope1 = mlp_fwd_call(nm1, w_up, b_up, w_down, 0)
    do2 = lax.dot_general(
        g2, w_out[1], (((1,), (1,)), ((), ())), preferred_element_type=f32
    ).astype(bf16)
    att1, lse1 = attend_call(first, q1, kv)
    x2, na2, nm2, q2 = middle_call(
        att1, x1, y1, w_out, out_bias[0:1], norm_gains[1], norm_biases[1], w_q2, b_q2, tab
    )

    y2, dnm2, send, keep, bup2 = mlp_back_call(core_row, nm2, g2, w_up, w_down, 1, b_up=b_up)
    mlp2 = reduce_parts(send.reshape(hidden, width), keep.reshape(hidden, width))
    att2, lse2 = attend_call(first, q2, kv)
    dq2, dkv2 = attend_back_call(first, q2, kv, att2, do2, lse2, tab)
    hidden_out, grads2, g1, do1, small2 = turn_call(
        x2, y2, att2, att1, g2, na2, dq2, dnm2, w_out, w_q2, out_bias[1:2], norm_gains[1]
    )
    outs2 = reduce_parts(*halves(grads2, core))
    dq1, dkv1 = attend_back_call(first, q1, kv, att1, do1, lse1, tab, dkv2)
    dkv = lax.psum_scatter(dkv1.astype(bf16), (Z, C), scatter_dimension=0, tiled=True)
    dnm1, send, keep, bup1 = mlp_back_call(
        core_row, nm1, g1, w_up, w_down, 0, kept=(act1, slope1)
    )
    mlp1 = reduce_parts(send.reshape(hidden, width), keep.reshape(hidden, width))
    grad_input, grads1, small1 = last_call(x1, g1, na1, dq1, dkv, dnm1, w_qkv, norm_gains[0], tab)
    small = jnp.concatenate(
        [small1, small2, bup1.reshape(-1, width), bup2.reshape(-1, width)], axis=0
    ).astype(bf16)
    used = grads1.shape[0] + small.shape[0]
    total = -(-used // 256) * 256
    grads1 = jnp.concatenate([grads1, small, jnp.zeros((total - used, width), bf16)], axis=0)
    outs1 = reduce_parts(*halves(grads1, core))

    placed = place_call(gather_parts(mlp2), 1)
    outs2 = gather_parts(outs2)
    grad_down, grad_up = place_call(gather_parts(mlp1), 0, placed)
    outs1 = gather_parts(outs1)

    grad_out = jnp.stack([outs2[2 * width :], outs2[:width]]).astype(f32)
    grad_q2 = outs2[width : 2 * width].astype(f32)
    kv_rows = outs1[width : width + 128]
    grad_qkv = jnp.concatenate([outs1[:width], kv_rows.T], axis=1).astype(f32)
    small = outs1[width + 128 :].astype(f32)
    one, two = small[0:8], small[8:16]
    ups = hidden // width
    grad_up_bias = jnp.stack([small[16 : 16 + ups].reshape(-1), small[16 + ups : 16 + 2 * ups].reshape(-1)])
    grad_gains = jnp.stack([one[0:2], two[0:2]])
    grad_biases = jnp.stack([one[2:4], two[2:4]])
    grad_qkv_bias = jnp.concatenate([one[4], one[5, :128]])
    grad_out_bias = jnp.stack([two[6], two[4]])
    return (
        hidden_out.reshape(seqs, group, width),
        grad_input.reshape(seqs, group, width),
        grad_gains,
        grad_biases,
        grad_qkv,
        grad_qkv_bias,
        grad_q2,
        two[5],
        grad_out,
        grad_up,
        grad_up_bias,
        grad_down,
        grad_out_bias,
    )


def solution(mesh):
    batch, seq = mesh.shape["batch"], mesh.shape["seq"]
    fine = jax.sharding.Mesh(
        mesh.devices.reshape(2, batch // 2, seq // 2, 2), ("b0", "b1", "z", "c")
    )
    rows = P(B, (Z, C), None)
    return jax.shard_map(
        local,
        mesh=fine,
        in_specs=(rows, P(B, (Z, C)), rows) + (P(),) * 11,
        out_specs=(rows, rows) + (P(),) * 11,
        check_vma=False,
    )
```

time: 1270 us -> 842 us (0.66)
  matrix products: 187 us -> 2.97 us
  waiting for transfers between devices: 765 us -> 616 us
  Pallas kernels: 0 us -> 138 us
  blocking collectives: 123 us -> 0 us
  other arithmetic: 113 us -> 36.4 us
  local copies, waits for them, and re-layouts: 51.4 us -> 27.4 us
    dot_general x38 -> x1, matrix products: 187 us -> 2.97 us  [local(): lax.dot_general(g2, w_out[1], (((1,), (1,)), ((), ())), preferred_element...]
    unnamed x28 -> x14, waiting for transfers between devices: 167 us -> 0.88 us
    pallas_call x0 -> x13, Pallas kernels: none -> 138 us  [the longest x2 45.1 us: mlp_back_call(): pl.pallas_call(kernel, grid_spec=pltpu.PrefetchScalarGridSpec(num_scalar_...]
    psum x1 -> x0, waiting for transfers between devices: 73 us -> none  [reduce_grads(): lax.psum(proj_weight.astype(jnp.bfloat16), 'batch').astype(jnp.float32)]
    all_gather x6 -> x0, blocking collectives: 62.8 us -> none  [the longest x2 25.4 us: reduce_grads(): lax.all_gather(up_bias.astype(jnp.bfloat16), 'seq', axis=0, tiled=True)]
    all_gather x9 -> x5, waiting for transfers between devices: 208 us -> 270 us  [the longest x4 261 us: gather_parts(): return lax.all_gather(part, (C,) + B + (Z,), axis=0, tiled=True)]
    unnamed x2 -> x0, blocking collectives: 40 us -> none
    another operation x11 -> x10, other arithmetic: 33.8 us -> 7.31 us  [the longest x1 3.7 us: local(): grad_out = jnp.stack([outs2[2 * width:], outs2[:width]]).astype(f32)]
  transfers between devices with their start and end apart: 23 -> 18, of which waited for: 17 -> 16; matrix products, arithmetic and copies ran while one was open for 12% -> 4% of each run, Pallas kernels for 0% -> 5%
where the time goes in v1:
time: 842 us; the launch traced here: 837 us
  waiting for transfers between devices  616 us (73%)
  Pallas kernels  138 us (16%)
  other arithmetic  36.4 us (4%)
  local copies, waits for them, and re-layouts  27.4 us (3%)
  between operations  14.5 us (2%)
    all_gather x4, waiting for transfers between devices, gather_parts(): return lax.all_gather(part, (C,) + B + (Z,), axis=0, tiled=True)  261 us
    reduce_scatter x4, waiting for transfers between devices, reduce_parts(): part = lax.psum_scatter(part, B, scatter_dimension=0, tiled=True)  150 us
    reduce_scatter x4, waiting for transfers between devices, reduce_parts(): return lax.psum_scatter(part, Z, scatter_dimension=0, tiled=True)  103 us
    reduce_scatter x1, waiting for transfers between devices, local(): lax.psum_scatter(dkv1.astype(bf16), (Z, C), scatter_dimension=0, tiled=True)  79 us
    pallas_call x2, Pallas kernels, mlp_back_call(): pl.pallas_call(kernel, grid_spec=pltpu.PrefetchScalarGridSpec(num_scalar_...  45.1 us
    pallas_call x2, Pallas kernels, place_call(): pl.pallas_call(place_kernel, grid=(hidden // step_rows,), in_specs=in_spe...  22.8 us
    pallas_call x2, Pallas kernels, attend_back_call(): pl.pallas_call(partial(attend_back_kernel, start is not None), grid_spec=...  19.7 us
    convert_element_type x4, other arithmetic, reduce_parts(): part = (swap_cores(send).astype(f32) + keep.astype(f32)).astype(bf16)  18.7 us
  transfers between devices with their start and end apart: 18, of which 16 were waited for; matrix products, arithmetic and copies ran while one was open for 4% of the time, Pallas kernels for 5%

profile of v1, /device:TPU:0, one launch (start us, length us, event | category | flops | bytes accessed | tf_op | source)
XLA Modules:
  0.0 836.7 jit_solution(15735024020396215731)
XLA Ops:
  12.8 4.0 first.1
  21.7 11.8 %mlp_fwd.1 = (f32[512,768]{1,0:T(8,128)S(1)}, bf16[512,3072]{1,0:T(8,128)(2,1)}, bf16[512,3072]{1,0:T(8,128)(2,1)}) custom-call(bf16[512,768]{1,0:T(8,128)(2,1)S(1)} %get-tuple-element.56.nm_ref, bf16[2,768,3072]{2,1,0:T(8,128)(2,1)} %up_ref.5, f32[1,3072]{1,0:T(1,128)S(1)} %get-tuple-element.109.bup_ref, bf16[2,3072,768]{2,1,0:T(8,128)(2,1)} %down_ref.5), custom_call_target="tpu_custom_call" | custom-call | flops 4831838208 | bytes 20971520 | tf_op jit(solution)/shard_map/mlp_fwd/pallas_call | solution.py:135
  34.7 8.9 %all-gather.6.cloned.1.call-done.kv_ref.refs_1_ = bf16[1024,512]{1,0:T(8,128)(2,1)} async-done(((bf16[128,512]{1,0:T(8,128)(2,1)}), bf16[1024,512]{1,0:T(8,128)(2,1)}) %all-gather.6.cloned.1.call-update) | async-done | bytes 1048592 | tf_op jit(solution)/shard_map/all_gather | solution.py:706
  44.8 6.6 attend.2
  51.4 5.1 middle.1
  57.4 25.5 %mlp_both.1 = (f32[512,768]{1,0:T(8,128)S(1)}, f32[512,768]{1,0:T(8,128)}, bf16[2,1536,768]{2,1,0:T(8,128)(2,1)}, bf16[2,1536,768]{2,1,0:T(8,128)(2,1)}, f32[1,3072]{1,0:T(1,128)S(1)}) custom-call(s32[1]{0:T(128)} %bitcast.10.core_ref, bf16[512,768]{1,0:T(8,128)(2,1)S(1)} %get-tuple-element.59.nm_ref, bf16[512,768]{1,0:T(8,128)(2,1)S(1)} %bitcast.60, ...), custom_call_target="tpu_custom_call" | custom-call | flops 14495514624 | bytes 26214400 | tf_op jit(solution)/shard_map/mlp_both/pallas_call | solution.py:262
  84.1 6.8 attend.3
  90.9 9.6 %attend_back.2 = (bf16[512,768]{1,0:T(8,128)(2,1)S(1)}, f32[1024,512]{1,0:T(8,128)}) custom-call(s32[1]{0:T(128)} %bitcast.first_ref, bf16[512,768]{1,0:T(8,128)(2,1)S(1)} %get-tuple-element.61.q_ref.refs_0_, bf16[1024,512]{1,0:T(8,128)(2,1)} %all-gather.6.cloned.1.call-done.kv_ref.refs_1_, bf16[512,768]{1,0:T(8,128)(2,1)S(1)} %get-tuple-element.62.refs_2_.att2_ref, ...), custom_call_target="tpu_custom_call" | custom-call | flops 8053063680 | bytes 8388608 | tf_op jit(solution)/shard_map/attend_back/pallas_call | solution.py:441
  101.3 10.5 %turn.1 = (bf16[512,768]{1,0:T(8,128)(2,1)}, bf16[2304,768]{1,0:T(8,128)(2,1)}, bf16[512,768]{1,0:T(8,128)(2,1)S(1)}, bf16[512,768]{1,0:T(8,128)(2,1)S(1)}, f32[8,768]{1,0:T(8,128)S(1)}) custom-call(bf16[512,768]{1,0:T(8,128)(2,1)S(1)} %get-tuple-element.58.x2_ref, f32[512,768]{1,0:T(8,128)} %copy-done.4, ...), custom_call_target="tpu_custom_call" | custom-call | flops 3623878656 | bytes 20971520 | tf_op jit(solution)/shard_map/turn/pallas_call | solution.py:548
  112.7 10.1 %attend_back.3 = (bf16[512,768]{1,0:T(8,128)(2,1)S(1)}, f32[1024,512]{1,0:T(8,128)}) custom-call(s32[1]{0:T(128)} %bitcast.first_ref, bf16[512,768]{1,0:T(8,128)(2,1)S(1)} %copy-done.21, bf16[1024,512]{1,0:T(8,128)(2,1)} %all-gather.6.cloned.1.call-done.kv_ref.refs_1_, bf16[512,768]{1,0:T(8,128)(2,1)S(1)} %get-tuple-element.55.att_ref.att1_ref.refs_2_, ...), custom_call_target="tpu_custom_call" | custom-call | flops 8053063680 | bytes 8388608 | tf_op jit(solution)/shard_map/attend_back/pallas_call | solution.py:441
  127.7 19.7 %mlp_back.1 = (f32[512,768]{1,0:T(8,128)S(1)}, bf16[2,1536,768]{2,1,0:T(8,128)(2,1)}, bf16[2,1536,768]{2,1,0:T(8,128)(2,1)}, f32[1,3072]{1,0:T(1,128)S(1)}) custom-call(s32[1]{0:T(128)} %bitcast.10.core_ref, bf16[512,768]{1,0:T(8,128)(2,1)S(1)} %get-tuple-element.56.nm_ref, bf16[512,768]{1,0:T(8,128)(2,1)S(1)} %copy-done.13, bf16[2,768,3072]{2,1,0:T(8,128)(2,1)} %up_ref.5, ...), custom_call_target="tpu_custom_call" | custom-call | flops 9663676416 | bytes 26214400 | tf_op jit(solution)/shard_map/mlp_back/pallas_call | solution.py:262
  148.6 79.0 %reduce-scatter.10.cloned.1.call-done.dkv_ref = bf16[128,512]{1,0:T(8,128)(2,1)} async-done(((bf16[1024,512]{1,0:T(8,128)(2,1)}), bf16[128,512]{1,0:T(8,128)(2,1)}) %reduce-scatter.10.cloned.1.call-update) | async-done | bytes 131088 | tf_op jit(solution)/shard_map/reduce_scatter | solution.py:725
  230.8 5.8 last.1
  236.6 5.7 concatenate.30
  248.8 3.7 collective-permute-done.1
  256.9 7.4 fusion
  264.9 7.8 collective-permute-done.2
  272.7 6.0 fusion.1
  279.6 29.9 %reduce-scatter.16.cloned.1.call-done = bf16[288,768]{1,0:T(8,128)(2,1)} async-done(((bf16[1152,768]{1,0:T(8,128)(2,1)}), bf16[288,768]{1,0:T(8,128)(2,1)}) %reduce-scatter.16.cloned.1.call-update) | async-done | bytes 442384 | tf_op jit(solution)/shard_map/reduce_scatter | solution.py:611
  309.5 59.9 %reduce-scatter.24.cloned.1.call-done = bf16[768,768]{1,0:T(8,128)(2,1)} async-done(((bf16[3072,768]{1,0:T(8,128)(2,1)}), bf16[768,768]{1,0:T(8,128)(2,1)}) %reduce-scatter.24.cloned.1.call-update) | async-done | bytes 1179664 | tf_op jit(solution)/shard_map/reduce_scatter | solution.py:611
  369.5 60.5 %reduce-scatter.20.cloned.1.call-done = bf16[768,768]{1,0:T(8,128)(2,1)} async-done(((bf16[3072,768]{1,0:T(8,128)(2,1)}), bf16[768,768]{1,0:T(8,128)(2,1)}) %reduce-scatter.20.cloned.1.call-update) | async-done | bytes 1179664 | tf_op jit(solution)/shard_map/reduce_scatter | solution.py:611
  430.0 21.6 %reduce-scatter.14.cloned.1.call-done = bf16[32,768]{1,0:T(8,128)(2,1)} async-done(((bf16[128,768]{1,0:T(8,128)(2,1)}), bf16[32,768]{1,0:T(8,128)(2,1)}) %reduce-scatter.14.cloned.1.call-update) | async-done | bytes 49168 | tf_op jit(solution)/shard_map/reduce_scatter | solution.py:612
  451.7 21.6 %reduce-scatter.18.cloned.1.call-done = bf16[72,768]{1,0:T(8,128)(2,1)} async-done(((bf16[288,768]{1,0:T(8,128)(2,1)}), bf16[72,768]{1,0:T(8,128)(2,1)}) %reduce-scatter.18.cloned.1.call-update) | async-done | bytes 110608 | tf_op jit(solution)/shard_map/reduce_scatter | solution.py:612
  473.4 29.7 %reduce-scatter.26.cloned.1.call-done = bf16[192,768]{1,0:T(8,128)(2,1)} async-done(((bf16[768,768]{1,0:T(8,128)(2,1)}), bf16[192,768]{1,0:T(8,128)(2,1)}) %reduce-scatter.26.cloned.1.call-update) | async-done | bytes 294928 | tf_op jit(solution)/shard_map/reduce_scatter | solution.py:612
  503.2 30.0 %reduce-scatter.22.cloned.1.call-done = bf16[192,768]{1,0:T(8,128)(2,1)} async-done(((bf16[768,768]{1,0:T(8,128)(2,1)}), bf16[192,768]{1,0:T(8,128)(2,1)}) %reduce-scatter.22.cloned.1.call-update) | async-done | bytes 294928 | tf_op jit(solution)/shard_map/reduce_scatter | solution.py:612
  533.2 56.7 %all-gather.8.cloned.1.call-done = bf16[1024,768]{1,0:T(8,128)(2,1)} async-done(((bf16[32,768]{1,0:T(8,128)(2,1)}), bf16[1024,768]{1,0:T(8,128)(2,1)}) %all-gather.8.cloned.1.call-update) | async-done | bytes 1572880 | tf_op jit(solution)/shard_map/all_gather | solution.py:616
  596.7 54.9 %all-gather.10.cloned.1.call-done = bf16[2304,768]{1,0:T(8,128)(2,1)} async-done(((bf16[72,768]{1,0:T(8,128)(2,1)}), bf16[2304,768]{1,0:T(8,128)(2,1)}) %all-gather.10.cloned.1.call-update) | async-done | bytes 3538960 | tf_op jit(solution)/shard_map/all_gather | solution.py:616
  651.6 3.7 slice_bitcast_fusion.1
  657.8 77.5 %all-gather.14.cloned.1.call-done.in_ref = bf16[6144,768]{1,0:T(8,128)(2,1)} async-done(((bf16[192,768]{1,0:T(8,128)(2,1)}), bf16[6144,768]{1,0:T(8,128)(2,1)}) %all-gather.14.cloned.1.call-update) | async-done | bytes 9437200 | tf_op jit(solution)/shard_map/all_gather | solution.py:616
  735.3 11.4 %place.2 = (f32[2,3072,768]{2,1,0:T(8,128)}, f32[2,768,3072]{2,1,0:T(8,128)}) custom-call(bf16[6144,768]{1,0:T(8,128)(2,1)} %all-gather.14.cloned.1.call-done.in_ref), custom_call_target="tpu_custom_call" | custom-call | bytes 28311552 | tf_op jit(solution)/shard_map/place/pallas_call | solution.py:645
  746.7 71.9 %all-gather.12.cloned.1.call-done.in_ref = bf16[6144,768]{1,0:T(8,128)(2,1)} async-done(((bf16[192,768]{1,0:T(8,128)(2,1)}), bf16[6144,768]{1,0:T(8,128)(2,1)}) %all-gather.12.cloned.1.call-update) | async-done | bytes 9437200 | tf_op jit(solution)/shard_map/all_gather | solution.py:616
  818.6 11.4 %place.3 = (f32[2,3072,768]{2,1,0:T(8,128)}, f32[2,768,3072]{2,1,0:T(8,128)}) custom-call(bf16[6144,768]{1,0:T(8,128)(2,1)} %all-gather.12.cloned.1.call-done.in_ref, f32[2,3072,768]{2,1,0:T(8,128)} %get-tuple-element.89.refs_0_, f32[2,768,3072]{2,1,0:T(8,128)} %get-tuple-element.90.refs_1_), custom_call_target="tpu_custom_call", output_to_operand_aliasing={{0}: (1, {}), {1}: (2, {})} | custom-call | bytes 28311552 | tf_op jit(solution)/shard_map/place/pallas_call | solution.py:645
  (136 shorter events, 47.7 us)
Async XLA Ops:
  7.2 36.4 %all-gather.6.cloned.1.call-start = ((), (), s32[]{:S(2)}) async-start(), calls=%async_computation.9 | async-start | bytes 1179648 | tf_op jit(solution)/shard_map/all_gather | solution.py:706
  8.6 2.0 copy-start.25
  10.1 2.7 copy-start.2
  11.7 6.9 copy-start.27
  11.7 7.0 copy-start.26
  11.7 7.0 copy-start.7
  12.8 8.9 %copy-start = (f32[3,512,128]{2,1,0:T(8,128)}, f32[3,512,128]{2,1,0:T(8,128)S(1)}, u32[]{:S(2)}) copy-start(f32[3,512,128]{2,1,0:T(8,128)S(1)} %pad_maximum_fusion.tab_ref.refs_5_) | copy-start | bytes 2359300
  18.6 3.1 copy-start.23
  18.6 209.0 %reduce-scatter.10.cloned.1.call-start = ((), (), s32[]{:S(2)}) async-start(), calls=%async_computation.10 | async-start | bytes 1179648 | tf_op jit(solution)/shard_map/reduce_scatter | solution.py:725
  21.7 21.8 %copy-start.21 = (bf16[512,768]{1,0:T(8,128)(2,1)S(1)}, bf16[512,768]{1,0:T(8,128)(2,1)}, u32[]{:S(2)}) copy-start(bf16[512,768]{1,0:T(8,128)(2,1)} %copy-done.20) | copy-start | bytes 2359300
  57.4 26.6 %copy-start.19 = (bf16[1024,512]{1,0:T(8,128)(2,1)S(1)}, bf16[1024,512]{1,0:T(8,128)(2,1)}, u32[]{:S(2)}) copy-start(bf16[1024,512]{1,0:T(8,128)(2,1)} %all-gather.6.cloned.1.call-done.kv_ref.refs_1_) | copy-start | bytes 3145732
  84.1 6.8 copy-start.22
  126.4 152.4 %reduce-scatter.12.cloned.1.call-start = ((), (), s32[]{:S(2)}) async-start(), calls=%async_computation.11 | async-start | bytes 983040 | tf_op jit(solution)/shard_map/reduce_scatter | solution.py:611
  127.7 99.9 %copy-start.1 = (f32[3,512,128]{2,1,0:T(8,128)S(1)}, f32[3,512,128]{2,1,0:T(8,128)}, u32[]{:S(2)}) copy-start(f32[3,512,128]{2,1,0:T(8,128)} %copy-done) | copy-start | bytes 2359300
  127.7 99.9 %copy-start.3 = (bf16[4,128,768]{2,1,0:T(8,128)(2,1)S(1)}, bf16[4,128,768]{2,1,0:T(8,128)(2,1)}, u32[]{:S(2)}) copy-start(bf16[4,128,768]{2,1,0:T(8,128)(2,1)} %param.14) | copy-start | bytes 2359300
  127.7 99.9 %copy-start.11 = (bf16[512,768]{1,0:T(8,128)(2,1)S(1)}, bf16[512,768]{1,0:T(8,128)(2,1)}, u32[]{:S(2)}) copy-start(bf16[512,768]{1,0:T(8,128)(2,1)} %copy-done.10) | copy-start | bytes 2359300
  243.2 3.3 collective-permute-start
  246.0 6.5 collective-permute-start.1
  246.5 10.4 %collective-permute-start.3 = (bf16[3072,768]{1,0:T(8,128)(2,1)}, bf16[3072,768]{1,0:T(8,128)(2,1)}, u32[]{:S(2)}, u32[]{:S(2)}) collective-permute-start(bf16[3072,768]{1,0:T(8,128)(2,1)} %bitcast.66), channel_id=1, source_target_pairs={{0,1},{1,0},{2,3},{3,2},{4,5},{5,4},{6,7},{7,6},{8,9},{9,8},{10,11... | collective-permute-start | bytes 14155784 | tf_op jit(solution)/shard_map/ppermute | solution.py:606
  248.7 60.7 %reduce-scatter.16.cloned.1.call-start = ((), (), s32[]{:S(2)}) async-start(), calls=%async_computation.14 | async-start | bytes 2211840 | tf_op jit(solution)/shard_map/reduce_scatter | solution.py:611
  255.7 113.7 %reduce-scatter.24.cloned.1.call-start = ((), (), s32[]{:S(2)}) async-start(), calls=%async_computation.20 | async-start | bytes 5898240 | tf_op jit(solution)/shard_map/reduce_scatter | solution.py:611
  264.3 165.7 %reduce-scatter.20.cloned.1.call-start = ((), (), s32[]{:S(2)}) async-start(), calls=%async_computation.17 | async-start | bytes 5898240 | tf_op jit(solution)/shard_map/reduce_scatter | solution.py:611
  264.5 8.2 collective-permute-start.2
  278.8 172.9 %reduce-scatter.14.cloned.1.call-start = ((), (), s32[]{:S(2)}) async-start(), calls=%async_computation.12 | async-start | bytes 245760 | tf_op jit(solution)/shard_map/reduce_scatter | solution.py:612
  279.5 193.8 %reduce-scatter.18.cloned.1.call-start = ((), (), s32[]{:S(2)}) async-start(), calls=%async_computation.15 | async-start | bytes 552960 | tf_op jit(solution)/shard_map/reduce_scatter | solution.py:612
  309.5 193.6 %reduce-scatter.26.cloned.1.call-start = ((), (), s32[]{:S(2)}) async-start(), calls=%async_computation.21 | async-start | bytes 1474560 | tf_op jit(solution)/shard_map/reduce_scatter | solution.py:612
  369.4 163.8 %reduce-scatter.22.cloned.1.call-start = ((), (), s32[]{:S(2)}) async-start(), calls=%async_computation.18 | async-start | bytes 1474560 | tf_op jit(solution)/shard_map/reduce_scatter | solution.py:612
  430.0 159.9 %all-gather.8.cloned.1.call-start = ((), (), s32[]{:S(2)}) async-start(), calls=%async_computation.13 | async-start | bytes 1622016 | tf_op jit(solution)/shard_map/all_gather | solution.py:616
  451.7 200.0 %all-gather.10.cloned.1.call-start = ((), (), s32[]{:S(2)}) async-start(), calls=%async_computation.16 | async-start | bytes 3649536 | tf_op jit(solution)/shard_map/all_gather | solution.py:616
  473.4 261.9 %all-gather.14.cloned.1.call-start = ((), (), s32[]{:S(2)}) async-start(), calls=%async_computation.22 | async-start | bytes 9732096 | tf_op jit(solution)/shard_map/all_gather | solution.py:616
  503.2 315.4 %all-gather.12.cloned.1.call-start = ((), (), s32[]{:S(2)}) async-start(), calls=%async_computation.19 | async-start | bytes 9732096 | tf_op jit(solution)/shard_map/all_gather | solution.py:616
  589.9 4.4 slice-start
  (15 other events, 16.2 us)
Sparse Core Ops, SparseCore 0:
  18.7 24.7 all-gather.5
  126.6 100.9 reduce-scatter.9
  248.9 24.5 reduce-scatter.11
  277.0 32.4 reduce-scatter.15
  312.3 57.0 reduce-scatter.23
  372.8 57.0 reduce-scatter.19
  432.2 19.3 reduce-scatter.13
  454.0 19.2 reduce-scatter.17
  475.6 27.4 reduce-scatter.25
  505.3 27.8 reduce-scatter.21
  536.1 53.7 all-gather.7
  592.6 58.9 all-gather.9
  654.4 80.8 all-gather.13
  737.9 80.6 all-gather.11

commit v2 on v1

v2 whole, which is shorter than its diff:
```python
from functools import partial

import jax
import jax.numpy as jnp
from jax import lax
from jax.experimental import pallas as pl
from jax.experimental.pallas import tpu as pltpu
from jax.sharding import PartitionSpec as P

ROT = 16
EPSILON = 1e-05
SCALE = 0.125
NEGATIVE = -1e30
BASE = 10000.0

B = ("b0", "b1")
Z = "z"
C = "c"
TILE = 768
QUARTER = TILE // 2
KB = 256

f32 = jnp.float32
bf16 = jnp.bfloat16


def dot_nn(a, b):
    return lax.dot_general(a, b, (((1,), (0,)), ((), ())), preferred_element_type=f32)


def dot_nt(a, b):
    return lax.dot_general(a, b, (((1,), (1,)), ((), ())), preferred_element_type=f32)


def dot_tn(a, b):
    return lax.dot_general(a, b, (((0,), (0,)), ((), ())), preferred_element_type=f32)


def invoke(
    kernel, operands, deps, *, grid, in_specs, out_specs, out_shape, name, scalars=(), scratch=(), aliases={}, us=2
):
    ahead = len(scalars) + len(operands)

    def body(*refs):
        kernel(*refs[:ahead], *refs[ahead + len(deps) :])

    return pl.pallas_call(
        body,
        grid_spec=pltpu.PrefetchScalarGridSpec(
            num_scalar_prefetch=len(scalars),
            grid=grid,
            in_specs=list(in_specs) + [pl.BlockSpec(memory_space=pl.ANY)] * len(deps),
            out_specs=out_specs,
            scratch_shapes=scratch,
        ),
        out_shape=out_shape,
        input_output_aliases=aliases,
        compiler_params=pltpu.CompilerParams(vmem_limit_bytes=50 << 20),
        cost_estimate=pl.CostEstimate(
            flops=us * 600_000_000, bytes_accessed=us * 1_000_000, transcendentals=0
        ),
        name=name,
    )(*scalars, *operands, *deps)


def layer_spec(shape, layer):
    return pl.BlockSpec((1,) + shape, lambda *i: (layer,) + (0,) * len(shape))


def full_spec(shape):
    return pl.BlockSpec(shape, lambda *i: (0,) * len(shape))


def unit_rows(values):
    center = values - jnp.mean(values, axis=-1, keepdims=True)
    spread = jnp.mean(center * center, axis=-1, keepdims=True)
    inverse = lax.rsqrt(spread + EPSILON)
    return center * inverse, inverse


def turn(values, cos_tab, sin_low, sin_high):
    return (
        values * cos_tab
        + pltpu.roll(values, 120, 1) * sin_low
        + pltpu.roll(values, 8, 1) * sin_high
    )


def pairs_down(values):
    return jnp.concatenate(
        [values[:, p * 128 : (p + 1) * 128] for p in range(values.shape[1] // 128)], axis=0
    )


def gelu_parts(lifted):
    cdf = 0.5 + 0.5 * lax.erf(lifted * 0.7071067811865476)
    slope = cdf + lifted * (0.3989422804014327 * jnp.exp(-0.5 * lifted * lifted))
    return lifted * cdf, slope


def first_kernel(x_ref, gain_ref, off_ref, w_ref, b_ref, tab_ref, na_ref, nm_ref, q_ref, kv_ref):
    tokens, width = x_ref.shape
    unit = unit_rows(x_ref[...].astype(f32))[0]
    norm_a = (unit * gain_ref[0:1] + off_ref[0:1]).astype(bf16)
    na_ref[...] = norm_a
    nm_ref[...] = (unit * gain_ref[1:2] + off_ref[1:2]).astype(bf16)
    cos_tab, sin_low, sin_high = tab_ref[0], tab_ref[1], tab_ref[2]
    kv = dot_nn(norm_a, w_ref[:, width:]) + b_ref[:, width:]
    low_half = lax.broadcasted_iota(jnp.int32, kv.shape, 1) < 64
    kv = jnp.where(low_half, turn(kv, cos_tab, sin_low, sin_high), kv).astype(bf16)
    group = kv_ref.shape[0]
    for s in range(tokens // group):
        kv_ref[:, s * 128 : (s + 1) * 128] = kv[s * group : (s + 1) * group]
    proj = dot_nn(norm_a, w_ref[:, :width]) + b_ref[:, :width]
    for p in range(width // 128):
        cols = slice(p * 128, (p + 1) * 128)
        q_ref[:, cols] = (turn(proj[:, cols], cos_tab, sin_low, sin_high) * SCALE).astype(bf16)


def first_call(x, gains, offs, w_qkv, b_qkv, tab, group):
    tokens, width = x.shape
    operands = (x, gains, offs, w_qkv, b_qkv.reshape(1, -1), tab)
    shapes = [(tokens, width)] * 3 + [(group, tokens // group * 128)]
    return invoke(
        first_kernel,
        operands,
        (),
        grid=(1,),
        in_specs=[full_spec(v.shape) for v in operands],
        out_specs=[full_spec(v) for v in shapes],
        out_shape=[jax.ShapeDtypeStruct(v, bf16) for v in shapes],
        name="first",
        us=3,
    )


def mlp_fwd_kernel(nm_ref, up_ref, bup_ref, down_ref, y_ref, act_ref, slope_ref):
    lifted = dot_nn(nm_ref[...], up_ref[0]) + bup_ref[...]
    active, slope = gelu_parts(lifted)
    active = active.astype(bf16)
    act_ref[...] = active
    slope_ref[...] = slope.astype(bf16)

    @pl.when(pl.program_id(0) == 0)
    def _():
        y_ref[...] = jnp.zeros_like(y_ref)

    y_ref[...] += dot_nn(active, down_ref[0])


def mlp_fwd_call(nm, w_up, b_up, w_down, layer):
    tokens, width = nm.shape
    hidden = w_up.shape[2]
    return invoke(
        mlp_fwd_kernel,
        (nm, w_up, b_up[layer : layer + 1], w_down),
        (),
        grid=(hidden // TILE,),
        in_specs=[
            full_spec((tokens, width)),
            pl.BlockSpec((1, width, TILE), lambda t: (layer, 0, t)),
            pl.BlockSpec((1, TILE), lambda t: (0, t)),
            pl.BlockSpec((1, TILE, width), lambda t: (layer, t, 0)),
        ],
        out_specs=[
            full_spec((tokens, width)),
            pl.BlockSpec((tokens, TILE), lambda t: (0, t)),
            pl.BlockSpec((tokens, TILE), lambda t: (0, t)),
        ],
        out_shape=[
            jax.ShapeDtypeStruct((tokens, width), f32),
            jax.ShapeDtypeStruct((tokens, hidden), bf16),
            jax.ShapeDtypeStruct((tokens, hidden), bf16),
        ],
        name="mlp_fwd",
        us=10,
    )


def mlp_grads(active, slope, nm, nm_turned, grad, up, down, start, refs):
    grad_norm_ref, rows_ref, bias_ref = refs
    grad_lifted = (dot_nt(grad, down) * slope).astype(bf16)
    bias_ref[...] = jnp.sum(grad_lifted.astype(f32), axis=0, keepdims=True)

    @pl.when(pl.program_id(0) == 0)
    def _():
        grad_norm_ref[...] = jnp.zeros_like(grad_norm_ref) if start is None else start[...]
        nm_turned[...] = nm.T

    grad_norm_ref[...] += dot_nt(grad_lifted, up)
    grad_down = dot_tn(active, grad).astype(bf16)
    grad_up = dot_nn(nm_turned[...], grad_lifted).astype(bf16)
    for j in range(2):
        rows = slice(j * QUARTER, (j + 1) * QUARTER)
        rows_ref[0, 2 * j * QUARTER : (2 * j + 1) * QUARTER] = grad_down[rows]
        rows_ref[0, (2 * j + 1) * QUARTER : (2 * j + 2) * QUARTER] = grad_up[rows]


def mlp_both_kernel(more, core_ref, nm_ref, g_ref, up_ref, bup_ref, down_ref, *refs):
    y_start, grad_start = refs[:2] if more else (None, None)
    y_ref, *outs, nm_turned = refs[2:] if more else refs
    nm, up, down = nm_ref[...], up_ref[0], down_ref[0]
    active, slope = gelu_parts(dot_nn(nm, up) + bup_ref[...])
    active = active.astype(bf16)

    @pl.when(pl.program_id(0) == 0)
    def _():
        y_ref[...] = y_start[...] if more else jnp.zeros_like(y_ref)

    y_ref[...] += dot_nn(active, down)
    mlp_grads(active, slope, nm, nm_turned, g_ref[...], up, down, grad_start, outs)


def mlp_back_kernel(more, core_ref, nm_ref, g_ref, up_ref, down_ref, act_ref, slope_ref, *refs):
    grad_start = refs[0] if more else None
    *outs, nm_turned = refs[1:] if more else refs
    slope = slope_ref[...].astype(f32)
    mlp_grads(
        act_ref[...], slope, nm_ref[...], nm_turned, g_ref[...], up_ref[0], down_ref[0], grad_start, outs
    )


def mlp_back_call(core, nm, grad, w_up, w_down, layer, b_up=None, kept=None, before=None, deps=()):
    tokens, width = nm.shape
    hidden = w_up.shape[2]
    half = hidden // TILE // 2
    other = before is None

    def tile(t, core_ref):
        c = core_ref[0]
        return (1 - c if other else c) * half + t

    whole = full_spec((tokens, width))
    whole_shape = jax.ShapeDtypeStruct((tokens, width), f32)
    up_spec = pl.BlockSpec((1, width, TILE), lambda t, c: (layer, 0, tile(t, c)))
    down_spec = pl.BlockSpec((1, TILE, width), lambda t, c: (layer, tile(t, c), 0))
    cols_spec = pl.BlockSpec((tokens, TILE), lambda t, c: (0, tile(t, c)))
    both = kept is None
    if both:
        bias_spec = pl.BlockSpec((1, TILE), lambda t, c: (0, tile(t, c)))
        in_specs = [whole, whole, up_spec, bias_spec, down_spec]
        operands = (nm, grad, w_up, b_up[layer : layer + 1], w_down)
    else:
        in_specs = [whole, whole, up_spec, down_spec, cols_spec, cols_spec]
        operands = (nm, grad, w_up, w_down) + kept
    before = tuple(before or ())
    count = 2 if both else 1
    return invoke(
        partial(mlp_both_kernel if both else mlp_back_kernel, not other),
        operands + before,
        deps,
        scalars=(core,),
        grid=(half,),
        in_specs=in_specs + [whole] * len(before),
        out_specs=[whole] * count
        + [
            pl.BlockSpec((1, 2 * TILE, width), lambda t, c: (t, 0, 0)),
            pl.BlockSpec((1, TILE), lambda t, c: (0, t)),
        ],
        out_shape=[whole_shape] * count
        + [
            jax.ShapeDtypeStruct((half, 2 * TILE, width), bf16),
            jax.ShapeDtypeStruct((1, hidden // 2), f32),
        ],
        scratch=[pltpu.VMEM((width, tokens), bf16)],
        name="mlp_both" if both else "mlp_back",
        us=40 if both else 12,
    )


def spread_kv(pieces, order_ref, k0, k1, turned, forward):
    at = 0
    for ref in pieces:
        for p in range(ref.shape[0]):
            kv = ref[p].astype(f32)
            rows = kv.shape[0]
            swapped = pltpu.roll(kv, 64, 1)
            low_half = lax.broadcasted_iota(jnp.int32, kv.shape, 1) < 64
            zero = jnp.zeros_like(kv)
            block = order_ref[1 + at]
            place = pl.ds(pl.multiple_of(block * rows, rows), rows)
            k0[place] = jnp.where(low_half, kv, zero).astype(bf16)
            k1[place] = jnp.where(low_half, zero, swapped).astype(bf16)
            if forward:
                t0, t1 = turned
                rest = jnp.ones((64, rows), f32)
                part = kv.T[64:]
            else:
                v0, v1, t0, t1 = turned
                v0[place] = jnp.where(low_half, swapped, zero).astype(bf16)
                v1[place] = jnp.where(low_half, zero, kv).astype(bf16)
                rest = jnp.zeros((64, rows), f32)
                part = kv.T[:64]
            t0[block] = jnp.concatenate([part, rest], axis=0).astype(bf16)
            t1[block] = jnp.concatenate([rest, part], axis=0).astype(bf16)
            at += 1


def block_rows(index):
    return pl.ds(pl.multiple_of(index * KB, KB), KB)


def turned_block(ref, index):
    return jnp.concatenate([ref[2 * index], ref[2 * index + 1]], axis=1)


def visible(shape, first, start, group):
    key = lax.broadcasted_iota(jnp.int32, shape, 0)
    token = lax.broadcasted_iota(jnp.int32, shape, 1) % group
    return key - token <= first - start


def attend_kernel(count, first_ref, q_ref, *refs):
    pieces, (o_ref, lse_ref, k0, k1, t0, t1) = refs[:count], refs[count:]
    first = first_ref[0]
    group, width = q_ref.shape
    spread_kv(pieces, first_ref, k0, k1, (t0, t1), True)
    q6 = pairs_down(q_ref[...])
    full = first // KB

    def block(kb, carry):
        done = []
        for keys, vals, (top, summed) in zip((k0, k1), (t0, t1), carry or (2 * ((None, None),))):
            scores = dot_nt(keys[block_rows(kb), :], q6)
            if carry is None:
                scores = jnp.where(
                    visible(scores.shape, first, full * KB, group), scores, NEGATIVE
                )
            new_top = jnp.max(scores, axis=0, keepdims=True)
            if carry is not None:
                new_top = jnp.maximum(top, new_top)
            weights = jnp.exp(scores - new_top).astype(bf16)
            part = dot_nn(turned_block(vals, kb), weights)
            if carry is not None:
                part = part + summed * jnp.exp(top - new_top)
            done.append((new_top, part))
        return tuple(done)

    (top0, sum0), (top1, sum1) = lax.fori_loop(0, full, block, block(full, None))
    total0, total1 = sum0[64:65], sum1[0:1]
    both = jnp.concatenate([sum0[:64] / total0, sum1[64:] / total1], axis=0).T.astype(bf16)
    for p in range(width // 128):
        o_ref[:, p * 128 : (p + 1) * 128] = both[p * group : (p + 1) * group]
    shape = lse_ref.shape[2:]
    lse_ref[0, 0] = jnp.broadcast_to(top0 + jnp.log(total0), shape)
    lse_ref[0, 1] = jnp.broadcast_to(top1 + jnp.log(total1), shape)


def piece_specs(kv):
    return [pl.BlockSpec(v.shape[:2] + (128,), lambda s, f: (0, 0, s)) for v in kv]


def attend_call(first, q, kv, deps=()):
    tokens, width = q.shape
    length = sum(v.shape[0] for v in kv) * kv[0].shape[1]
    seqs = kv[0].shape[2] // 128
    group = tokens // seqs
    rows = group * width // 128
    return invoke(
        partial(attend_kernel, len(kv)),
        (q,) + kv,
        deps,
        scalars=(first,),
        grid=(seqs,),
        in_specs=[pl.BlockSpec((group, width), lambda s, f: (s, 0))] + piece_specs(kv),
        out_specs=[
            pl.BlockSpec((group, width), lambda s, f: (s, 0)),
            pl.BlockSpec((1, 2, 8, rows), lambda s, f: (s, 0, 0, 0)),
        ],
        scratch=[pltpu.VMEM((length, 128), bf16)] * 2
        + [pltpu.VMEM((length // 128, 128, 128), bf16)] * 2,
        out_shape=[
            jax.ShapeDtypeStruct((tokens, width), bf16),
            jax.ShapeDtypeStruct((seqs, 2, 8, rows), f32),
        ],
        name="attend",
        us=60,
    )


def attend_back_kernel(count, has_start, first_ref, q_ref, *refs):
    pieces, refs = refs[:count], refs[count:]
    if has_start:
        o_ref, do_ref, lse_ref, tab_ref, start_ref, dq_out, dkv_ref, k0, k1, v0, v1, t0, t1, dq_ref = refs
        dkv_ref[...] = start_ref[...]
    else:
        o_ref, do_ref, lse_ref, tab_ref, dq_out, dkv_ref, k0, k1, v0, v1, t0, t1, dq_ref = refs
        dkv_ref[...] = jnp.zeros_like(dkv_ref)
    first = first_ref[0]
    group = q_ref.shape[0]
    spread_kv(pieces, first_ref, k0, k1, (v0, v1, t0, t1), False)
    q6 = pairs_down(q_ref[...])
    do6 = pairs_down(do_ref[...])
    deltas = (do6.astype(f32) * pairs_down(o_ref[...]).astype(f32)).T
    halves = (
        (k0, v0, lse_ref[0, 0, 0:1], jnp.sum(deltas[:64], axis=0, keepdims=True)),
        (k1, v1, lse_ref[0, 1, 0:1], jnp.sum(deltas[64:], axis=0, keepdims=True)),
    )
    dq_ref[...] = jnp.zeros_like(dq_ref)
    full = first // KB
    low_half = lax.broadcasted_iota(jnp.int32, (KB, 128), 1) < 64

    def block(kb, masked):
        rows = block_rows(kb)
        grads, keys, vals = [], [], []
        for k, v, lse, delta in halves:
            probs = jnp.exp(dot_nt(k[rows, :], q6) - lse)
            if masked:
                probs = jnp.where(visible(probs.shape, first, full * KB, group), probs, 0.0)
            grad_probs = dot_nt(v[rows, :], do6)
            grad_scores = (probs * (grad_probs - delta)).astype(bf16)
            grads.append(grad_scores)
            keys.append(dot_nn(grad_scores, q6))
            vals.append(dot_nn(probs.astype(bf16), do6))
        dkv_ref[rows, :] += jnp.where(low_half, keys[0], vals[1]) + pltpu.roll(
            jnp.where(low_half, vals[0], keys[1]), 64, 1
        )
        turned = jnp.concatenate([turned_block(t0, kb), turned_block(t1, kb)], axis=1)
        dq_ref[...] += dot_nn(turned, jnp.concatenate(grads, axis=0))

    block(full, True)

    def step(kb, carry):
        block(kb, False)
        return carry

    lax.fori_loop(0, full, step, 0)
    cos_tab, sin_low, sin_high = tab_ref[0], -tab_ref[1], -tab_ref[2]
    dq = dq_ref[...].T * SCALE
    for p in range(q_ref.shape[1] // 128):
        part = dq[p * group : (p + 1) * group]
        dq_out[:, p * 128 : (p + 1) * 128] = turn(part, cos_tab, sin_low, sin_high).astype(bf16)


def attend_back_call(first, q, kv, attended, grad, lse, tab, start=None, deps=()):
    tokens, width = q.shape
    length = sum(v.shape[0] for v in kv) * kv[0].shape[1]
    seqs = kv[0].shape[2] // 128
    group = tokens // seqs
    rows = group * width // 128
    tok_spec = pl.BlockSpec((group, width), lambda s, f: (s, 0))
    len_spec = pl.BlockSpec((length, 128), lambda s, f: (0, s))
    in_specs = [
        tok_spec,
        *piece_specs(kv),
        tok_spec,
        tok_spec,
        pl.BlockSpec((1, 2, 8, rows), lambda s, f: (s, 0, 0, 0)),
        pl.BlockSpec((3, group, 128), lambda s, f: (0, s, 0)),
    ]
    operands = [q, *kv, attended, grad, lse, tab]
    if start is not None:
        in_specs.append(len_spec)
        operands.append(start)
    return invoke(
        partial(attend_back_kernel, len(kv), start is not None),
        operands,
        deps,
        scalars=(first,),
        grid=(seqs,),
        in_specs=in_specs,
        out_specs=[tok_spec, len_spec],
        scratch=[pltpu.VMEM((length, 128), bf16)] * 4
        + [pltpu.VMEM((length // 128, 128, 128), bf16)] * 2
        + [pltpu.VMEM((128, rows), f32)],
        out_shape=[
            jax.ShapeDtypeStruct((tokens, width), bf16),
            jax.ShapeDtypeStruct((length, seqs * 128), f32),
        ],
        name="attend_back",
        us=90,
    )


def back_kernel(g_ref, w_ref, out_ref):
    out_ref[...] = dot_nt(g_ref[...], w_ref[0]).astype(bf16)


def back_call(grad, w_out, layer, deps=()):
    tokens, width = grad.shape
    return invoke(
        back_kernel,
        (grad, w_out),
        deps,
        grid=(1,),
        in_specs=[full_spec((tokens, width)), layer_spec((width, width), layer)],
        out_specs=full_spec((tokens, width)),
        out_shape=jax.ShapeDtypeStruct((tokens, width), bf16),
        name="back",
    )


def middle_kernel(
    att_ref, x_ref, y_ref, wo_ref, bias_ref, gain_ref, off_ref, wq_ref, bq_ref, tab_ref,
    x2_ref, na_ref, nm_ref, q_ref,
):
    second = (
        x_ref[...].astype(f32) + dot_nn(att_ref[...], wo_ref[0]) + y_ref[...] + bias_ref[...]
    ).astype(bf16)
    x2_ref[...] = second
    unit = unit_rows(second.astype(f32))[0]
    norm_a = (unit * gain_ref[0:1] + off_ref[0:1]).astype(bf16)
    na_ref[...] = norm_a
    nm_ref[...] = (unit * gain_ref[1:2] + off_ref[1:2]).astype(bf16)
    proj = dot_nn(norm_a, wq_ref[...]) + bq_ref[...]
    cos_tab, sin_low, sin_high = tab_ref[0], tab_ref[1], tab_ref[2]
    for p in range(proj.shape[1] // 128):
        cols = slice(p * 128, (p + 1) * 128)
        q_ref[:, cols] = (turn(proj[:, cols], cos_tab, sin_low, sin_high) * SCALE).astype(bf16)


def middle_call(att, x, y, w_out, bias, gains, offs, w_q2, b_q2, tab):
    tokens, width = x.shape
    operands = (att, x, y, w_out, bias, gains, offs, w_q2, b_q2.reshape(1, -1), tab)
    specs = [full_spec(v.shape) for v in operands]
    specs[3] = layer_spec((width, width), 0)
    return invoke(
        middle_kernel,
        operands,
        (),
        grid=(1,),
        in_specs=specs,
        out_specs=[full_spec((tokens, width))] * 4,
        out_shape=[jax.ShapeDtypeStruct((tokens, width), bf16)] * 4,
        name="middle",
        us=5,
    )


def norm_back(values, grad_a, grad_m, gain_ref, small_ref, row):
    unit, inverse = unit_rows(values)
    small_ref[row : row + 1] = jnp.sum(grad_a * unit, axis=0, keepdims=True)
    small_ref[row + 1 : row + 2] = jnp.sum(grad_m * unit, axis=0, keepdims=True)
    small_ref[row + 2 : row + 3] = jnp.sum(grad_a, axis=0, keepdims=True)
    small_ref[row + 3 : row + 4] = jnp.sum(grad_m, axis=0, keepdims=True)
    grad_unit = grad_a * gain_ref[0:1] + grad_m * gain_ref[1:2]
    return inverse * (
        grad_unit
        - jnp.mean(grad_unit, axis=-1, keepdims=True)
        - unit * jnp.mean(grad_unit * unit, axis=-1, keepdims=True)
    )


def turn_kernel(
    x2_ref, y_ref, att2_ref, att1_ref, g_ref, na_ref, dq_ref, dnm_ref, wo1_ref, wo2_ref, wq_ref, bias_ref, gain_ref,
    hidden_ref, grads_ref, g1_ref, do1_ref, small_ref,
):
    width = x2_ref.shape[1]
    second = x2_ref[...].astype(f32)
    att2, grad, dq = att2_ref[...], g_ref[...], dq_ref[...]
    wide = grad.astype(f32)
    small_ref[...] = jnp.zeros_like(small_ref)
    grad_a = dot_nt(dq, wq_ref[...])
    g1 = (norm_back(second, grad_a, dnm_ref[...], gain_ref, small_ref, 0) + wide).astype(bf16)
    g1_ref[...] = g1
    do1_ref[...] = dot_nt(g1, wo1_ref[0]).astype(bf16)
    small_ref[4:5] = jnp.sum(wide, axis=0, keepdims=True)
    small_ref[5:6] = jnp.sum(dq.astype(f32), axis=0, keepdims=True)
    small_ref[6:7] = jnp.sum(g1.astype(f32), axis=0, keepdims=True)
    grads_ref[0:width] = dot_tn(att2, grad).astype(bf16)
    grads_ref[width : 2 * width] = dot_tn(na_ref[...], dq).astype(bf16)
    grads_ref[2 * width : 3 * width] = dot_tn(att1_ref[...], g1).astype(bf16)
    hidden_ref[...] = (second + dot_nn(att2, wo2_ref[0]) + y_ref[...] + bias_ref[...]).astype(bf16)


def turn_call(x2, y2, att2, att1, g, na2, dq2, dnm2, w_out, w_q2, bias, gains, deps=()):
    tokens, width = x2.shape
    operands = (x2, y2, att2, att1, g, na2, dq2, dnm2, w_out, w_out, w_q2, bias, gains)
    specs = [full_spec(v.shape) for v in operands]
    specs[8] = layer_spec((width, width), 0)
    specs[9] = layer_spec((width, width), 1)
    tok = full_spec((tokens, width))
    tok_shape = jax.ShapeDtypeStruct((tokens, width), bf16)
    return invoke(
        turn_kernel,
        operands,
        deps,
        grid=(1,),
        in_specs=specs,
        out_specs=[tok, full_spec((3 * width, width)), tok, tok, full_spec((8, width))],
        out_shape=[
            tok_shape,
            jax.ShapeDtypeStruct((3 * width, width), bf16),
            tok_shape,
            tok_shape,
            jax.ShapeDtypeStruct((8, width), f32),
        ],
        name="turn",
        us=60,
    )


def last_kernel(
    x_ref, g1_ref, na_ref, dq_ref, dkv_ref, dnm_ref, w_ref, gain_ref, tab_ref, grad_ref, grads_ref, small_ref
):
    tokens, width = x_ref.shape
    group = dkv_ref.shape[0]
    dkv = jnp.concatenate(
        [dkv_ref[:, s * 128 : (s + 1) * 128] for s in range(tokens // group)], axis=0
    ).astype(f32)
    low_half = lax.broadcasted_iota(jnp.int32, dkv.shape, 1) < 64
    dkv = jnp.where(low_half, turn(dkv, tab_ref[0], -tab_ref[1], -tab_ref[2]), dkv).astype(bf16)
    dq, norm_a = dq_ref[...], na_ref[...]
    small_ref[...] = jnp.zeros_like(small_ref)
    small_ref[4:5] = jnp.sum(dq.astype(f32), axis=0, keepdims=True)
    small_ref[5:6, 0:128] = jnp.sum(dkv.astype(f32), axis=0, keepdims=True)
    grads_ref[0:width] = dot_tn(norm_a, dq).astype(bf16)
    grads_ref[width : width + 128] = dot_tn(dkv, norm_a).astype(bf16)
    grad_a = dot_nt(dq, w_ref[:, :width]) + dot_nt(dkv, w_ref[:, width:])
    grad_ref[...] = g1_ref[...].astype(f32) + norm_back(
        x_ref[...].astype(f32), grad_a, dnm_ref[...], gain_ref, small_ref, 0
    )


def last_call(x, g1, na1, dq1, dkv, dnm1, w_qkv, gains, tab, deps=()):
    tokens, width = x.shape
    operands = (x, g1, na1, dq1, dkv, dnm1, w_qkv, gains, tab)
    out_shape = [
        jax.ShapeDtypeStruct((tokens, width), f32),
        jax.ShapeDtypeStruct((width + 128, width), bf16),
        jax.ShapeDtypeStruct((8, width), f32),
    ]
    return invoke(
        last_kernel,
        operands,
        deps,
        grid=(1,),
        in_specs=[full_spec(v.shape) for v in operands],
        out_specs=[full_spec(v.shape) for v in out_shape],
        out_shape=out_shape,
        name="last",
        us=10,
    )


PAIR = [(0, 1), (1, 0)]


def swap(values, axis):
    return lax.ppermute(values, axis, PAIR)


def add_low(first, *rest):
    total = first.astype(f32)
    for value in rest:
        total = total + value.astype(f32)
    return total.astype(bf16)


def pick(values, index):
    return lax.dynamic_index_in_dim(values, index, 0, keepdims=False)


def square():
    return lax.axis_size("b0") == 2 and lax.axis_size("b1") == 2 and lax.axis_size(Z) == 4


def turns(values_at):
    size = lax.axis_size(Z)
    return [
        lax.ppermute(values_at(k), Z, [(i, (i + k) % size) for i in range(size)])
        for k in range(1, size)
    ]


def reduce_offloaded(part):
    part = lax.psum_scatter(part, B, scatter_dimension=0, tiled=True)
    return lax.psum_scatter(part, Z, scatter_dimension=0, tiled=True)


def gather_offloaded(part):
    return lax.all_gather(part, (C,) + B + (Z,), axis=0, tiled=True)


def combine(groups, where, deps, grid=(1,), name="combine", us=2):
    terms = [t for sums, *_ in groups for parts in sums for t in parts]

    def kernel(where_ref, *refs):
        ins, outs = iter(refs[: len(terms)]), refs[len(terms) :]
        for (sums, *_), out_ref in zip(groups, outs):
            for i, parts in enumerate(sums):
                total = next(ins)[...].astype(f32)
                for _ in parts[1:]:
                    total = total + next(ins)[...].astype(f32)
                if len(sums) == 1:
                    out_ref[...] = total.reshape(out_ref.shape).astype(bf16)
                else:
                    out_ref[i] = total.reshape(out_ref.shape[1:]).astype(bf16)

    return invoke(
        kernel,
        [t[0] for t in terms],
        deps,
        scalars=(where,),
        grid=grid,
        in_specs=[pl.BlockSpec(t[1], t[2]) for t in terms],
        out_specs=[pl.BlockSpec(g[1], g[2]) for g in groups],
        out_shape=[jax.ShapeDtypeStruct(g[3], bf16) for g in groups],
        name=name,
        us=us,
    )


def sum_cores(keep, got, where, deps=()):
    width = keep.shape[-1]
    keep, got = (v.reshape(2, 2, 2, -1, width) for v in (keep, got))
    quarter = keep.shape[3]
    half = quarter // 2
    maps = (
        lambda i, j, w: (i, 1 - w[1], 0, j, 0),
        lambda i, j, w: (i, w[1], 0, j, 0),
        lambda i, j, w: (1 - w[0], i, 1, j, 0),
        lambda i, j, w: (w[0], i, 1, j, 0),
    )
    block = (1, 1, 1, half, width)
    groups = [
        (
            [[(keep, block, m), (got, block, m)]],
            (1, half, width),
            lambda i, j, w: (i, j, 0),
            (2, quarter, width),
        )
        for m in maps
    ]
    return combine(groups, where, deps, grid=(2, 2), name="sum_cores")


def sum_first(one, one_got, two, two_got, where, deps=()):
    _, quarter, width = one.shape
    half = quarter // 2
    groups = []
    for values, got, m in (
        (one, one_got, lambda j, w: (1 - w[0], j, 0)),
        (one, one_got, lambda j, w: (w[0], j, 0)),
        (two, two_got, lambda j, w: (1 - w[1], j, 0)),
        (two, two_got, lambda j, w: (w[1], j, 0)),
    ):
        block = (1, half, width)
        groups.append(
            ([[(values, block, m), (got, block, m)]], block, lambda j, w: (0, j, 0), (1, quarter, width))
        )
    return combine(groups, where, deps, grid=(2,), name="sum_first")


def sum_second(one, one_got, two, two_got, where, deps=()):
    width = one.shape[-1]
    one, one_got, two, two_got = (v.reshape(4, -1, width) for v in (one, one_got, two, two_got))
    block = (1,) + one.shape[1:]
    groups = []
    for k in range(4):
        m = lambda i, w, k=k: (lax.rem(w[2] + k, 4), 0, 0)
        groups.append(
            (
                [[(a, block, m), (b, block, m)] for a, b in ((one, one_got), (two, two_got))],
                (2,) + one.shape[1:],
                lambda i, w: (0, 0, 0),
                (2,) + one.shape[1:],
            )
        )
    return combine(groups, where, deps, name="sum_second", us=100)


def sum_third(parts, where, deps=()):
    shape = parts[0].shape
    m = lambda i, w: (0, 0, 0)
    return combine([([[(p, shape, m) for p in parts]], shape, m, shape)], where, deps, name="sum_third")[0]


def join(parts, leads, where, deps=()):
    shape = parts[0].shape[1:]
    groups = [
        (
            [[(p, (1,) + shape, lambda i, w, a=a: (a,) + (0,) * len(shape))] for p in parts],
            (len(parts),) + shape,
            lambda i, w: (0,) * (len(shape) + 1),
            (len(parts),) + shape,
        )
        for a in leads
    ]
    return combine(groups, where, deps, name="join")


def gather_blocks(both):
    return lax.all_gather(both, (C,) + B + (Z,), axis=0, tiled=False)


def place_kernel(count, quarter, where_ref, *refs):
    ins, out_ref = refs[:count], refs[-1]
    step = pl.program_id(0)
    z = where_ref[2 * count]
    unit = quarter // 4
    for a in range(count):

        @pl.when(step // 2 == a)
        def _():
            for k in range(4):
                rows = pl.ds(pl.multiple_of(lax.rem(z - k + 4, 4) * unit, 16), unit)
                out_ref[0, rows] = ins[a][k * unit : (k + 1) * unit].astype(f32)


def place_relative(parts, out_map, out_shape, before, deps=()):
    values = [v for v, _ in parts]
    count, width = len(parts), values[0].shape[1]
    quarter = values[0].shape[0] // 2
    where = jnp.stack([m for _, marks in parts for m in marks] + [lax.axis_index(Z)])
    return invoke(
        partial(place_kernel, count, quarter),
        values + [before],
        deps,
        scalars=(where.astype(jnp.int32),),
        grid=(2 * count,),
        in_specs=[
            pl.BlockSpec((quarter, width), lambda i, w, a=a: (jnp.clip(i - 2 * a, 0, 1), 0))
            for a in range(count)
        ]
        + [pl.BlockSpec(memory_space=pl.ANY)],
        out_specs=pl.BlockSpec((1, quarter, width), lambda i, w: out_map(w[i])),
        out_shape=jax.ShapeDtypeStruct(out_shape, f32),
        aliases={1 + count: 0},
        name="place",
        us=6,
    )


def spread_kernel(z_first, in_ref, *refs):
    down_ref, up_ref = refs[-2:]
    unit = QUARTER // 4
    for z in range(4):
        rows = slice(z * unit, (z + 1) * unit)
        down_ref[0, rows] = (in_ref[0, z, 0] if z_first else in_ref[0, 0, z]).astype(f32)
        up_ref[0, rows] = (in_ref[0, z, 1] if z_first else in_ref[0, 1, z]).astype(f32)


def place_ordered(rows, layer, before=None, z_first=False, deps=()):
    width = rows.shape[-1]
    hidden = rows.size // width // 2
    inner = (4, 2) if z_first else (2, 4)
    rows = rows.reshape((hidden // QUARTER,) + inner + (QUARTER // 4, width))
    return invoke(
        partial(spread_kernel, z_first),
        [rows] + list(before or ()),
        deps,
        grid=(hidden // QUARTER,),
        in_specs=[pl.BlockSpec((1,) + rows.shape[1:], lambda i: (i, 0, 0, 0, 0))]
        + [pl.BlockSpec(memory_space=pl.ANY)] * len(before or ()),
        out_specs=[
            pl.BlockSpec((1, QUARTER, width), lambda i: (layer, i, 0)),
            pl.BlockSpec((1, QUARTER, TILE), lambda i: (layer, i % 2, i // 2)),
        ],
        out_shape=[
            jax.ShapeDtypeStruct((2, hidden, width), f32),
            jax.ShapeDtypeStruct((2, width, hidden), f32),
        ],
        aliases={1: 0, 2: 1} if before else {},
        name="spread",
        us=10,
    )


def finish_kernel(in_ref, out_ref, q2_ref, qkv_ref, small_ref, flat):
    width = out_ref.shape[2]
    size = in_ref.shape[2]
    for w in range(8):
        for two in range(2):
            for z in range(4):
                at = ((w * 2 + two) * 4 + z) * size
                flat[at : at + size] = in_ref[w * 4 + z, two].astype(f32)
    half = flat.shape[0] // 2
    rest = half - 2 * width
    out_ref[1] = flat[:width]
    q2_ref[...] = flat[width : 2 * width]
    out_ref[0] = flat[half : half + width]
    qkv_ref[:, :width] = flat[half + width : half + 2 * width]
    qkv_ref[:, width:] = flat[2 * width : 2 * width + 128].T
    small_ref[: rest - 128] = flat[2 * width + 128 : half]
    small_ref[rest - 128 :] = flat[half + 2 * width :]


def finish_call(blocks, deps=()):
    width = blocks.shape[-1]
    rows = blocks.size // width
    shapes = [(2, width, width), (width, width), (width, width + 128), (rows - 4 * width - 128, width)]
    return invoke(
        finish_kernel,
        (blocks,),
        deps,
        grid=(1,),
        in_specs=[full_spec(blocks.shape)],
        out_specs=[full_spec(v) for v in shapes],
        out_shape=[jax.ShapeDtypeStruct(v, f32) for v in shapes],
        scratch=[pltpu.VMEM((rows, width), f32)],
        name="finish",
        us=6,
    )


def rotary_tables(positions):
    half_rot = ROT // 2
    inverse = BASE ** (-(jnp.arange(half_rot, dtype=f32) * 2.0 / ROT))
    angles = positions.astype(f32).reshape(-1, 1) * inverse
    cos, sin = jnp.cos(angles), jnp.sin(angles)
    zero = jnp.zeros_like(sin)
    rest = jnp.zeros((cos.shape[0], 64 - ROT), f32)
    head = [
        jnp.concatenate([cos, cos, rest + 1.0], axis=-1),
        jnp.concatenate([-sin, zero, rest], axis=-1),
        jnp.concatenate([zero, sin, rest], axis=-1),
    ]
    return jnp.stack([jnp.concatenate([h, h], axis=-1) for h in head])


def local(
    hidden_in,
    positions,
    cotangent,
    norm_gains,
    norm_biases,
    w_qkv,
    b_qkv,
    w_q2,
    b_q2,
    w_out,
    w_up,
    b_up,
    w_down,
    out_bias,
):
    seqs, group, width = hidden_in.shape
    tokens = seqs * group
    hidden = w_up.shape[2]
    y, x, z, core = (lax.axis_index(a) for a in ("b0", "b1", Z, C))
    core_row = core.reshape(1).astype(jnp.int32)
    where = jnp.stack([y, x, z, core]).astype(jnp.int32)
    direct = square()
    x1 = hidden_in.reshape(tokens, width)
    g2 = cotangent.reshape(tokens, width)
    tab = rotary_tables(positions)

    na1, nm1, q1, kv_own = first_call(x1, norm_gains[0], norm_biases[0], w_qkv, b_qkv, tab, group)
    if direct:
        got = turns(lambda k: kv_own)
        y1, act1, slope1 = mlp_fwd_call(nm1, w_up, b_up, w_down, 0)
        mine = join([v[None] for v in (kv_own, *got)], (0,), where, (y1,))[0]
        theirs = swap(mine, C)
        kv = (mine, theirs)
        back = (z - jnp.arange(4)) % 4 * 2
        order = jnp.concatenate([back + core, back + 1 - core])
        do2 = back_call(g2, w_out, 1, (mine,))
    else:
        kv = (lax.all_gather(kv_own, (Z, C), axis=0, tiled=False),)
        order = jnp.arange(kv[0].shape[0])
        y1, act1, slope1 = mlp_fwd_call(nm1, w_up, b_up, w_down, 0)
        do2 = back_call(g2, w_out, 1)
    first = jnp.concatenate([((z * 2 + core) * group).reshape(1), order]).astype(jnp.int32)
    att1, lse1 = attend_call(first, q1, kv, (do2,))
    x2, na2, nm2, q2 = middle_call(
        att1, x1, y1, w_out, out_bias[0:1], norm_gains[1], norm_biases[1], w_q2, b_q2, tab
    )
    y2, dnm2, send, bup_send = mlp_back_call(core_row, nm2, g2, w_up, w_down, 1, b_up=b_up)
    got = swap(send.reshape(hidden, width), C)
    y2, dnm2, keep, bup_keep = mlp_back_call(
        core_row, nm2, g2, w_up, w_down, 1, b_up=b_up, before=(y2, dnm2)
    )
    keep = keep.reshape(hidden, width)

    def in_order(own, other):
        both = jnp.concatenate([own, other], axis=0)
        return jnp.where(core == 0, both, jnp.concatenate([other, own], axis=0)).reshape(-1, width)

    bup2 = in_order(bup_keep, bup_send)

    def swaps(one, two, axes):
        return swap(one, axes[0]), swap(two, axes[1])

    wait = ()
    if direct:
        one_send, one, two_send, two = sum_cores(keep, got, where)
        one_got, two_got = swaps(one_send, two_send, ("b1", "b0"))
        wait = (one,)
    else:
        mlp2 = add_low(keep, got)
    att2, lse2 = attend_call(first, q2, kv, wait)
    dq2, dkv2 = attend_back_call(first, q2, kv, att2, do2, lse2, tab)
    if direct:
        one_send, one, two_send, two = sum_first(one, one_got, two, two_got, where, (dq2,))
        one_got, two_got = swaps(one_send, two_send, ("b0", "b1"))
        wait = (one,)
    hidden_out, grads2, g1, do1, small2 = turn_call(
        x2, y2, att2, att1, g2, na2, dq2, dnm2, w_out, w_q2, out_bias[1:2], norm_gains[1], deps=wait
    )
    if direct:
        parts = sum_second(one, one_got, two, two_got, where, (g1,))
        ahead = turns(lambda k: parts[k])
        wait = (parts[0],)
    dnm1, send, bup_send = mlp_back_call(
        core_row, nm1, g1, w_up, w_down, 0, kept=(act1, slope1), deps=wait
    )
    got = swap(send.reshape(hidden, width), C)
    dnm1, keep, bup_keep = mlp_back_call(
        core_row, nm1, g1, w_up, w_down, 0, kept=(act1, slope1), before=(dnm1,)
    )
    keep = keep.reshape(hidden, width)
    bup1 = in_order(bup_keep, bup_send)
    if direct:
        one_send, one, two_send, two = sum_cores(keep, got, where)
        one_got, two_got = swaps(one_send, two_send, ("b1", "b0"))
        mlp2 = sum_third([parts[0]] + ahead, where, (one,))
        wait = (mlp2,)
        mlp2 = gather_blocks(mlp2)
    dq1, dkv1 = attend_back_call(
        first, q1, kv, att1, do1, lse1, tab, dkv2, deps=wait + (dnm1,)
    )
    low = dkv1.astype(bf16)
    if direct:
        low = low.reshape(4, 2, group, -1)
        at = lambda c: lax.dynamic_index_in_dim(low, c, 1, keepdims=False)
        dkv_got = swap(at(1 - core), C)
        one_send, one, two_send, two = sum_first(one, one_got, two, two_got, where, (dq1,))
        one_got, two_got = swaps(one_send, two_send, ("b0", "b1"))
        block = (1,) + low.shape[2:]
        dkv_parts = combine(
            [
                (
                    [
                        [
                            (
                                low.reshape((8,) + low.shape[2:]),
                                block,
                                lambda i, w, k=k: (lax.rem(w[2] + k, 4) * 2 + w[3], 0, 0),
                            ),
                            (dkv_got, block, lambda i, w, k=k: (lax.rem(w[2] + k, 4), 0, 0)),
                        ]
                    ],
                    block,
                    lambda i, w: (0, 0, 0),
                    block,
                )
                for k in range(4)
            ],
            where,
            (one,),
            name="sum_kv",
        )
        dkv_got = turns(lambda k: dkv_parts[k])
        dkv = sum_third([dkv_parts[0]] + dkv_got, where)[0]
    else:
        dkv = lax.psum_scatter(low, (Z, C), scatter_dimension=0, tiled=True)
        mlp1 = add_low(keep, got)
    grad_input, grads1, small1 = last_call(x1, g1, na1, dq1, dkv, dnm1, w_qkv, norm_gains[0], tab)
    small = jnp.concatenate(
        [grads1[width:]] + [v.astype(bf16) for v in (small1, small2, bup1, bup2)], axis=0
    )
    extra = 256
    small = jnp.concatenate(
        [small, jnp.zeros((2 * extra - small.shape[0], width), bf16)], axis=0
    )
    rows = jnp.concatenate(
        [grads2[: 2 * width], small[:extra], grads2[2 * width :], grads1[:width], small[extra:]], axis=0
    ).reshape(2, -1, width)
    outs_keep, outs_got = pick(rows, core), swap(pick(rows, 1 - core), C)

    if direct:
        parts = sum_second(one, one_got, two, two_got, where, (grad_input,))
        ahead = turns(lambda k: parts[k])
        o1_send, o1, o2_send, o2 = sum_cores(outs_keep, outs_got, where, (parts[0],))
        o1_got, o2_got = swaps(o1_send, o2_send, ("b1", "b0"))
        both = sum_third([parts[0]] + ahead, where, (o1,))
        ahead = turns(lambda k: both)
        o1_send, o1, o2_send, o2 = sum_first(o1, o1_got, o2, o2_got, where, (both,))
        o1_got, o2_got = swaps(o1_send, o2_send, ("b0", "b1"))
        parts = sum_second(o1, o1_got, o2, o2_got, where)
        outs_ahead = turns(lambda k: parts[k])
        one, two = join([both] + ahead, (0, 1), where, (parts[0],))
        one_got, two_got = swaps(one, two, ("b0", "b1"))
        outs = sum_third([parts[0]] + outs_ahead, where, (one, mlp2))
        outs = gather_blocks(outs)
        one_near, two_near = (
            join([v[None], g[None]], (0,), where)[0].reshape(-1, width)
            for v, g in ((one, one_got), (two, two_got))
        )
        one_far, two_far = swaps(one_near, two_near, ("b1", "b0"))
        one_near_got, two_near_got = swap(one_near, C), swap(two_near, C)
        grad_down, grad_up = place_ordered(mlp2, 1, z_first=True, deps=(one_near, two_near))
        mark = lambda c, v, u: c * 4 + v * 2 + u
        down_map = lambda w: (0, w, 0)
        up_map = lambda w: (0, w % 2, w // 2)

        def down_marks(c, far):
            u = 1 - x if far else x
            return (mark(c, y, u), mark(c, 1 - y, u))

        def up_marks(c, far):
            v = 1 - y if far else y
            return (mark(c, v, x), mark(c, v, 1 - x))

        def put(down, up, one, two, far, cores):
            down = place_relative(
                [(o, down_marks(c, far)) for o, c in zip(one, cores)], down_map, down.shape, down
            )
            up = place_relative(
                [(t, up_marks(c, far)) for t, c in zip(two, cores)], up_map, up.shape, up
            )
            return down, up

        near_one, near_two = (one_near, one_near_got), (two_near, two_near_got)
        grad_down, grad_up = put(grad_down, grad_up, near_one, near_two, False, (core, 1 - core))
        one_far_got, two_far_got = swap(one_far, C), swap(two_far, C)
        grad_down, grad_up = put(grad_down, grad_up, (one_far,), (two_far,), True, (core,))
        grad_down, grad_up = put(
            grad_down, grad_up, (one_far_got,), (two_far_got,), True, (1 - core,)
        )
    else:
        mlp2 = gather_offloaded(reduce_offloaded(mlp2))
        placed = place_ordered(mlp2, 1)
        grad_down, grad_up = place_ordered(gather_offloaded(reduce_offloaded(mlp1)), 0, placed)
        outs = gather_offloaded(reduce_offloaded(add_low(outs_keep, outs_got)))
        outs = outs.reshape(8, 2, 4, -1, width).transpose(0, 2, 1, 3, 4).reshape(32, 2, -1, width)
    grad_out, grad_q2, grad_qkv, small = finish_call(outs)
    one, two = small[0:8], small[8:16]
    ups = hidden // width
    grad_up_bias = jnp.stack([small[16 : 16 + ups].reshape(-1), small[16 + ups : 16 + 2 * ups].reshape(-1)])
    grad_gains = jnp.stack([one[0:2], two[0:2]])
    grad_biases = jnp.stack([one[2:4], two[2:4]])
    grad_qkv_bias = jnp.concatenate([one[4], one[5, :128]])
    grad_out_bias = jnp.stack([two[6], two[4]])
    return (
        hidden_out.reshape(seqs, group, width),
        grad_input.reshape(seqs, group, width),
        grad_gains,
        grad_biases,
        grad_qkv,
        grad_qkv_bias,
        grad_q2,
        two[5],
        grad_out,
        grad_up,
        grad_up_bias,
        grad_down,
        grad_out_bias,
    )


def solution(mesh):
    batch, seq = mesh.shape["batch"], mesh.shape["seq"]
    fine = jax.sharding.Mesh(
        mesh.devices.reshape(2, batch // 2, seq // 2, 2), ("b0", "b1", "z", "c")
    )
    rows = P(B, (Z, C), None)
    return jax.shard_map(
        local,
        mesh=fine,
        in_specs=(rows, P(B, (Z, C)), rows) + (P(),) * 11,
        out_specs=(rows, rows) + (P(),) * 11,
        check_vma=False,
    )
```

time: 842 us -> 467 us (0.55)
  waiting for transfers between devices: 616 us -> 123 us
  starting transfers between devices: 1.64 us -> 84.1 us
  Pallas kernels: 138 us -> 196 us
  other arithmetic: 36.4 us -> 7.12 us
    reduce_scatter x9 -> x0, waiting for transfers between devices: 332 us -> none  [the longest x4 150 us: reduce_parts(): part = lax.psum_scatter(part, B, scatter_dimension=0, tiled=True)]
    all_gather x5 -> x2, waiting for transfers between devices: 270 us -> 0.01 us  [gather_blocks(): return lax.all_gather(both, (C,) + B + (Z,), axis=0, tiled=False)]
    ppermute x4 -> x43, waiting for transfers between devices: 12.7 us -> 123 us  [the longest x25 67.9 us: swap(): return lax.ppermute(values, axis, PAIR)]
    ppermute x4 -> x43, starting transfers between devices: 0.91 us -> 84 us  [the longest x18 67.2 us: turns(): lax.ppermute(values_at(k), Z, [(i, (i + k) % size) for i in range(size)])]
    pallas_call x13 -> x40, Pallas kernels: 138 us -> 196 us  [invoke(): pl.pallas_call(body, grid_spec=pltpu.PrefetchScalarGridSpec(num_scalar_pr...]
    convert_element_type x7 -> x5, other arithmetic: 25.6 us -> 1.93 us  [the longest x1 1.87 us: local(): low = dkv1.astype(bf16)]
    unnamed x59 -> x107, local copies, waits for them, and re-layouts: 14.4 us -> 23.9 us
  transfers between devices with their start and end apart: 18 -> 45, of which waited for: 16 -> 15; matrix products, arithmetic and copies ran while one was open for 4% -> 4% of each run, Pallas kernels for 5% -> 30%
where the time goes in v2:
time: 467 us; the launch traced here: 459 us
  Pallas kernels  196 us (42%)
  waiting for transfers between devices  123 us (26%)
  starting transfers between devices  84.1 us (18%)
  local copies, waits for them, and re-layouts  34.5 us (7%)
  between operations  15.3 us (3%)
  other arithmetic  7.12 us (2%)
    pallas_call x40, Pallas kernels, invoke(): pl.pallas_call(body, grid_spec=pltpu.PrefetchScalarGridSpec(num_scalar_pr...  196 us
    ppermute x25, waiting for transfers between devices, swap(): return lax.ppermute(values, axis, PAIR)  67.9 us
    ppermute x18, starting transfers between devices, turns(): lax.ppermute(values_at(k), Z, [(i, (i + k) % size) for i in range(size)])  67.2 us
    ppermute x18, waiting for transfers between devices, turns(): lax.ppermute(values_at(k), Z, [(i, (i + k) % size) for i in range(size)])  54.9 us
    unnamed x107, local copies, waits for them, and re-layouts  23.9 us
    ppermute x25, starting transfers between devices, swap(): return lax.ppermute(values, axis, PAIR)  16.8 us
  transfers between devices with their start and end apart: 45, of which 15 were waited for; matrix products, arithmetic and copies ran while one was open for 4% of the time, Pallas kernels for 30%

profile of v2, /device:TPU:0, one launch (start us, length us, event | category | flops | bytes accessed | tf_op | source)
XLA Modules:
  0.0 459.5 jit_solution(542734041389001129)
XLA Ops:
  22.3 11.6 %mlp_fwd.1 = (f32[512,768]{1,0:T(8,128)S(1)}, bf16[512,3072]{1,0:T(8,128)(2,1)}, bf16[512,3072]{1,0:T(8,128)(2,1)}) custom-call(bf16[512,768]{1,0:T(8,128)(2,1)S(1)} %get-tuple-element.104.refs_0_.refs_1_, bf16[2,768,3072]{2,1,0:T(8,128)(2,1)} %refs_3_.13, f32[1,3072]{1,0:T(1,128)S(1)} %get-tuple-element.204.refs_2_, bf16[2,3072,768]{2,1,0:T(8,128)(2,1)} %refs_4_.3), custom_call_target="tpu_custom_call" | custom-call | flops 6000000000 | bytes 10000000 | tf_op jit(solution)/shard_map/mlp_fwd/pallas_call | solution.py:47
  39.6 5.8 %attend.2 = (bf16[512,768]{1,0:T(8,128)(2,1)S(1)}, f32[4,2,8,768]{3,2,1,0:T(8,128)S(1)}) custom-call(s32[9]{0:T(128)S(1)} %pad_add_fusion.refs_0_, bf16[512,768]{1,0:T(8,128)(2,1)S(1)} %copy-done.31, bf16[4,128,512]{2,1,0:T(8,128)(2,1)S(1)} %join.4.refs_2_, bf16[4,128,512]{2,1,0:T(8,128)(2,1)S(1)} %collective-permute-done.3.refs_3_, ...), custom_call_target="tpu_custom_call" | custom-call | flops 35999997952 | bytes 60000000 | tf_op jit(solution)/shard_map/attend/pallas_call | solution.py:47
  45.5 5.5 %middle.1 = (bf16[512,768]{1,0:T(8,128)(2,1)S(1)}, bf16[512,768]{1,0:T(8,128)(2,1)S(1)}, bf16[512,768]{1,0:T(8,128)(2,1)S(1)}, bf16[512,768]{1,0:T(8,128)(2,1)S(1)}) custom-call(bf16[512,768]{1,0:T(8,128)(2,1)S(1)} %get-tuple-element.106.refs_0_.refs_3_.refs_4_, bf16[512,768]{1,0:T(8,128)(2,1)} %bitcast.109, f32[512,768]{1,0:T(8,128)} %copy-done.23, ...), custom_call_target="tpu_custom_call" | custom-call | flops 3000000000 | bytes 5000000 | tf_op jit(solution)/shard_map/middle/pallas_call | solution.py:47
  51.9 13.4 %mlp_both.2 = (f32[512,768]{1,0:T(8,128)S(1)}, f32[512,768]{1,0:T(8,128)}, bf16[2,1536,768]{2,1,0:T(8,128)(2,1)}, f32[1,1536]{1,0:T(1,128)S(1)}) custom-call(s32[1]{0:T(128)} %bitcast.11.refs_0_, bf16[512,768]{1,0:T(8,128)(2,1)S(1)} %get-tuple-element.108.refs_1_, bf16[512,768]{1,0:T(8,128)(2,1)S(1)} %bitcast.102, bf16[2,768,3072]{2,1,0:T(8,128)(2,1)} %refs_3_.13, ...), custom_call_target="tpu_custom_call" | custom-call | flops 24000000000 | bytes 40000000 | tf_op jit(solution)/shard_map/mlp_both/pallas_call | solution.py:47
  66.9 14.5 %mlp_both.3 = (f32[512,768]{1,0:T(8,128)S(1)}, f32[512,768]{1,0:T(8,128)}, bf16[2,1536,768]{2,1,0:T(8,128)(2,1)}, f32[1,1536]{1,0:T(1,128)S(1)}) custom-call(s32[1]{0:T(128)} %bitcast.11.refs_0_, bf16[512,768]{1,0:T(8,128)(2,1)S(1)} %get-tuple-element.108.refs_1_, bf16[512,768]{1,0:T(8,128)(2,1)S(1)} %bitcast.103, bf16[2,768,3072]{2,1,0:T(8,128)(2,1)} %refs_3_.13, ...), custom_call_target="tpu_custom_call" | custom-call | flops 24000000000 | bytes 40000000 | tf_op jit(solution)/shard_map/mlp_both/pallas_call | solution.py:47
  81.4 6.0 %sum_cores.3 = (bf16[2,384,768]{2,1,0:T(8,128)(2,1)S(1)}, bf16[2,384,768]{2,1,0:T(8,128)(2,1)S(1)}, bf16[2,384,768]{2,1,0:T(8,128)(2,1)S(1)}, bf16[2,384,768]{2,1,0:T(8,128)(2,1)}) custom-call(s32[4]{0:T(128)S(1)} %pad_add_fusion.1.refs_0_, bf16[2,2,2,384,768]{4,3,2,1,0:T(8,128)(2,1)} %bitcast.156, ...), custom_call_target="tpu_custom_call" | custom-call | flops 1200000000 | bytes 2000000 | tf_op jit(solution)/shard_map/sum_cores/pallas_call | solution.py:47
  90.5 5.9 %attend.3 = (bf16[512,768]{1,0:T(8,128)(2,1)S(1)}, f32[4,2,8,768]{3,2,1,0:T(8,128)S(1)}) custom-call(s32[9]{0:T(128)S(1)} %pad_add_fusion.refs_0_, bf16[512,768]{1,0:T(8,128)(2,1)S(1)} %get-tuple-element.112.refs_1_, bf16[4,128,512]{2,1,0:T(8,128)(2,1)S(1)} %join.4.refs_2_, bf16[4,128,512]{2,1,0:T(8,128)(2,1)S(1)} %collective-permute-done.3.refs_3_, ...), custom_call_target="tpu_custom_call" | custom-call | flops 35999997952 | bytes 60000000 | tf_op jit(solution)/shard_map/attend/pallas_call | solution.py:47
  96.4 9.7 %attend_back.2 = (bf16[512,768]{1,0:T(8,128)(2,1)S(1)}, f32[1024,512]{1,0:T(8,128)}) custom-call(s32[9]{0:T(128)S(1)} %pad_add_fusion.refs_0_, bf16[512,768]{1,0:T(8,128)(2,1)S(1)} %get-tuple-element.112.refs_1_, bf16[4,128,512]{2,1,0:T(8,128)(2,1)S(1)} %join.4.refs_2_, bf16[4,128,512]{2,1,0:T(8,128)(2,1)S(1)} %collective-permute-done.3.refs_3_, ...), custom_call_target="tpu_custom_call" | custom-call | flops 54000001024 | bytes 90000000 | tf_op jit(solution)/shard_map/attend_back/pallas_call | solution.py:47
  106.1 9.3 %collective-permute-done.5.refs_2_.refs_4_ = bf16[2,384,768]{2,1,0:T(8,128)(2,1)S(1)} collective-permute-done((bf16[2,384,768]{2,1,0:T(8,128)(2,1)S(1)}, bf16[2,384,768]{2,1,0:T(8,128)(2,1)S(1)}, u32[]{:S(2)}, u32[]{:S(2)}) %collective-permute-start.5) | collective-permute-done | bytes 1179680 | tf_op jit(solution)/shard_map/ppermute | solution.py:640
  123.4 10.7 %turn.1 = (bf16[512,768]{1,0:T(8,128)(2,1)}, bf16[2304,768]{1,0:T(8,128)(2,1)}, bf16[512,768]{1,0:T(8,128)(2,1)S(1)}, bf16[512,768]{1,0:T(8,128)(2,1)S(1)}, f32[8,768]{1,0:T(8,128)S(1)}) custom-call(bf16[512,768]{1,0:T(8,128)(2,1)S(1)} %get-tuple-element.107.refs_0_, f32[512,768]{1,0:T(8,128)} %copy-done.33, ...), custom_call_target="tpu_custom_call" | custom-call | flops 35999997952 | bytes 60000000 | tf_op jit(solution)/shard_map/turn/pallas_call | solution.py:47
  138.1 10.8 %mlp_back.2 = (f32[512,768]{1,0:T(8,128)S(1)}, bf16[2,1536,768]{2,1,0:T(8,128)(2,1)}, f32[1,1536]{1,0:T(1,128)S(1)}) custom-call(s32[1]{0:T(128)} %bitcast.11.refs_0_, bf16[512,768]{1,0:T(8,128)(2,1)S(1)} %copy-done.3, bf16[512,768]{1,0:T(8,128)(2,1)S(1)} %copy-done.5, bf16[2,768,3072]{2,1,0:T(8,128)(2,1)} %refs_3_.13, bf16[2,3072,768]{2,1,0:T(8,128)(2,1)} %refs_4_.3, ...), custom_call_target="tpu_custom_call" | custom-call | flops 7200000000 | bytes 12000000 | tf_op jit(solution)/shard_map/mlp_back/pallas_call | solution.py:47
  150.2 14.1 %collective-permute-start.10 = (bf16[2,96,768]{2,1,0:T(8,128)(2,1)}, bf16[2,96,768]{2,1,0:T(8,128)(2,1)S(1)}, u32[]{:S(2)}, u32[]{:S(2)}) collective-permute-start(bf16[2,96,768]{2,1,0:T(8,128)(2,1)} %get-tuple-element.136), channel_id=1, source_target_pairs={{0,4},{2,6},{4,0},{6,2},{1,5},{3,7},{5,1},{7,3},{8,12},{10,14},{12... | collective-permute-start | bytes 884744 | tf_op jit(solution)/shard_map/ppermute | solution.py:661
  164.3 12.1 %collective-permute-start.11 = (bf16[2,96,768]{2,1,0:T(8,128)(2,1)}, bf16[2,96,768]{2,1,0:T(8,128)(2,1)S(1)}, u32[]{:S(2)}, u32[]{:S(2)}) collective-permute-start(bf16[2,96,768]{2,1,0:T(8,128)(2,1)} %get-tuple-element.137), channel_id=1, source_target_pairs={{0,6},{2,0},{4,2},{6,4},{1,7},{3,1},{5,3},{7,5},{8,14},{10,8},{12,... | collective-permute-start | bytes 884744 | tf_op jit(solution)/shard_map/ppermute | solution.py:661
  176.9 11.7 %mlp_back.3 = (f32[512,768]{1,0:T(8,128)S(1)}, bf16[2,1536,768]{2,1,0:T(8,128)(2,1)}, f32[1,1536]{1,0:T(1,128)S(1)}) custom-call(s32[1]{0:T(128)} %bitcast.11.refs_0_, bf16[512,768]{1,0:T(8,128)(2,1)S(1)} %copy-done.3, bf16[512,768]{1,0:T(8,128)(2,1)S(1)} %copy-done.5, bf16[2,768,3072]{2,1,0:T(8,128)(2,1)} %refs_3_.13, bf16[2,3072,768]{2,1,0:T(8,128)(2,1)} %refs_4_.3, ...), custom_call_target="tpu_custom_call" | custom-call | flops 7200000000 | bytes 12000000 | tf_op jit(solution)/shard_map/mlp_back/pallas_call | solution.py:47
  189.8 6.4 %sum_cores.4 = (bf16[2,384,768]{2,1,0:T(8,128)(2,1)}, bf16[2,384,768]{2,1,0:T(8,128)(2,1)S(1)}, bf16[2,384,768]{2,1,0:T(8,128)(2,1)}, bf16[2,384,768]{2,1,0:T(8,128)(2,1)}) custom-call(s32[4]{0:T(128)S(1)} %pad_add_fusion.1.refs_0_, bf16[2,2,2,384,768]{4,3,2,1,0:T(8,128)(2,1)} %bitcast.160, ...), custom_call_target="tpu_custom_call" | custom-call | flops 1200000000 | bytes 2000000 | tf_op jit(solution)/shard_map/sum_cores/pallas_call | solution.py:47
  204.1 10.1 %attend_back.3 = (bf16[512,768]{1,0:T(8,128)(2,1)S(1)}, f32[1024,512]{1,0:T(8,128)}) custom-call(s32[9]{0:T(128)S(1)} %pad_add_fusion.refs_0_, bf16[512,768]{1,0:T(8,128)(2,1)S(1)} %copy-done.32, bf16[4,128,512]{2,1,0:T(8,128)(2,1)S(1)} %join.4.refs_2_, bf16[4,128,512]{2,1,0:T(8,128)(2,1)S(1)} %copy-done.22, bf16[512,768]{1,0:T(8,128)(2,1)S(1)} %copy-done.26, ...), custom_call_target="tpu_custom_call" | custom-call | flops 54000001024 | bytes 90000000 | tf_op jit(solution)/shard_map/attend_back/pallas_call | solution.py:47
  218.4 8.1 %collective-permute-done.14.refs_2_.refs_4_ = bf16[2,384,768]{2,1,0:T(8,128)(2,1)} collective-permute-done((bf16[2,384,768]{2,1,0:T(8,128)(2,1)}, bf16[2,384,768]{2,1,0:T(8,128)(2,1)}, u32[]{:S(2)}, u32[]{:S(2)}) %collective-permute-start.14) | collective-permute-done | bytes 1179680 | tf_op jit(solution)/shard_map/ppermute | solution.py:640
  233.4 7.6 %collective-permute-start.17 = (bf16[1,128,512]{2,1,0:T(8,128)(2,1)S(1)}, bf16[1,128,512]{2,1,0:T(8,128)(2,1)}, u32[]{:S(2)}, u32[]{:S(2)}) collective-permute-start(bf16[1,128,512]{2,1,0:T(8,128)(2,1)S(1)} %get-tuple-element.153), channel_id=1, source_target_pairs={{0,4},{2,6},{4,0},{6,2},{1,5},{3,7},{5,1},{7,3},{8,12},{10,14},{12... | collective-permute-start | bytes 393224 | tf_op jit(solution)/shard_map/ppermute | solution.py:661
  247.4 7.4 %collective-permute-done.17.refs_3_ = bf16[1,128,512]{2,1,0:T(8,128)(2,1)} collective-permute-done((bf16[1,128,512]{2,1,0:T(8,128)(2,1)S(1)}, bf16[1,128,512]{2,1,0:T(8,128)(2,1)}, u32[]{:S(2)}, u32[]{:S(2)}) %collective-permute-start.17) | collective-permute-done | bytes 131104 | tf_op jit(solution)/shard_map/ppermute | solution.py:661
  256.5 5.8 %last.1 = (f32[512,768]{1,0:T(8,128)}, bf16[896,768]{1,0:T(8,128)(2,1)}, f32[8,768]{1,0:T(8,128)S(1)}) custom-call(bf16[512,768]{1,0:T(8,128)(2,1)S(1)} %bitcast.111, bf16[512,768]{1,0:T(8,128)(2,1)S(1)} %copy-done.5, bf16[512,768]{1,0:T(8,128)(2,1)S(1)} %copy-done.29, bf16[512,768]{1,0:T(8,128)(2,1)S(1)} %get-tuple-element.145.refs_9_.refs_3_, ...), custom_call_target="tpu_custom_call" | custom-call | flops 6000000000 | bytes 10000000 | tf_op jit(solution)/shard_map/last/pallas_call | solution.py:47
  270.2 4.6 %dynamic-slice_bitcast_fusion = (bf16[1792,768]{1,0:T(8,128)(2,1)S(1)}, bf16[1,1792,768]{2,1,0:T(8,128)(2,1)}) fusion(bf16[2,1792,768]{2,1,0:T(8,128)(2,1)} %bitcast.172, s32[]{:T(128)S(6)} %select_n.33, s32[]{:T(128)S(6)} %select_n.37), kind=kLoop, calls=%fused_computation | loop fusion | bytes 11010056 | tf_op jit(solution)/shard_map/jit(dynamic_index_in_dim)/squeeze | solution.py:651
  293.5 6.0 %collective-permute-done.24.refs_2_ = bf16[2,96,768]{2,1,0:T(8,128)(2,1)S(1)} collective-permute-done((bf16[2,96,768]{2,1,0:T(8,128)(2,1)S(1)}, bf16[2,96,768]{2,1,0:T(8,128)(2,1)S(1)}, u32[]{:S(2)}, u32[]{:S(2)}) %collective-permute-start.24) | collective-permute-done | bytes 294944 | tf_op jit(solution)/shard_map/ppermute | solution.py:661
  299.5 11.5 %collective-permute-done.25.refs_3_ = bf16[2,96,768]{2,1,0:T(8,128)(2,1)S(1)} collective-permute-done((bf16[2,96,768]{2,1,0:T(8,128)(2,1)S(1)}, bf16[2,96,768]{2,1,0:T(8,128)(2,1)S(1)}, u32[]{:S(2)}, u32[]{:S(2)}) %collective-permute-start.25) | collective-permute-done | bytes 294944 | tf_op jit(solution)/shard_map/ppermute | solution.py:661
  316.7 6.8 %collective-permute-start.32 = (bf16[2,96,768]{2,1,0:T(8,128)(2,1)S(1)}, bf16[2,96,768]{2,1,0:T(8,128)(2,1)S(1)}, u32[]{:S(2)}, u32[]{:S(2)}) collective-permute-start(bf16[2,96,768]{2,1,0:T(8,128)(2,1)S(1)} %sum_third.6.refs_9_.refs_1_.refs_5_), channel_id=1, source_target_pairs={{0,2},{2,4},{4,6},{6,0},{1,3},{3,5},{5,7},{7,1},{8,10},{10,12},{12... | collective-permute-start | bytes 884744 | tf_op jit(solution)/shard_map/ppermute | solution.py:661
  326.8 6.0 %collective-permute-start.29 = (bf16[2,56,768]{2,1,0:T(8,128)(2,1)S(1)}, bf16[2,56,768]{2,1,0:T(8,128)(2,1)S(1)}, u32[]{:S(2)}, u32[]{:S(2)}) collective-permute-start(bf16[2,56,768]{2,1,0:T(8,128)(2,1)S(1)} %get-tuple-element.180), channel_id=1, source_target_pairs={{0,2},{2,4},{4,6},{6,0},{1,3},{3,5},{5,7},{7,1},{8,10},{10,12},{12... | collective-permute-start | bytes 516104 | tf_op jit(solution)/shard_map/ppermute | solution.py:661
  335.3 11.0 %collective-permute-done.33.refs_3_.refs_7_ = bf16[2,96,768]{2,1,0:T(8,128)(2,1)S(1)} collective-permute-done((bf16[2,96,768]{2,1,0:T(8,128)(2,1)S(1)}, bf16[2,96,768]{2,1,0:T(8,128)(2,1)S(1)}, u32[]{:S(2)}, u32[]{:S(2)}) %collective-permute-start.33) | collective-permute-done | bytes 294944 | tf_op jit(solution)/shard_map/ppermute | solution.py:661
  349.9 11.6 %collective-permute-done.30.refs_3_ = bf16[2,56,768]{2,1,0:T(8,128)(2,1)S(1)} collective-permute-done((bf16[2,56,768]{2,1,0:T(8,128)(2,1)S(1)}, bf16[2,56,768]{2,1,0:T(8,128)(2,1)S(1)}, u32[]{:S(2)}, u32[]{:S(2)}) %collective-permute-start.30) | collective-permute-done | bytes 172064 | tf_op jit(solution)/shard_map/ppermute | solution.py:661
  363.6 15.7 %collective-permute-done.39 = bf16[4,96,768]{2,1,0:T(8,128)(2,1)S(1)} collective-permute-done((bf16[4,96,768]{2,1,0:T(8,128)(2,1)S(1)}, bf16[4,96,768]{2,1,0:T(8,128)(2,1)S(1)}, u32[]{:S(2)}, u32[]{:S(2)}) %collective-permute-start.39) | collective-permute-done | bytes 589856 | tf_op jit(solution)/shard_map/ppermute | solution.py:640
  383.3 29.8 %collective-permute-done.40.refs_1_ = bf16[768,768]{1,0:T(8,128)(2,1)S(1)} collective-permute-done((bf16[768,768]{1,0:T(8,128)(2,1)}, bf16[768,768]{1,0:T(8,128)(2,1)S(1)}, u32[]{:S(2)}, u32[]{:S(2)}) %collective-permute-start.40) | collective-permute-done | bytes 1179680 | tf_op jit(solution)/shard_map/ppermute | solution.py:640
  413.5 11.4 %spread.1 = (f32[2,3072,768]{2,1,0:T(8,128)}, f32[2,768,3072]{2,1,0:T(8,128)}) custom-call(bf16[8,4,2,96,768]{4,3,2,1,0:T(8,128)(2,1)} %bitcast.174, bf16[768,768]{1,0:T(8,128)(2,1)} %bitcast.68.refs_1_, bf16[768,768]{1,0:T(8,128)(2,1)S(1)} %bitcast.98), custom_call_target="tpu_custom_call" | custom-call | flops 6000000000 | bytes 10000000 | tf_op jit(solution)/shard_map/spread/pallas_call | solution.py:47
  424.9 5.4 %place.9.refs_2_ = f32[2,3072,768]{2,1,0:T(8,128)} custom-call(s32[5]{0:T(128)S(1)} %stack.136.refs_0_, bf16[768,768]{1,0:T(8,128)(2,1)} %bitcast.68.refs_1_, bf16[768,768]{1,0:T(8,128)(2,1)} %collective-permute-done.42.refs_2_, f32[2,3072,768]{2,1,0:T(8,128)} %get-tuple-element.190.refs_3_), custom_call_target="tpu_custom_call", output_to_operand_aliasing={{}: (3, {})} | custom-call | flops 3600000000 | bytes 6000000 | tf_op jit(solution)/shard_map/place/pallas_call | solution.py:47
  441.8 6.6 %finish.1 = (f32[2,768,768]{2,1,0:T(8,128)}, f32[768,768]{1,0:T(8,128)}, f32[768,896]{1,0:T(8,128)}, f32[384,768]{1,0:T(8,128)S(1)}) custom-call(bf16[32,2,56,768]{3,2,1,0:T(8,128)(2,1)} %bitcast.180), custom_call_target="tpu_custom_call" | custom-call | flops 3600000000 | bytes 6000000 | tf_op jit(solution)/shard_map/finish/pallas_call | solution.py:47
  (251 shorter events, 131.1 us)
Async XLA Ops:
  7.2 354.4 %all-gather.5.cloned.1.call-start = ((), (), s32[]{:S(2)}) async-start(), calls=%async_computation | async-start | bytes 9732096 | tf_op jit(solution)/shard_map/all_gather | solution.py:784
  14.9 20.3 %collective-permute-start = (bf16[128,512]{1,0:T(8,128)(2,1)S(1)}, bf16[128,512]{1,0:T(8,128)(2,1)S(1)}, u32[]{:S(2)}, u32[]{:S(2)}) collective-permute-start(bf16[128,512]{1,0:T(8,128)(2,1)S(1)} %get-tuple-element.103), channel_id=1, source_target_pairs={{0,2},{2,4},{4,6},{6,0},{1,3},{3,5},{5,7},{7,1},{8,10},{10,12},{12... | collective-permute-start | bytes 393224 | tf_op jit(solution)/shard_map/ppermute | solution.py:661
  17.9 17.3 %collective-permute-start.1 = (bf16[128,512]{1,0:T(8,128)(2,1)S(1)}, bf16[128,512]{1,0:T(8,128)(2,1)S(1)}, u32[]{:S(2)}, u32[]{:S(2)}) collective-permute-start(bf16[128,512]{1,0:T(8,128)(2,1)S(1)} %get-tuple-element.103), channel_id=1, source_target_pairs={{0,4},{2,6},{4,0},{6,2},{1,5},{3,7},{5,1},{7,3},{8,12},{10,14},{12... | collective-permute-start | bytes 393224 | tf_op jit(solution)/shard_map/ppermute | solution.py:661
  87.4 28.0 %collective-permute-start.5 = (bf16[2,384,768]{2,1,0:T(8,128)(2,1)S(1)}, bf16[2,384,768]{2,1,0:T(8,128)(2,1)S(1)}, u32[]{:S(2)}, u32[]{:S(2)}) collective-permute-start(bf16[2,384,768]{2,1,0:T(8,128)(2,1)S(1)} %get-tuple-element.121), channel_id=1, source_target_pairs={{0,8},{8,0},{1,9},{9,1},{2,10},{10,2},{3,11},{11,3},{4,12},{12,4},... | collective-permute-start | bytes 3538952 | tf_op jit(solution)/shard_map/ppermute | solution.py:640
  89.0 27.6 %collective-permute-start.6 = (bf16[2,384,768]{2,1,0:T(8,128)(2,1)S(1)}, bf16[2,384,768]{2,1,0:T(8,128)(2,1)S(1)}, u32[]{:S(2)}, u32[]{:S(2)}) collective-permute-start(bf16[2,384,768]{2,1,0:T(8,128)(2,1)S(1)} %get-tuple-element.123), channel_id=1, source_target_pairs={{0,16},{16,0},{1,17},{17,1},{2,18},{18,2},{3,19},{19,3},{4,20},{20... | collective-permute-start | bytes 3538952 | tf_op jit(solution)/shard_map/ppermute | solution.py:640
  150.1 39.7 %collective-permute-start.12 = (bf16[3072,768]{1,0:T(8,128)(2,1)}, bf16[3072,768]{1,0:T(8,128)(2,1)}, u32[]{:S(2)}, u32[]{:S(2)}) collective-permute-start(bf16[3072,768]{1,0:T(8,128)(2,1)} %bitcast.181), channel_id=1, source_target_pairs={{0,1},{1,0},{2,3},{3,2},{4,5},{5,4},{6,7},{7,6},{8,9},{9,8},{10,11... | collective-permute-start | bytes 14155784 | tf_op jit(solution)/shard_map/ppermute | solution.py:640
  150.2 48.2 %collective-permute-start.10 = (bf16[2,96,768]{2,1,0:T(8,128)(2,1)}, bf16[2,96,768]{2,1,0:T(8,128)(2,1)S(1)}, u32[]{:S(2)}, u32[]{:S(2)}) collective-permute-start(bf16[2,96,768]{2,1,0:T(8,128)(2,1)} %get-tuple-element.136), channel_id=1, source_target_pairs={{0,4},{2,6},{4,0},{6,2},{1,5},{3,7},{5,1},{7,3},{8,12},{10,14},{12... | collective-permute-start | bytes 884744 | tf_op jit(solution)/shard_map/ppermute | solution.py:661
  164.3 34.1 %collective-permute-start.11 = (bf16[2,96,768]{2,1,0:T(8,128)(2,1)}, bf16[2,96,768]{2,1,0:T(8,128)(2,1)S(1)}, u32[]{:S(2)}, u32[]{:S(2)}) collective-permute-start(bf16[2,96,768]{2,1,0:T(8,128)(2,1)} %get-tuple-element.137), channel_id=1, source_target_pairs={{0,6},{2,0},{4,2},{6,4},{1,7},{3,1},{5,3},{7,5},{8,14},{10,8},{12,... | collective-permute-start | bytes 884744 | tf_op jit(solution)/shard_map/ppermute | solution.py:661
  176.4 21.9 %collective-permute-start.9 = (bf16[2,96,768]{2,1,0:T(8,128)(2,1)S(1)}, bf16[2,96,768]{2,1,0:T(8,128)(2,1)S(1)}, u32[]{:S(2)}, u32[]{:S(2)}) collective-permute-start(bf16[2,96,768]{2,1,0:T(8,128)(2,1)S(1)} %get-tuple-element.135), channel_id=1, source_target_pairs={{0,2},{2,4},{4,6},{6,0},{1,3},{3,5},{5,7},{7,1},{8,10},{10,12},{12... | collective-permute-start | bytes 884744 | tf_op jit(solution)/shard_map/ppermute | solution.py:661
  196.2 30.3 %collective-permute-start.14 = (bf16[2,384,768]{2,1,0:T(8,128)(2,1)}, bf16[2,384,768]{2,1,0:T(8,128)(2,1)}, u32[]{:S(2)}, u32[]{:S(2)}) collective-permute-start(bf16[2,384,768]{2,1,0:T(8,128)(2,1)} %get-tuple-element.147), channel_id=1, source_target_pairs={{0,8},{8,0},{1,9},{9,1},{2,10},{10,2},{3,11},{11,3},{4,12},{12,4},... | collective-permute-start | bytes 3538952 | tf_op jit(solution)/shard_map/ppermute | solution.py:640
  196.9 30.0 %collective-permute-start.15 = (bf16[2,384,768]{2,1,0:T(8,128)(2,1)}, bf16[2,384,768]{2,1,0:T(8,128)(2,1)}, u32[]{:S(2)}, u32[]{:S(2)}) collective-permute-start(bf16[2,384,768]{2,1,0:T(8,128)(2,1)} %get-tuple-element.149), channel_id=1, source_target_pairs={{0,16},{16,0},{1,17},{17,1},{2,18},{18,2},{3,19},{19,3},{4,20},{20... | collective-permute-start | bytes 3538952 | tf_op jit(solution)/shard_map/ppermute | solution.py:640
  199.8 242.0 %all-gather.7.cloned.1.call-start = ((), (), s32[]{:S(2)}) async-start(), calls=%async_computation.1 | async-start | bytes 5677056 | tf_op jit(solution)/shard_map/all_gather | solution.py:784
  233.4 21.4 %collective-permute-start.17 = (bf16[1,128,512]{2,1,0:T(8,128)(2,1)S(1)}, bf16[1,128,512]{2,1,0:T(8,128)(2,1)}, u32[]{:S(2)}, u32[]{:S(2)}) collective-permute-start(bf16[1,128,512]{2,1,0:T(8,128)(2,1)S(1)} %get-tuple-element.153), channel_id=1, source_target_pairs={{0,4},{2,6},{4,0},{6,2},{1,5},{3,7},{5,1},{7,3},{8,12},{10,14},{12... | collective-permute-start | bytes 393224 | tf_op jit(solution)/shard_map/ppermute | solution.py:661
  241.0 33.9 %collective-permute-start.20 = (bf16[1,384,768]{2,1,0:T(8,128)(2,1)}, bf16[1,384,768]{2,1,0:T(8,128)(2,1)}, u32[]{:S(2)}, u32[]{:S(2)}) collective-permute-start(bf16[1,384,768]{2,1,0:T(8,128)(2,1)} %copy-done.20), channel_id=1, source_target_pairs={{0,16},{16,0},{1,17},{17,1},{2,18},{18,2},{3,19},{19,3},{4,20},{20... | collective-permute-start | bytes 1769480 | tf_op jit(solution)/shard_map/ppermute | solution.py:640
  241.6 33.3 %collective-permute-start.21 = (bf16[1,384,768]{2,1,0:T(8,128)(2,1)}, bf16[1,384,768]{2,1,0:T(8,128)(2,1)}, u32[]{:S(2)}, u32[]{:S(2)}) collective-permute-start(bf16[1,384,768]{2,1,0:T(8,128)(2,1)} %copy-done.19), channel_id=1, source_target_pairs={{0,8},{8,0},{1,9},{9,1},{2,10},{10,2},{3,11},{11,3},{4,12},{12,4},... | collective-permute-start | bytes 1769480 | tf_op jit(solution)/shard_map/ppermute | solution.py:640
  285.8 25.9 %collective-permute-start.22 = (bf16[2,224,768]{2,1,0:T(8,128)(2,1)S(1)}, bf16[2,224,768]{2,1,0:T(8,128)(2,1)S(1)}, u32[]{:S(2)}, u32[]{:S(2)}) collective-permute-start(bf16[2,224,768]{2,1,0:T(8,128)(2,1)S(1)} %get-tuple-element.169), channel_id=1, source_target_pairs={{0,8},{8,0},{1,9},{9,1},{2,10},{10,2},{3,11},{11,3},{4,12},{12,4},... | collective-permute-start | bytes 2064392 | tf_op jit(solution)/shard_map/ppermute | solution.py:640
  286.8 24.9 %collective-permute-start.23 = (bf16[2,224,768]{2,1,0:T(8,128)(2,1)S(1)}, bf16[2,224,768]{2,1,0:T(8,128)(2,1)S(1)}, u32[]{:S(2)}, u32[]{:S(2)}) collective-permute-start(bf16[2,224,768]{2,1,0:T(8,128)(2,1)S(1)} %get-tuple-element.171), channel_id=1, source_target_pairs={{0,16},{16,0},{1,17},{17,1},{2,18},{18,2},{3,19},{19,3},{4,20},{20... | collective-permute-start | bytes 2064392 | tf_op jit(solution)/shard_map/ppermute | solution.py:640
  291.1 19.9 %collective-permute-start.25 = (bf16[2,96,768]{2,1,0:T(8,128)(2,1)S(1)}, bf16[2,96,768]{2,1,0:T(8,128)(2,1)S(1)}, u32[]{:S(2)}, u32[]{:S(2)}) collective-permute-start(bf16[2,96,768]{2,1,0:T(8,128)(2,1)S(1)} %get-tuple-element.173), channel_id=1, source_target_pairs={{0,4},{2,6},{4,0},{6,2},{1,5},{3,7},{5,1},{7,3},{8,12},{10,14},{12... | collective-permute-start | bytes 884744 | tf_op jit(solution)/shard_map/ppermute | solution.py:661
  291.5 19.5 %collective-permute-start.26 = (bf16[2,96,768]{2,1,0:T(8,128)(2,1)S(1)}, bf16[2,96,768]{2,1,0:T(8,128)(2,1)S(1)}, u32[]{:S(2)}, u32[]{:S(2)}) collective-permute-start(bf16[2,96,768]{2,1,0:T(8,128)(2,1)S(1)} %get-tuple-element.174), channel_id=1, source_target_pairs={{0,6},{2,0},{4,2},{6,4},{1,7},{3,1},{5,3},{7,5},{8,14},{10,8},{12,... | collective-permute-start | bytes 884744 | tf_op jit(solution)/shard_map/ppermute | solution.py:661
  316.7 17.3 %collective-permute-start.32 = (bf16[2,96,768]{2,1,0:T(8,128)(2,1)S(1)}, bf16[2,96,768]{2,1,0:T(8,128)(2,1)S(1)}, u32[]{:S(2)}, u32[]{:S(2)}) collective-permute-start(bf16[2,96,768]{2,1,0:T(8,128)(2,1)S(1)} %sum_third.6.refs_9_.refs_1_.refs_5_), channel_id=1, source_target_pairs={{0,2},{2,4},{4,6},{6,0},{1,3},{3,5},{5,7},{7,1},{8,10},{10,12},{12... | collective-permute-start | bytes 884744 | tf_op jit(solution)/shard_map/ppermute | solution.py:661
  323.5 22.8 %collective-permute-start.33 = (bf16[2,96,768]{2,1,0:T(8,128)(2,1)S(1)}, bf16[2,96,768]{2,1,0:T(8,128)(2,1)S(1)}, u32[]{:S(2)}, u32[]{:S(2)}) collective-permute-start(bf16[2,96,768]{2,1,0:T(8,128)(2,1)S(1)} %sum_third.6.refs_9_.refs_1_.refs_5_), channel_id=1, source_target_pairs={{0,4},{2,6},{4,0},{6,2},{1,5},{3,7},{5,1},{7,3},{8,12},{10,14},{12... | collective-permute-start | bytes 884744 | tf_op jit(solution)/shard_map/ppermute | solution.py:661
  326.1 20.2 %collective-permute-start.34 = (bf16[2,96,768]{2,1,0:T(8,128)(2,1)S(1)}, bf16[2,96,768]{2,1,0:T(8,128)(2,1)S(1)}, u32[]{:S(2)}, u32[]{:S(2)}) collective-permute-start(bf16[2,96,768]{2,1,0:T(8,128)(2,1)S(1)} %sum_third.6.refs_9_.refs_1_.refs_5_), channel_id=1, source_target_pairs={{0,6},{2,0},{4,2},{6,4},{1,7},{3,1},{5,3},{7,5},{8,14},{10,8},{12,... | collective-permute-start | bytes 884744 | tf_op jit(solution)/shard_map/ppermute | solution.py:661
  326.8 23.1 %collective-permute-start.29 = (bf16[2,56,768]{2,1,0:T(8,128)(2,1)S(1)}, bf16[2,56,768]{2,1,0:T(8,128)(2,1)S(1)}, u32[]{:S(2)}, u32[]{:S(2)}) collective-permute-start(bf16[2,56,768]{2,1,0:T(8,128)(2,1)S(1)} %get-tuple-element.180), channel_id=1, source_target_pairs={{0,2},{2,4},{4,6},{6,0},{1,3},{3,5},{5,7},{7,1},{8,10},{10,12},{12... | collective-permute-start | bytes 516104 | tf_op jit(solution)/shard_map/ppermute | solution.py:661
  332.8 28.7 %collective-permute-start.30 = (bf16[2,56,768]{2,1,0:T(8,128)(2,1)S(1)}, bf16[2,56,768]{2,1,0:T(8,128)(2,1)S(1)}, u32[]{:S(2)}, u32[]{:S(2)}) collective-permute-start(bf16[2,56,768]{2,1,0:T(8,128)(2,1)S(1)} %get-tuple-element.181), channel_id=1, source_target_pairs={{0,4},{2,6},{4,0},{6,2},{1,5},{3,7},{5,1},{7,3},{8,12},{10,14},{12... | collective-permute-start | bytes 516104 | tf_op jit(solution)/shard_map/ppermute | solution.py:661
  334.0 27.5 %collective-permute-start.31 = (bf16[2,56,768]{2,1,0:T(8,128)(2,1)S(1)}, bf16[2,56,768]{2,1,0:T(8,128)(2,1)S(1)}, u32[]{:S(2)}, u32[]{:S(2)}) collective-permute-start(bf16[2,56,768]{2,1,0:T(8,128)(2,1)S(1)} %get-tuple-element.182), channel_id=1, source_target_pairs={{0,6},{2,0},{4,2},{6,4},{1,7},{3,1},{5,3},{7,5},{8,14},{10,8},{12,... | collective-permute-start | bytes 516104 | tf_op jit(solution)/shard_map/ppermute | solution.py:661
  363.3 17.9 %collective-permute-start.35 = (bf16[4,96,768]{2,1,0:T(8,128)(2,1)S(1)}, bf16[4,96,768]{2,1,0:T(8,128)(2,1)S(1)}, u32[]{:S(2)}, u32[]{:S(2)}) collective-permute-start(bf16[4,96,768]{2,1,0:T(8,128)(2,1)S(1)} %get-tuple-element.188), channel_id=1, source_target_pairs={{0,8},{8,0},{1,9},{9,1},{2,10},{10,2},{3,11},{11,3},{4,12},{12,4},... | collective-permute-start | bytes 1769480 | tf_op jit(solution)/shard_map/ppermute | solution.py:640
  380.9 32.1 %collective-permute-start.40 = (bf16[768,768]{1,0:T(8,128)(2,1)}, bf16[768,768]{1,0:T(8,128)(2,1)S(1)}, u32[]{:S(2)}, u32[]{:S(2)}) collective-permute-start(bf16[768,768]{1,0:T(8,128)(2,1)} %bitcast.68.refs_1_), channel_id=1, source_target_pairs={{0,8},{8,0},{1,9},{9,1},{2,10},{10,2},{3,11},{11,3},{4,12},{12,4},... | collective-permute-start | bytes 3538952 | tf_op jit(solution)/shard_map/ppermute | solution.py:640
  381.9 31.2 %collective-permute-start.36 = (bf16[768,768]{1,0:T(8,128)(2,1)S(1)}, bf16[768,768]{1,0:T(8,128)(2,1)S(1)}, u32[]{:S(2)}, u32[]{:S(2)}) collective-permute-start(bf16[768,768]{1,0:T(8,128)(2,1)S(1)} %bitcast.96), channel_id=1, source_target_pairs={{0,16},{16,0},{1,17},{17,1},{2,18},{18,2},{3,19},{19,3},{4,20},{20... | collective-permute-start | bytes 3538952 | tf_op jit(solution)/shard_map/ppermute | solution.py:640
  382.3 42.6 %collective-permute-start.42 = (bf16[768,768]{1,0:T(8,128)(2,1)}, bf16[768,768]{1,0:T(8,128)(2,1)}, u32[]{:S(2)}, u32[]{:S(2)}) collective-permute-start(bf16[768,768]{1,0:T(8,128)(2,1)} %bitcast.68.refs_1_), channel_id=1, source_target_pairs={{0,1},{1,0},{2,3},{3,2},{4,5},{5,4},{6,7},{7,6},{8,9},{9,8},{10,11... | collective-permute-start | bytes 3538952 | tf_op jit(solution)/shard_map/ppermute | solution.py:640
  382.7 49.6 %collective-permute-start.38 = (bf16[768,768]{1,0:T(8,128)(2,1)S(1)}, bf16[768,768]{1,0:T(8,128)(2,1)S(1)}, u32[]{:S(2)}, u32[]{:S(2)}) collective-permute-start(bf16[768,768]{1,0:T(8,128)(2,1)S(1)} %bitcast.97), channel_id=1, source_target_pairs={{0,1},{1,0},{2,3},{3,2},{4,5},{5,4},{6,7},{7,6},{8,9},{9,8},{10,11... | collective-permute-start | bytes 3538952 | tf_op jit(solution)/shard_map/ppermute | solution.py:640
  413.0 24.6 %collective-permute-start.41 = (bf16[768,768]{1,0:T(8,128)(2,1)S(1)}, bf16[768,768]{1,0:T(8,128)(2,1)S(1)}, u32[]{:S(2)}, u32[]{:S(2)}) collective-permute-start(bf16[768,768]{1,0:T(8,128)(2,1)S(1)} %collective-permute-done.40.refs_1_), channel_id=1, source_target_pairs={{0,1},{1,0},{2,3},{3,2},{4,5},{5,4},{6,7},{7,6},{8,9},{9,8},{10,11... | collective-permute-start | bytes 3538952 | tf_op jit(solution)/shard_map/ppermute | solution.py:640
  413.0 26.7 %collective-permute-start.37 = (bf16[768,768]{1,0:T(8,128)(2,1)S(1)}, bf16[768,768]{1,0:T(8,128)(2,1)S(1)}, u32[]{:S(2)}, u32[]{:S(2)}) collective-permute-start(bf16[768,768]{1,0:T(8,128)(2,1)S(1)} %collective-permute-done.36.refs_1_), channel_id=1, source_target_pairs={{0,1},{1,0},{2,3},{3,2},{4,5},{5,4},{6,7},{7,6},{8,9},{9,8},{10,11... | collective-permute-start | bytes 3538952 | tf_op jit(solution)/shard_map/ppermute | solution.py:640
  (63 other events, 497.4 us)
Sparse Core Ops, SparseCore 0:
  199.9 92.0 all-gather.4
  363.0 72.3 all-gather.6

commit v3 on v2

--- a/solution.py
+++ b/solution.py
@@ -18,6 +18,7 @@
 C = "c"
 TILE = 768
 QUARTER = TILE // 2
+EXTRA = 256
 KB = 256
 
 f32 = jnp.float32
@@ -37,7 +38,7 @@
 
 
 def invoke(
-    kernel, operands, deps, *, grid, in_specs, out_specs, out_shape, name, scalars=(), scratch=(), aliases={}, us=2
+    kernel, operands, deps, *, grid, in_specs, out_specs, out_shape, name, scalars=(), scratch=(), aliases={}, us=2, vmem=50
 ):
     ahead = len(scalars) + len(operands)
 
@@ -55,7 +56,7 @@
         ),
         out_shape=out_shape,
         input_output_aliases=aliases,
-        compiler_params=pltpu.CompilerParams(vmem_limit_bytes=50 << 20),
+        compiler_params=pltpu.CompilerParams(vmem_limit_bytes=vmem << 20),
         cost_estimate=pl.CostEstimate(
             flops=us * 600_000_000, bytes_accessed=us * 1_000_000, transcendentals=0
         ),
@@ -264,7 +265,7 @@
         ],
         scratch=[pltpu.VMEM((width, tokens), bf16)],
         name="mlp_both" if both else "mlp_back",
-        us=40 if both else 12,
+        us=40 if both else (12 if other else 150),
     )
 
 
@@ -378,8 +379,10 @@
     )
 
 
-def attend_back_kernel(count, has_start, first_ref, q_ref, *refs):
+def attend_back_kernel(count, has_start, unread, first_ref, q_ref, *refs):
     pieces, refs = refs[:count], refs[count:]
+    ins = 5 if has_start else 4
+    refs = refs[:ins] + refs[ins + unread :]
     if has_start:
         o_ref, do_ref, lse_ref, tab_ref, start_ref, dq_out, dkv_ref, k0, k1, v0, v1, t0, t1, dq_ref = refs
         dkv_ref[...] = start_ref[...]
@@ -432,33 +435,35 @@
         dq_out[:, p * 128 : (p + 1) * 128] = turn(part, cos_tab, sin_low, sin_high).astype(bf16)
 
 
-def attend_back_call(first, q, kv, attended, grad, lse, tab, start=None, deps=()):
+def attend_back_call(first, q, kv, attended, grad, lse, tab, part, start=None, before=(), deps=()):
     tokens, width = q.shape
     length = sum(v.shape[0] for v in kv) * kv[0].shape[1]
     seqs = kv[0].shape[2] // 128
     group = tokens // seqs
     rows = group * width // 128
-    tok_spec = pl.BlockSpec((group, width), lambda s, f: (s, 0))
-    len_spec = pl.BlockSpec((length, 128), lambda s, f: (0, s))
+    count = seqs if part is None else seqs // 2
+    at = (part or 0) * count
+    tok_spec = pl.BlockSpec((group, width), lambda s, f: (at + s, 0))
+    len_spec = pl.BlockSpec((length, 128), lambda s, f: (0, at + s))
     in_specs = [
         tok_spec,
-        *piece_specs(kv),
+        *[pl.BlockSpec(v.shape[:2] + (128,), lambda s, f: (0, 0, at + s)) for v in kv],
         tok_spec,
         tok_spec,
-        pl.BlockSpec((1, 2, 8, rows), lambda s, f: (s, 0, 0, 0)),
-        pl.BlockSpec((3, group, 128), lambda s, f: (0, s, 0)),
+        pl.BlockSpec((1, 2, 8, rows), lambda s, f: (at + s, 0, 0, 0)),
+        pl.BlockSpec((3, group, 128), lambda s, f: (0, at + s, 0)),
     ]
     operands = [q, *kv, attended, grad, lse, tab]
     if start is not None:
         in_specs.append(len_spec)
         operands.append(start)
     return invoke(
-        partial(attend_back_kernel, len(kv), start is not None),
-        operands,
+        partial(attend_back_kernel, len(kv), start is not None, len(before)),
+        operands + list(before),
         deps,
         scalars=(first,),
-        grid=(seqs,),
-        in_specs=in_specs,
+        grid=(count,),
+        in_specs=in_specs + [pl.BlockSpec(memory_space=pl.ANY)] * len(before),
         out_specs=[tok_spec, len_spec],
         scratch=[pltpu.VMEM((length, 128), bf16)] * 4
         + [pltpu.VMEM((length // 128, 128, 128), bf16)] * 2
@@ -467,8 +472,9 @@
             jax.ShapeDtypeStruct((tokens, width), bf16),
             jax.ShapeDtypeStruct((length, seqs * 128), f32),
         ],
+        aliases={1 + len(operands) + i: i for i in range(len(before))},
         name="attend_back",
-        us=90,
+        us=45,
     )
 
 
@@ -539,6 +545,16 @@
         - jnp.mean(grad_unit, axis=-1, keepdims=True)
         - unit * jnp.mean(grad_unit * unit, axis=-1, keepdims=True)
     )
+
+
+def by_core(core, send_ref, keep_ref, put):
+    @pl.when(core == 0)
+    def _():
+        put(keep_ref, send_ref)
+
+    @pl.when(core != 0)
+    def _():
+        put(send_ref, keep_ref)
 
 
 def turn_kernel(
@@ -591,7 +607,8 @@
 
 
 def last_kernel(
-    x_ref, g1_ref, na_ref, dq_ref, dkv_ref, dnm_ref, w_ref, gain_ref, tab_ref, grad_ref, grads_ref, small_ref
+    core_ref, x_ref, g1_ref, na_ref, dq_ref, dkv_ref, dnm_ref, w_ref, gain_ref, tab_ref, small2_ref, bup1_ref, bup2_ref,
+    early_ref, grad_ref, send_ref, keep_ref, small_ref,
 ):
     tokens, width = x_ref.shape
     group = dkv_ref.shape[0]
@@ -604,30 +621,45 @@
     small_ref[...] = jnp.zeros_like(small_ref)
     small_ref[4:5] = jnp.sum(dq.astype(f32), axis=0, keepdims=True)
     small_ref[5:6, 0:128] = jnp.sum(dkv.astype(f32), axis=0, keepdims=True)
-    grads_ref[0:width] = dot_tn(norm_a, dq).astype(bf16)
-    grads_ref[width : width + 128] = dot_tn(dkv, norm_a).astype(bf16)
     grad_a = dot_nt(dq, w_ref[:, :width]) + dot_nt(dkv, w_ref[:, width:])
     grad_ref[...] = g1_ref[...].astype(f32) + norm_back(
         x_ref[...].astype(f32), grad_a, dnm_ref[...], gain_ref, small_ref, 0
     )
-
-
-def last_call(x, g1, na1, dq1, dkv, dnm1, w_qkv, gains, tab, deps=()):
+    q1 = dot_tn(norm_a, dq).astype(bf16)
+    kv = dot_tn(dkv, norm_a).astype(bf16)
+    smalls = [small_ref[...], small2_ref[...], bup1_ref[...], bup2_ref[...]]
+    smalls.append(jnp.zeros((EXTRA - 128 - sum(v.shape[0] for v in smalls), width), f32))
+    smalls = jnp.concatenate(smalls, axis=0).astype(bf16)
+
+    def put(one, two):
+        one[: 2 * width] = early_ref[: 2 * width]
+        one[2 * width : 2 * width + 128] = kv
+        one[2 * width + 128 :] = smalls
+        two[:width] = early_ref[2 * width :]
+        two[width : 2 * width] = q1
+        two[2 * width :] = jnp.zeros((EXTRA, width), bf16)
+
+    by_core(core_ref[0], send_ref, keep_ref, put)
+
+
+def last_call(core, x, g1, na1, dq1, dkv, dnm1, w_qkv, gains, tab, small2, bup1, bup2, early, deps=()):
     tokens, width = x.shape
-    operands = (x, g1, na1, dq1, dkv, dnm1, w_qkv, gains, tab)
+    operands = (x, g1, na1, dq1, dkv, dnm1, w_qkv, gains, tab, small2, bup1, bup2, early)
     out_shape = [
         jax.ShapeDtypeStruct((tokens, width), f32),
-        jax.ShapeDtypeStruct((width + 128, width), bf16),
-        jax.ShapeDtypeStruct((8, width), f32),
+        jax.ShapeDtypeStruct((2 * width + EXTRA, width), bf16),
+        jax.ShapeDtypeStruct((2 * width + EXTRA, width), bf16),
     ]
     return invoke(
         last_kernel,
         operands,
         deps,
+        scalars=(core,),
         grid=(1,),
         in_specs=[full_spec(v.shape) for v in operands],
         out_specs=[full_spec(v.shape) for v in out_shape],
         out_shape=out_shape,
+        scratch=[pltpu.VMEM((8, width), f32)],
         name="last",
         us=10,
     )
@@ -672,7 +704,7 @@
     return lax.all_gather(part, (C,) + B + (Z,), axis=0, tiled=True)
 
 
-def combine(groups, where, deps, grid=(1,), name="combine", us=2):
+def combine(groups, where, deps, grid=(1,), name="combine", us=2, vmem=50):
     terms = [t for sums, *_ in groups for parts in sums for t in parts]
 
     def kernel(where_ref, *refs):
@@ -698,10 +730,11 @@
         out_shape=[jax.ShapeDtypeStruct(g[3], bf16) for g in groups],
         name=name,
         us=us,
-    )
-
-
-def sum_cores(keep, got, where, deps=()):
+        vmem=vmem,
+    )
+
+
+def sum_cores(keep, got, where, deps=(), us=20):
     width = keep.shape[-1]
     keep, got = (v.reshape(2, 2, 2, -1, width) for v in (keep, got))
     quarter = keep.shape[3]
@@ -722,10 +755,10 @@
         )
         for m in maps
     ]
-    return combine(groups, where, deps, grid=(2, 2), name="sum_cores")
-
-
-def sum_first(one, one_got, two, two_got, where, deps=()):
+    return combine(groups, where, deps, grid=(2, 2), name="sum_cores", us=us)
+
+
+def sum_first(one, one_got, two, two_got, where, deps=(), us=30):
     _, quarter, width = one.shape
     half = quarter // 2
     groups = []
@@ -739,10 +772,10 @@
         groups.append(
             ([[(values, block, m), (got, block, m)]], block, lambda j, w: (0, j, 0), (1, quarter, width))
         )
-    return combine(groups, where, deps, grid=(2,), name="sum_first")
-
-
-def sum_second(one, one_got, two, two_got, where, deps=()):
+    return combine(groups, where, deps, grid=(2,), name="sum_first", us=us)
+
+
+def sum_second(one, one_got, two, two_got, where, deps=(), us=100):
     width = one.shape[-1]
     one, one_got, two, two_got = (v.reshape(4, -1, width) for v in (one, one_got, two, two_got))
     block = (1,) + one.shape[1:]
@@ -757,13 +790,13 @@
                 (2,) + one.shape[1:],
             )
         )
-    return combine(groups, where, deps, name="sum_second", us=100)
-
-
-def sum_third(parts, where, deps=()):
+    return combine(groups, where, deps, name="sum_second", us=us)
+
+
+def sum_third(parts, where, deps=(), us=10):
     shape = parts[0].shape
     m = lambda i, w: (0, 0, 0)
-    return combine([([[(p, shape, m) for p in parts]], shape, m, shape)], where, deps, name="sum_third")[0]
+    return combine([([[(p, shape, m) for p in parts]], shape, m, shape)], where, deps, name="sum_third", us=us)[0]
 
 
 def join(parts, leads, where, deps=()):
@@ -782,6 +815,13 @@
 
 def gather_blocks(both):
     return lax.all_gather(both, (C,) + B + (Z,), axis=0, tiled=False)
+
+
+def relay(values, where, deps):
+    block = (values[0].shape[0] // 2, values[0].shape[1])
+    m = lambda i, w: (i, 0)
+    groups = [([[(v, block, m)]], block, m, v.shape) for v in values]
+    return combine(groups, where, deps, grid=(2,), name="relay")
 
 
 def place_kernel(count, quarter, where_ref, *refs):
@@ -818,7 +858,7 @@
         out_shape=jax.ShapeDtypeStruct(out_shape, f32),
         aliases={1 + count: 0},
         name="place",
-        us=6,
+        us=2,
     )
 
 
@@ -853,7 +893,7 @@
         ],
         aliases={1: 0, 2: 1} if before else {},
         name="spread",
-        us=10,
+        us=2,
     )
 
 
@@ -866,24 +906,22 @@
                 at = ((w * 2 + two) * 4 + z) * size
                 flat[at : at + size] = in_ref[w * 4 + z, two].astype(f32)
     half = flat.shape[0] // 2
-    rest = half - 2 * width
     out_ref[1] = flat[:width]
     q2_ref[...] = flat[width : 2 * width]
     out_ref[0] = flat[half : half + width]
     qkv_ref[:, :width] = flat[half + width : half + 2 * width]
     qkv_ref[:, width:] = flat[2 * width : 2 * width + 128].T
-    small_ref[: rest - 128] = flat[2 * width + 128 : half]
-    small_ref[rest - 128 :] = flat[half + 2 * width :]
-
-
-def finish_call(blocks, deps=()):
+    small_ref[...] = flat[2 * width + 128 : half]
+
+
+def finish_call(blocks):
     width = blocks.shape[-1]
     rows = blocks.size // width
-    shapes = [(2, width, width), (width, width), (width, width + 128), (rows - 4 * width - 128, width)]
+    shapes = [(2, width, width), (width, width), (width, width + 128), (EXTRA - 128, width)]
     return invoke(
         finish_kernel,
         (blocks,),
-        deps,
+        (),
         grid=(1,),
         in_specs=[full_spec(blocks.shape)],
         out_specs=[full_spec(v) for v in shapes],
@@ -980,43 +1018,48 @@
     else:
         mlp2 = add_low(keep, got)
     att2, lse2 = attend_call(first, q2, kv, wait)
-    dq2, dkv2 = attend_back_call(first, q2, kv, att2, do2, lse2, tab)
+    back2 = attend_back_call(first, q2, kv, att2, do2, lse2, tab, 0)
     if direct:
-        one_send, one, two_send, two = sum_first(one, one_got, two, two_got, where, (dq2,))
+        one_send, one, two_send, two = sum_first(one, one_got, two, two_got, where, (back2[0],))
         one_got, two_got = swaps(one_send, two_send, ("b0", "b1"))
         wait = (one,)
-    hidden_out, grads2, g1, do1, small2 = turn_call(
-        x2, y2, att2, att1, g2, na2, dq2, dnm2, w_out, w_q2, out_bias[1:2], norm_gains[1], deps=wait
-    )
+    dq2, dkv2 = attend_back_call(first, q2, kv, att2, do2, lse2, tab, 1, before=back2, deps=wait)
     if direct:
-        parts = sum_second(one, one_got, two, two_got, where, (g1,))
+        parts = sum_second(one, one_got, two, two_got, where, (dq2,))
         ahead = turns(lambda k: parts[k])
         wait = (parts[0],)
+    hidden_out, early, g1, do1, small2 = turn_call(
+        x2, y2, att2, att1, g2, na2, dq2, dnm2, w_out, w_q2, out_bias[1:2], norm_gains[1], deps=wait
+    )
     dnm1, send, bup_send = mlp_back_call(
-        core_row, nm1, g1, w_up, w_down, 0, kept=(act1, slope1), deps=wait
+        core_row, nm1, g1, w_up, w_down, 0, kept=(act1, slope1)
     )
     got = swap(send.reshape(hidden, width), C)
+    wait = ()
+    if direct:
+        mlp2 = sum_third([parts[0]] + ahead, where, (dnm1,))
+        wait = (mlp2,)
+        mlp2 = gather_blocks(mlp2)
     dnm1, keep, bup_keep = mlp_back_call(
-        core_row, nm1, g1, w_up, w_down, 0, kept=(act1, slope1), before=(dnm1,)
+        core_row, nm1, g1, w_up, w_down, 0, kept=(act1, slope1), before=(dnm1,), deps=wait
     )
     keep = keep.reshape(hidden, width)
     bup1 = in_order(bup_keep, bup_send)
     if direct:
         one_send, one, two_send, two = sum_cores(keep, got, where)
         one_got, two_got = swaps(one_send, two_send, ("b1", "b0"))
-        mlp2 = sum_third([parts[0]] + ahead, where, (one,))
-        wait = (mlp2,)
-        mlp2 = gather_blocks(mlp2)
+        wait = (one,)
     dq1, dkv1 = attend_back_call(
-        first, q1, kv, att1, do1, lse1, tab, dkv2, deps=wait + (dnm1,)
-    )
+        first, q1, kv, att1, do1, lse1, tab, None, dkv2, deps=wait + (dnm1,)
+    )
+    if direct:
+        one_send, one, two_send, two = sum_first(one, one_got, two, two_got, where, (dq1,))
+        one_got, two_got = swaps(one_send, two_send, ("b0", "b1"))
     low = dkv1.astype(bf16)
     if direct:
         low = low.reshape(4, 2, group, -1)
         at = lambda c: lax.dynamic_index_in_dim(low, c, 1, keepdims=False)
         dkv_got = swap(at(1 - core), C)
-        one_send, one, two_send, two = sum_first(one, one_got, two, two_got, where, (dq1,))
-        one_got, two_got = swaps(one_send, two_send, ("b0", "b1"))
         block = (1,) + low.shape[2:]
         dkv_parts = combine(
             [
@@ -1043,39 +1086,33 @@
         )
         dkv_got = turns(lambda k: dkv_parts[k])
         dkv = sum_third([dkv_parts[0]] + dkv_got, where)[0]
+        parts = sum_second(one, one_got, two, two_got, where, (dkv,))
+        ahead = turns(lambda k: parts[k])
+        wait = (parts[0],)
     else:
         dkv = lax.psum_scatter(low, (Z, C), scatter_dimension=0, tiled=True)
         mlp1 = add_low(keep, got)
-    grad_input, grads1, small1 = last_call(x1, g1, na1, dq1, dkv, dnm1, w_qkv, norm_gains[0], tab)
-    small = jnp.concatenate(
-        [grads1[width:]] + [v.astype(bf16) for v in (small1, small2, bup1, bup2)], axis=0
-    )
-    extra = 256
-    small = jnp.concatenate(
-        [small, jnp.zeros((2 * extra - small.shape[0], width), bf16)], axis=0
-    )
-    rows = jnp.concatenate(
-        [grads2[: 2 * width], small[:extra], grads2[2 * width :], grads1[:width], small[extra:]], axis=0
-    ).reshape(2, -1, width)
-    outs_keep, outs_got = pick(rows, core), swap(pick(rows, 1 - core), C)
+        wait = ()
+    grad_input, late_send, late = last_call(
+        core_row, x1, g1, na1, dq1, dkv, dnm1, w_qkv, norm_gains[0], tab, small2, bup1, bup2, early, deps=wait
+    )
+    late_got = swap(late_send, C)
 
     if direct:
-        parts = sum_second(one, one_got, two, two_got, where, (grad_input,))
-        ahead = turns(lambda k: parts[k])
-        o1_send, o1, o2_send, o2 = sum_cores(outs_keep, outs_got, where, (parts[0],))
-        o1_got, o2_got = swaps(o1_send, o2_send, ("b1", "b0"))
-        both = sum_third([parts[0]] + ahead, where, (o1,))
+        both = sum_third([parts[0]] + ahead, where, (grad_input,), us=400)
         ahead = turns(lambda k: both)
-        o1_send, o1, o2_send, o2 = sum_first(o1, o1_got, o2, o2_got, where, (both,))
-        o1_got, o2_got = swaps(o1_send, o2_send, ("b0", "b1"))
-        parts = sum_second(o1, o1_got, o2, o2_got, where)
-        outs_ahead = turns(lambda k: parts[k])
-        one, two = join([both] + ahead, (0, 1), where, (parts[0],))
+        l1_send, l1, l2_send, l2 = sum_cores(late, late_got, where, (both,), us=1)
+        l1_got, l2_got = swaps(l1_send, l2_send, ("b1", "b0"))
+        l1_send, l1, l2_send, l2 = sum_first(l1, l1_got, l2, l2_got, where, us=1)
+        l1_got, l2_got = swaps(l1_send, l2_send, ("b0", "b1"))
+        one, two = join([both] + ahead, (0, 1), where, (l1,))
         one_got, two_got = swaps(one, two, ("b0", "b1"))
-        outs = sum_third([parts[0]] + outs_ahead, where, (one, mlp2))
-        outs = gather_blocks(outs)
+        parts = sum_second(l1, l1_got, l2, l2_got, where, (one,), us=1)
+        late_ahead = turns(lambda k: parts[k])
+        late = sum_third([parts[0]] + late_ahead, where, (mlp2,))
+        outs = gather_blocks(late)
         one_near, two_near = (
-            join([v[None], g[None]], (0,), where)[0].reshape(-1, width)
+            join([v[None], g[None]], (0,), where, (late,))[0].reshape(-1, width)
             for v, g in ((one, one_got), (two, two_got))
         )
         one_far, two_far = swaps(one_near, two_near, ("b1", "b0"))
@@ -1104,6 +1141,7 @@
 
         near_one, near_two = (one_near, one_near_got), (two_near, two_near_got)
         grad_down, grad_up = put(grad_down, grad_up, near_one, near_two, False, (core, 1 - core))
+        one_far, two_far = relay((one_far, two_far), where, (grad_down, grad_up))
         one_far_got, two_far_got = swap(one_far, C), swap(two_far, C)
         grad_down, grad_up = put(grad_down, grad_up, (one_far,), (two_far,), True, (core,))
         grad_down, grad_up = put(
@@ -1113,7 +1151,7 @@
         mlp2 = gather_offloaded(reduce_offloaded(mlp2))
         placed = place_ordered(mlp2, 1)
         grad_down, grad_up = place_ordered(gather_offloaded(reduce_offloaded(mlp1)), 0, placed)
-        outs = gather_offloaded(reduce_offloaded(add_low(outs_keep, outs_got)))
+        outs = gather_offloaded(reduce_offloaded(add_low(late, late_got)))
         outs = outs.reshape(8, 2, 4, -1, width).transpose(0, 2, 1, 3, 4).reshape(32, 2, -1, width)
     grad_out, grad_q2, grad_qkv, small = finish_call(outs)
     one, two = small[0:8], small[8:16]

time: 467 us -> 454 us (0.972)
  starting transfers between devices: 84.1 us -> 72 us
  local copies, waits for them, and re-layouts: 34.5 us -> 23.3 us
  Pallas kernels: 196 us -> 204 us
    ppermute x18, waiting for transfers between devices: 54.9 us -> 37 us  [turns(): lax.ppermute(values_at(k), Z, [(i, (i + k) % size) for i in range(size)])]
    ppermute x18, starting transfers between devices: 67.2 us -> 52.3 us  [turns(): lax.ppermute(values_at(k), Z, [(i, (i + k) % size) for i in range(size)])]
    ppermute x25, waiting for transfers between devices: 67.9 us -> 82.7 us  [swap(): return lax.ppermute(values, axis, PAIR)]
    pallas_call x40 -> x42, Pallas kernels: 196 us -> 204 us  [invoke(): pl.pallas_call(body, grid_spec=pltpu.PrefetchScalarGridSpec(num_scalar_pr...]
    all_gather x2, waiting for transfers between devices: 0.01 us -> 7.54 us  [gather_blocks(): return lax.all_gather(both, (C,) + B + (Z,), axis=0, tiled=False)]
    unnamed x107 -> x119, local copies, waits for them, and re-layouts: 23.9 us -> 21 us
  transfers between devices with their start and end apart: 45 -> 45, of which waited for: 15 -> 20; matrix products, arithmetic and copies ran while one was open for 4% -> 1% of each run, Pallas kernels for 30% -> 35%
where the time goes in v3:
time: 454 us; the launch traced here: 449 us
  Pallas kernels  204 us (45%)
  waiting for transfers between devices  127 us (28%)
  starting transfers between devices  72 us (16%)
  local copies, waits for them, and re-layouts  23.3 us (5%)
  between operations  15 us (3%)
  other arithmetic  7.23 us (2%)
    pallas_call x42, Pallas kernels, invoke(): pl.pallas_call(body, grid_spec=pltpu.PrefetchScalarGridSpec(num_scalar_pr...  204 us
    ppermute x25, waiting for transfers between devices, swap(): return lax.ppermute(values, axis, PAIR)  82.7 us
    ppermute x18, starting transfers between devices, turns(): lax.ppermute(values_at(k), Z, [(i, (i + k) % size) for i in range(size)])  52.3 us
    ppermute x18, waiting for transfers between devices, turns(): lax.ppermute(values_at(k), Z, [(i, (i + k) % size) for i in range(size)])  37 us
    unnamed x119, local copies, waits for them, and re-layouts  21 us
    ppermute x25, starting transfers between devices, swap(): return lax.ppermute(values, axis, PAIR)  19.6 us
  transfers between devices with their start and end apart: 45, of which 20 were waited for; matrix products, arithmetic and copies ran while one was open for 1% of the time, Pallas kernels for 35%

profile of v3, /device:TPU:0, one launch (start us, length us, event | category | flops | bytes accessed | tf_op | source)
XLA Modules:
  0.0 448.7 jit_solution(15961738890903619661)
XLA Ops:
  22.7 11.6 %mlp_fwd.1 = (f32[512,768]{1,0:T(8,128)S(1)}, bf16[512,3072]{1,0:T(8,128)(2,1)}, bf16[512,3072]{1,0:T(8,128)(2,1)}) custom-call(bf16[512,768]{1,0:T(8,128)(2,1)S(1)} %get-tuple-element.108.refs_0_.refs_1_, bf16[2,768,3072]{2,1,0:T(8,128)(2,1)} %refs_3_.13, f32[1,3072]{1,0:T(1,128)S(1)} %get-tuple-element.210.refs_2_, bf16[2,3072,768]{2,1,0:T(8,128)(2,1)} %refs_4_.3), custom_call_target="tpu_custom_call" | custom-call | flops 6000000000 | bytes 10000000 | tf_op jit(solution)/shard_map/mlp_fwd/pallas_call | solution.py:48
  40.2 5.8 %attend.2 = (bf16[512,768]{1,0:T(8,128)(2,1)S(1)}, f32[4,2,8,768]{3,2,1,0:T(8,128)S(1)}) custom-call(s32[9]{0:T(128)S(1)} %pad_add_fusion.refs_0_, bf16[512,768]{1,0:T(8,128)(2,1)S(1)} %copy-done.32, bf16[4,128,512]{2,1,0:T(8,128)(2,1)S(1)} %join.4.refs_2_, bf16[4,128,512]{2,1,0:T(8,128)(2,1)S(1)} %collective-permute-done.3.refs_3_, ...), custom_call_target="tpu_custom_call" | custom-call | flops 35999997952 | bytes 60000000 | tf_op jit(solution)/shard_map/attend/pallas_call | solution.py:48
  46.1 5.5 %middle.1 = (bf16[512,768]{1,0:T(8,128)(2,1)S(1)}, bf16[512,768]{1,0:T(8,128)(2,1)S(1)}, bf16[512,768]{1,0:T(8,128)(2,1)S(1)}, bf16[512,768]{1,0:T(8,128)(2,1)S(1)}) custom-call(bf16[512,768]{1,0:T(8,128)(2,1)S(1)} %get-tuple-element.110.refs_0_.refs_3_.refs_4_, bf16[512,768]{1,0:T(8,128)(2,1)} %bitcast.126, f32[512,768]{1,0:T(8,128)} %copy-done.18, ...), custom_call_target="tpu_custom_call" | custom-call | flops 3000000000 | bytes 5000000 | tf_op jit(solution)/shard_map/middle/pallas_call | solution.py:48
  53.5 14.0 %mlp_both.2 = (f32[512,768]{1,0:T(8,128)S(1)}, f32[512,768]{1,0:T(8,128)}, bf16[2,1536,768]{2,1,0:T(8,128)(2,1)}, f32[1,1536]{1,0:T(1,128)S(1)}) custom-call(s32[1]{0:T(128)} %bitcast.11.refs_0_, bf16[512,768]{1,0:T(8,128)(2,1)S(1)} %get-tuple-element.112.refs_1_, bf16[512,768]{1,0:T(8,128)(2,1)S(1)} %bitcast.119, bf16[2,768,3072]{2,1,0:T(8,128)(2,1)} %refs_3_.13, ...), custom_call_target="tpu_custom_call" | custom-call | flops 24000000000 | bytes 40000000 | tf_op jit(solution)/shard_map/mlp_both/pallas_call | solution.py:48
  69.9 14.4 %mlp_both.3 = (f32[512,768]{1,0:T(8,128)S(1)}, f32[512,768]{1,0:T(8,128)}, bf16[2,1536,768]{2,1,0:T(8,128)(2,1)}, f32[1,1536]{1,0:T(1,128)S(1)}) custom-call(s32[1]{0:T(128)} %bitcast.11.refs_0_, bf16[512,768]{1,0:T(8,128)(2,1)S(1)} %copy-done.28, bf16[512,768]{1,0:T(8,128)(2,1)S(1)} %bitcast.120, bf16[2,768,3072]{2,1,0:T(8,128)(2,1)} %refs_3_.13, ...), custom_call_target="tpu_custom_call" | custom-call | flops 24000000000 | bytes 40000000 | tf_op jit(solution)/shard_map/mlp_both/pallas_call | solution.py:48
  85.5 6.0 %sum_cores.3 = (bf16[2,384,768]{2,1,0:T(8,128)(2,1)S(1)}, bf16[2,384,768]{2,1,0:T(8,128)(2,1)S(1)}, bf16[2,384,768]{2,1,0:T(8,128)(2,1)S(1)}, bf16[2,384,768]{2,1,0:T(8,128)(2,1)}) custom-call(s32[4]{0:T(128)S(1)} %pad_add_fusion.1.refs_0_, bf16[2,2,2,384,768]{4,3,2,1,0:T(8,128)(2,1)} %bitcast.173, ...), custom_call_target="tpu_custom_call" | custom-call | flops 12000000000 | bytes 20000000 | tf_op jit(solution)/shard_map/sum_cores/pallas_call | solution.py:48
  94.6 5.9 %attend.3 = (bf16[512,768]{1,0:T(8,128)(2,1)S(1)}, f32[4,2,8,768]{3,2,1,0:T(8,128)S(1)}) custom-call(s32[9]{0:T(128)S(1)} %pad_add_fusion.refs_0_, bf16[512,768]{1,0:T(8,128)(2,1)S(1)} %copy-done.26, bf16[4,128,512]{2,1,0:T(8,128)(2,1)S(1)} %join.4.refs_2_, bf16[4,128,512]{2,1,0:T(8,128)(2,1)S(1)} %copy-done.13, ...), custom_call_target="tpu_custom_call" | custom-call | flops 35999997952 | bytes 60000000 | tf_op jit(solution)/shard_map/attend/pallas_call | solution.py:48
  100.5 6.0 %attend_back.3 = (bf16[512,768]{1,0:T(8,128)(2,1)S(1)}, f32[1024,512]{1,0:T(8,128)}) custom-call(s32[9]{0:T(128)S(1)} %pad_add_fusion.refs_0_, bf16[512,768]{1,0:T(8,128)(2,1)S(1)} %copy-done.26, bf16[4,128,512]{2,1,0:T(8,128)(2,1)S(1)} %join.4.refs_2_, bf16[4,128,512]{2,1,0:T(8,128)(2,1)S(1)} %copy-done.13, ...), custom_call_target="tpu_custom_call" | custom-call | flops 27000000512 | bytes 45000000 | tf_op jit(solution)/shard_map/attend_back/pallas_call | solution.py:48
  106.5 13.4 %collective-permute-done.5.refs_2_.refs_4_ = bf16[2,384,768]{2,1,0:T(8,128)(2,1)S(1)} collective-permute-done((bf16[2,384,768]{2,1,0:T(8,128)(2,1)S(1)}, bf16[2,384,768]{2,1,0:T(8,128)(2,1)S(1)}, u32[]{:S(2)}, u32[]{:S(2)}) %collective-permute-start.5) | collective-permute-done | bytes 1179680 | tf_op jit(solution)/shard_map/ppermute | solution.py:672
  127.6 6.3 %attend_back.4 = (bf16[512,768]{1,0:T(8,128)(2,1)S(1)}, f32[1024,512]{1,0:T(8,128)}) custom-call(s32[9]{0:T(128)S(1)} %pad_add_fusion.refs_0_, bf16[512,768]{1,0:T(8,128)(2,1)S(1)} %copy-done.26, bf16[4,128,512]{2,1,0:T(8,128)(2,1)S(1)} %join.4.refs_2_, bf16[4,128,512]{2,1,0:T(8,128)(2,1)S(1)} %copy-done.13, ...), custom_call_target="tpu_custom_call", output_to_operand_aliasing={{0}: (8, {}), {1}: (9, {})} | custom-call | flops 27000000512 | bytes 45000000 | tf_op jit(solution)/shard_map/attend_back/pallas_call | solution.py:48
  141.9 7.9 %collective-permute-start.10 = (bf16[2,96,768]{2,1,0:T(8,128)(2,1)S(1)}, bf16[2,96,768]{2,1,0:T(8,128)(2,1)S(1)}, u32[]{:S(2)}, u32[]{:S(2)}) collective-permute-start(bf16[2,96,768]{2,1,0:T(8,128)(2,1)S(1)} %get-tuple-element.145), channel_id=1, source_target_pairs={{0,4},{2,6},{4,0},{6,2},{1,5},{3,7},{5,1},{7,3},{8,12},{10,14},{12... | collective-permute-start | bytes 884744 | tf_op jit(solution)/shard_map/ppermute | solution.py:693
  149.9 7.3 %collective-permute-start.11 = (bf16[2,96,768]{2,1,0:T(8,128)(2,1)S(1)}, bf16[2,96,768]{2,1,0:T(8,128)(2,1)S(1)}, u32[]{:S(2)}, u32[]{:S(2)}) collective-permute-start(bf16[2,96,768]{2,1,0:T(8,128)(2,1)S(1)} %get-tuple-element.146), channel_id=1, source_target_pairs={{0,6},{2,0},{4,2},{6,4},{1,7},{3,1},{5,3},{7,5},{8,14},{10,8},{12,... | collective-permute-start | bytes 884744 | tf_op jit(solution)/shard_map/ppermute | solution.py:693
  157.7 10.8 %turn.1 = (bf16[512,768]{1,0:T(8,128)(2,1)}, bf16[2304,768]{1,0:T(8,128)(2,1)}, bf16[512,768]{1,0:T(8,128)(2,1)S(1)}, bf16[512,768]{1,0:T(8,128)(2,1)S(1)}, f32[8,768]{1,0:T(8,128)S(1)}) custom-call(bf16[512,768]{1,0:T(8,128)(2,1)S(1)} %copy-done.23, f32[512,768]{1,0:T(8,128)} %copy-done.39, bf16[512,768]{1,0:T(8,128)(2,1)S(1)} %copy-done.44, ...), custom_call_target="tpu_custom_call" | custom-call | flops 35999997952 | bytes 60000000 | tf_op jit(solution)/shard_map/turn/pallas_call | solution.py:48
  168.5 11.1 %mlp_back.2 = (f32[512,768]{1,0:T(8,128)S(1)}, bf16[2,1536,768]{2,1,0:T(8,128)(2,1)}, f32[1,1536]{1,0:T(1,128)S(1)}) custom-call(s32[1]{0:T(128)} %bitcast.11.refs_0_, bf16[512,768]{1,0:T(8,128)(2,1)S(1)} %copy-done.3, bf16[512,768]{1,0:T(8,128)(2,1)S(1)} %get-tuple-element.136.refs_2_, bf16[2,768,3072]{2,1,0:T(8,128)(2,1)} %refs_3_.13, ...), custom_call_target="tpu_custom_call" | custom-call | flops 7200000000 | bytes 12000000 | tf_op jit(solution)/shard_map/mlp_back/pallas_call | solution.py:48
  182.3 12.1 %mlp_back.3 = (f32[512,768]{1,0:T(8,128)S(1)}, bf16[2,1536,768]{2,1,0:T(8,128)(2,1)}, f32[1,1536]{1,0:T(1,128)S(1)}) custom-call(s32[1]{0:T(128)} %bitcast.11.refs_0_, bf16[512,768]{1,0:T(8,128)(2,1)S(1)} %copy-done.3, bf16[512,768]{1,0:T(8,128)(2,1)S(1)} %get-tuple-element.136.refs_2_, bf16[2,768,3072]{2,1,0:T(8,128)(2,1)} %refs_3_.13, ...), custom_call_target="tpu_custom_call" | custom-call | flops 89999998976 | bytes 150000000 | tf_op jit(solution)/shard_map/mlp_back/pallas_call | solution.py:48
  195.6 6.1 %sum_cores.4 = (bf16[2,384,768]{2,1,0:T(8,128)(2,1)S(1)}, bf16[2,384,768]{2,1,0:T(8,128)(2,1)S(1)}, bf16[2,384,768]{2,1,0:T(8,128)(2,1)S(1)}, bf16[2,384,768]{2,1,0:T(8,128)(2,1)}) custom-call(s32[4]{0:T(128)S(1)} %pad_add_fusion.1.refs_0_, bf16[2,2,2,384,768]{4,3,2,1,0:T(8,128)(2,1)} %bitcast.177, ...), custom_call_target="tpu_custom_call" | custom-call | flops 12000000000 | bytes 20000000 | tf_op jit(solution)/shard_map/sum_cores/pallas_call | solution.py:48
  205.5 9.8 %attend_back.5 = (bf16[512,768]{1,0:T(8,128)(2,1)S(1)}, f32[1024,512]{1,0:T(8,128)}) custom-call(s32[9]{0:T(128)S(1)} %pad_add_fusion.refs_0_, bf16[512,768]{1,0:T(8,128)(2,1)S(1)} %copy-done.33, bf16[4,128,512]{2,1,0:T(8,128)(2,1)S(1)} %join.4.refs_2_, bf16[4,128,512]{2,1,0:T(8,128)(2,1)S(1)} %copy-done.14, bf16[512,768]{1,0:T(8,128)(2,1)S(1)} %copy-done.21, ...), custom_call_target="tpu_custom_call" | custom-call | flops 27000000512 | bytes 45000000 | tf_op jit(solution)/shard_map/attend_back/pallas_call | solution.py:48
  217.5 22.0 %collective-permute-done.14.refs_2_.refs_4_ = bf16[2,384,768]{2,1,0:T(8,128)(2,1)S(1)} collective-permute-done((bf16[2,384,768]{2,1,0:T(8,128)(2,1)S(1)}, bf16[2,384,768]{2,1,0:T(8,128)(2,1)S(1)}, u32[]{:S(2)}, u32[]{:S(2)}) %collective-permute-start.14) | collective-permute-done | bytes 1179680 | tf_op jit(solution)/shard_map/ppermute | solution.py:672
  256.2 9.1 %collective-permute-done.17.refs_3_ = bf16[1,128,512]{2,1,0:T(8,128)(2,1)S(1)} collective-permute-done((bf16[1,128,512]{2,1,0:T(8,128)(2,1)S(1)}, bf16[1,128,512]{2,1,0:T(8,128)(2,1)S(1)}, u32[]{:S(2)}, u32[]{:S(2)}) %collective-permute-start.17) | collective-permute-done | bytes 131104 | tf_op jit(solution)/shard_map/ppermute | solution.py:693
  266.9 6.2 %collective-permute-done.19 = bf16[1,384,768]{2,1,0:T(8,128)(2,1)} collective-permute-done((bf16[1,384,768]{2,1,0:T(8,128)(2,1)S(1)}, bf16[1,384,768]{2,1,0:T(8,128)(2,1)}, u32[]{:S(2)}, u32[]{:S(2)}) %collective-permute-start.19) | collective-permute-done | bytes 589856 | tf_op jit(solution)/shard_map/ppermute | solution.py:672
  280.8 8.9 %last.1 = (f32[512,768]{1,0:T(8,128)}, bf16[1792,768]{1,0:T(8,128)(2,1)}, bf16[1792,768]{1,0:T(8,128)(2,1)}) custom-call(s32[1]{0:T(128)} %bitcast.11.refs_0_, bf16[512,768]{1,0:T(8,128)(2,1)S(1)} %bitcast.128, bf16[512,768]{1,0:T(8,128)(2,1)S(1)} %get-tuple-element.136.refs_2_, bf16[512,768]{1,0:T(8,128)(2,1)S(1)} %copy-done.30, ...), custom_call_target="tpu_custom_call" | custom-call | flops 6000000000 | bytes 10000000 | tf_op jit(solution)/shard_map/last/pallas_call | solution.py:48
  289.7 10.5 %collective-permute-done.23.refs_3_ = bf16[2,96,768]{2,1,0:T(8,128)(2,1)S(1)} collective-permute-done((bf16[2,96,768]{2,1,0:T(8,128)(2,1)S(1)}, bf16[2,96,768]{2,1,0:T(8,128)(2,1)S(1)}, u32[]{:S(2)}, u32[]{:S(2)}) %collective-permute-start.23) | collective-permute-done | bytes 294944 | tf_op jit(solution)/shard_map/ppermute | solution.py:693
  309.4 6.9 %collective-permute-start.29 = (bf16[2,96,768]{2,1,0:T(8,128)(2,1)S(1)}, bf16[2,96,768]{2,1,0:T(8,128)(2,1)S(1)}, u32[]{:S(2)}, u32[]{:S(2)}) collective-permute-start(bf16[2,96,768]{2,1,0:T(8,128)(2,1)S(1)} %sum_third.6.refs_9_.refs_1_.refs_5_), channel_id=1, source_target_pairs={{0,2},{2,4},{4,6},{6,0},{1,3},{3,5},{5,7},{7,1},{8,10},{10,12},{12... | collective-permute-start | bytes 884744 | tf_op jit(solution)/shard_map/ppermute | solution.py:693
  318.7 5.5 %collective-permute-done.25.refs_2_.refs_4_ = bf16[2,224,768]{2,1,0:T(8,128)(2,1)S(1)} collective-permute-done((bf16[2,224,768]{2,1,0:T(8,128)(2,1)S(1)}, bf16[2,224,768]{2,1,0:T(8,128)(2,1)S(1)}, u32[]{:S(2)}, u32[]{:S(2)}) %collective-permute-start.25) | collective-permute-done | bytes 688160 | tf_op jit(solution)/shard_map/ppermute | solution.py:672
  329.8 5.7 %collective-permute-done.30.refs_3_.refs_7_ = bf16[2,96,768]{2,1,0:T(8,128)(2,1)S(1)} collective-permute-done((bf16[2,96,768]{2,1,0:T(8,128)(2,1)S(1)}, bf16[2,96,768]{2,1,0:T(8,128)(2,1)S(1)}, u32[]{:S(2)}, u32[]{:S(2)}) %collective-permute-start.30) | collective-permute-done | bytes 294944 | tf_op jit(solution)/shard_map/ppermute | solution.py:693
  338.8 6.9 %collective-permute-start.32 = (bf16[2,56,768]{2,1,0:T(8,128)(2,1)S(1)}, bf16[2,56,768]{2,1,0:T(8,128)(2,1)S(1)}, u32[]{:S(2)}, u32[]{:S(2)}) collective-permute-start(bf16[2,56,768]{2,1,0:T(8,128)(2,1)S(1)} %get-tuple-element.187), channel_id=1, source_target_pairs={{0,2},{2,4},{4,6},{6,0},{1,3},{3,5},{5,7},{7,1},{8,10},{10,12},{12... | collective-permute-start | bytes 516104 | tf_op jit(solution)/shard_map/ppermute | solution.py:693
  351.2 5.6 %collective-permute-done.33.refs_3_ = bf16[2,56,768]{2,1,0:T(8,128)(2,1)S(1)} collective-permute-done((bf16[2,56,768]{2,1,0:T(8,128)(2,1)S(1)}, bf16[2,56,768]{2,1,0:T(8,128)(2,1)S(1)}, u32[]{:S(2)}, u32[]{:S(2)}) %collective-permute-start.33) | collective-permute-done | bytes 172064 | tf_op jit(solution)/shard_map/ppermute | solution.py:693
  359.4 15.1 %collective-permute-done.37 = bf16[4,96,768]{2,1,0:T(8,128)(2,1)S(1)} collective-permute-done((bf16[4,96,768]{2,1,0:T(8,128)(2,1)S(1)}, bf16[4,96,768]{2,1,0:T(8,128)(2,1)S(1)}, u32[]{:S(2)}, u32[]{:S(2)}) %collective-permute-start.37) | collective-permute-done | bytes 589856 | tf_op jit(solution)/shard_map/ppermute | solution.py:672
  377.9 11.4 %spread.1 = (f32[2,3072,768]{2,1,0:T(8,128)}, f32[2,768,3072]{2,1,0:T(8,128)}) custom-call(bf16[8,4,2,96,768]{4,3,2,1,0:T(8,128)(2,1)} %bitcast.164, bf16[768,768]{1,0:T(8,128)(2,1)S(1)} %bitcast.115, bf16[768,768]{1,0:T(8,128)(2,1)S(1)} %bitcast.111), custom_call_target="tpu_custom_call" | custom-call | flops 1200000000 | bytes 2000000 | tf_op jit(solution)/shard_map/spread/pallas_call | solution.py:48
  399.4 7.6 %collective-permute-done.38.refs_2_ = bf16[768,768]{1,0:T(8,128)(2,1)} collective-permute-done((bf16[768,768]{1,0:T(8,128)(2,1)S(1)}, bf16[768,768]{1,0:T(8,128)(2,1)}, u32[]{:S(2)}, u32[]{:S(2)}) %collective-permute-start.38) | collective-permute-done | bytes 1179680 | tf_op jit(solution)/shard_map/ppermute | solution.py:672
  423.8 7.5 %all-gather.7.cloned.1.call-done = bf16[64,56,768]{2,1,0:T(8,128)(2,1)} async-done(((bf16[2,56,768]{2,1,0:T(8,128)(2,1)}), bf16[64,56,768]{2,1,0:T(8,128)(2,1)}) %all-gather.7.cloned.1.call-update) | async-done | bytes 5505040 | tf_op jit(solution)/shard_map/all_gather | solution.py:817
  431.3 6.6 %finish.1 = (f32[2,768,768]{2,1,0:T(8,128)}, f32[768,768]{1,0:T(8,128)}, f32[768,896]{1,0:T(8,128)}, f32[128,768]{1,0:T(8,128)S(1)}) custom-call(bf16[32,2,56,768]{3,2,1,0:T(8,128)(2,1)} %bitcast.170), custom_call_target="tpu_custom_call" | custom-call | flops 3600000000 | bytes 6000000 | tf_op jit(solution)/shard_map/finish/pallas_call | solution.py:48
  (258 shorter events, 144.2 us)
Async XLA Ops:
  7.2 349.6 %all-gather.5.cloned.1.call-start = ((), (), s32[]{:S(2)}) async-start(), calls=%async_computation | async-start | bytes 9732096 | tf_op jit(solution)/shard_map/all_gather | solution.py:817
  15.2 20.3 %collective-permute-start = (bf16[128,512]{1,0:T(8,128)(2,1)S(1)}, bf16[128,512]{1,0:T(8,128)(2,1)S(1)}, u32[]{:S(2)}, u32[]{:S(2)}) collective-permute-start(bf16[128,512]{1,0:T(8,128)(2,1)S(1)} %get-tuple-element.107), channel_id=1, source_target_pairs={{0,2},{2,4},{4,6},{6,0},{1,3},{3,5},{5,7},{7,1},{8,10},{10,12},{12... | collective-permute-start | bytes 393224 | tf_op jit(solution)/shard_map/ppermute | solution.py:693
  18.2 17.3 %collective-permute-start.1 = (bf16[128,512]{1,0:T(8,128)(2,1)S(1)}, bf16[128,512]{1,0:T(8,128)(2,1)S(1)}, u32[]{:S(2)}, u32[]{:S(2)}) collective-permute-start(bf16[128,512]{1,0:T(8,128)(2,1)S(1)} %get-tuple-element.107), channel_id=1, source_target_pairs={{0,4},{2,6},{4,0},{6,2},{1,5},{3,7},{5,1},{7,3},{8,12},{10,14},{12... | collective-permute-start | bytes 393224 | tf_op jit(solution)/shard_map/ppermute | solution.py:693
  20.8 14.7 %collective-permute-start.2 = (bf16[128,512]{1,0:T(8,128)(2,1)S(1)}, bf16[128,512]{1,0:T(8,128)(2,1)S(1)}, u32[]{:S(2)}, u32[]{:S(2)}) collective-permute-start(bf16[128,512]{1,0:T(8,128)(2,1)S(1)} %get-tuple-element.107), channel_id=1, source_target_pairs={{0,6},{2,0},{4,2},{6,4},{1,7},{3,1},{5,3},{7,5},{8,14},{10,8},{12,... | collective-permute-start | bytes 393224 | tf_op jit(solution)/shard_map/ppermute | solution.py:693
  68.6 16.9 %collective-permute-start.4 = (bf16[3072,768]{1,0:T(8,128)(2,1)}, bf16[3072,768]{1,0:T(8,128)(2,1)}, u32[]{:S(2)}, u32[]{:S(2)}) collective-permute-start(bf16[3072,768]{1,0:T(8,128)(2,1)} %bitcast.172), channel_id=1, source_target_pairs={{0,1},{1,0},{2,3},{3,2},{4,5},{5,4},{6,7},{7,6},{8,9},{9,8},{10,11... | collective-permute-start | bytes 14155784 | tf_op jit(solution)/shard_map/ppermute | solution.py:672
  91.6 28.3 %collective-permute-start.5 = (bf16[2,384,768]{2,1,0:T(8,128)(2,1)S(1)}, bf16[2,384,768]{2,1,0:T(8,128)(2,1)S(1)}, u32[]{:S(2)}, u32[]{:S(2)}) collective-permute-start(bf16[2,384,768]{2,1,0:T(8,128)(2,1)S(1)} %get-tuple-element.125), channel_id=1, source_target_pairs={{0,8},{8,0},{1,9},{9,1},{2,10},{10,2},{3,11},{11,3},{4,12},{12,4},... | collective-permute-start | bytes 3538952 | tf_op jit(solution)/shard_map/ppermute | solution.py:672
  93.1 28.0 %collective-permute-start.6 = (bf16[2,384,768]{2,1,0:T(8,128)(2,1)S(1)}, bf16[2,384,768]{2,1,0:T(8,128)(2,1)S(1)}, u32[]{:S(2)}, u32[]{:S(2)}) collective-permute-start(bf16[2,384,768]{2,1,0:T(8,128)(2,1)S(1)} %get-tuple-element.127), channel_id=1, source_target_pairs={{0,16},{16,0},{1,17},{17,1},{2,18},{18,2},{3,19},{19,3},{4,20},{20... | collective-permute-start | bytes 3538952 | tf_op jit(solution)/shard_map/ppermute | solution.py:672
  125.3 14.5 %collective-permute-start.7 = (bf16[1,384,768]{2,1,0:T(8,128)(2,1)S(1)}, bf16[1,384,768]{2,1,0:T(8,128)(2,1)S(1)}, u32[]{:S(2)}, u32[]{:S(2)}) collective-permute-start(bf16[1,384,768]{2,1,0:T(8,128)(2,1)S(1)} %get-tuple-element.131), channel_id=1, source_target_pairs={{0,16},{16,0},{1,17},{17,1},{2,18},{18,2},{3,19},{19,3},{4,20},{20... | collective-permute-start | bytes 1769480 | tf_op jit(solution)/shard_map/ppermute | solution.py:672
  141.9 37.7 %collective-permute-start.10 = (bf16[2,96,768]{2,1,0:T(8,128)(2,1)S(1)}, bf16[2,96,768]{2,1,0:T(8,128)(2,1)S(1)}, u32[]{:S(2)}, u32[]{:S(2)}) collective-permute-start(bf16[2,96,768]{2,1,0:T(8,128)(2,1)S(1)} %get-tuple-element.145), channel_id=1, source_target_pairs={{0,4},{2,6},{4,0},{6,2},{1,5},{3,7},{5,1},{7,3},{8,12},{10,14},{12... | collective-permute-start | bytes 884744 | tf_op jit(solution)/shard_map/ppermute | solution.py:693
  149.9 29.8 %collective-permute-start.11 = (bf16[2,96,768]{2,1,0:T(8,128)(2,1)S(1)}, bf16[2,96,768]{2,1,0:T(8,128)(2,1)S(1)}, u32[]{:S(2)}, u32[]{:S(2)}) collective-permute-start(bf16[2,96,768]{2,1,0:T(8,128)(2,1)S(1)} %get-tuple-element.146), channel_id=1, source_target_pairs={{0,6},{2,0},{4,2},{6,4},{1,7},{3,1},{5,3},{7,5},{8,14},{10,8},{12,... | collective-permute-start | bytes 884744 | tf_op jit(solution)/shard_map/ppermute | solution.py:693
  157.2 22.4 %collective-permute-start.9 = (bf16[2,96,768]{2,1,0:T(8,128)(2,1)S(1)}, bf16[2,96,768]{2,1,0:T(8,128)(2,1)S(1)}, u32[]{:S(2)}, u32[]{:S(2)}) collective-permute-start(bf16[2,96,768]{2,1,0:T(8,128)(2,1)S(1)} %get-tuple-element.144), channel_id=1, source_target_pairs={{0,2},{2,4},{4,6},{6,0},{1,3},{3,5},{5,7},{7,1},{8,10},{10,12},{12... | collective-permute-start | bytes 884744 | tf_op jit(solution)/shard_map/ppermute | solution.py:693
  179.6 16.0 %collective-permute-start.12 = (bf16[3072,768]{1,0:T(8,128)(2,1)}, bf16[3072,768]{1,0:T(8,128)(2,1)}, u32[]{:S(2)}, u32[]{:S(2)}) collective-permute-start(bf16[3072,768]{1,0:T(8,128)(2,1)} %bitcast.171), channel_id=1, source_target_pairs={{0,1},{1,0},{2,3},{3,2},{4,5},{5,4},{6,7},{7,6},{8,9},{9,8},{10,11... | collective-permute-start | bytes 14155784 | tf_op jit(solution)/shard_map/ppermute | solution.py:672
  182.3 249.1 %all-gather.7.cloned.1.call-start = ((), (), s32[]{:S(2)}) async-start(), calls=%async_computation.1 | async-start | bytes 5677056 | tf_op jit(solution)/shard_map/all_gather | solution.py:817
  202.7 36.8 %collective-permute-start.14 = (bf16[2,384,768]{2,1,0:T(8,128)(2,1)S(1)}, bf16[2,384,768]{2,1,0:T(8,128)(2,1)S(1)}, u32[]{:S(2)}, u32[]{:S(2)}) collective-permute-start(bf16[2,384,768]{2,1,0:T(8,128)(2,1)S(1)} %get-tuple-element.153), channel_id=1, source_target_pairs={{0,8},{8,0},{1,9},{9,1},{2,10},{10,2},{3,11},{11,3},{4,12},{12,4},... | collective-permute-start | bytes 3538952 | tf_op jit(solution)/shard_map/ppermute | solution.py:672
  204.0 35.5 %collective-permute-start.15 = (bf16[2,384,768]{2,1,0:T(8,128)(2,1)S(1)}, bf16[2,384,768]{2,1,0:T(8,128)(2,1)S(1)}, u32[]{:S(2)}, u32[]{:S(2)}) collective-permute-start(bf16[2,384,768]{2,1,0:T(8,128)(2,1)S(1)} %get-tuple-element.155), channel_id=1, source_target_pairs={{0,16},{16,0},{1,17},{17,1},{2,18},{18,2},{3,19},{19,3},{4,20},{20... | collective-permute-start | bytes 3538952 | tf_op jit(solution)/shard_map/ppermute | solution.py:672
  217.4 27.1 %collective-permute-start.13 = (bf16[4,128,512]{2,1,0:T(8,128)(2,1)S(1)}, bf16[4,128,512]{2,1,0:T(8,128)(2,1)S(1)}, u32[]{:S(2)}, u32[]{:S(2)}) collective-permute-start(bf16[4,128,512]{2,1,0:T(8,128)(2,1)S(1)} %dynamic-slice_bitcast_fusion), channel_id=1, source_target_pairs={{0,1},{1,0},{2,3},{3,2},{4,5},{5,4},{6,7},{7,6},{8,9},{9,8},{10,11... | collective-permute-start | bytes 1572872 | tf_op jit(solution)/shard_map/ppermute | solution.py:672
  247.2 18.2 %collective-permute-start.17 = (bf16[1,128,512]{2,1,0:T(8,128)(2,1)S(1)}, bf16[1,128,512]{2,1,0:T(8,128)(2,1)S(1)}, u32[]{:S(2)}, u32[]{:S(2)}) collective-permute-start(bf16[1,128,512]{2,1,0:T(8,128)(2,1)S(1)} %get-tuple-element.159), channel_id=1, source_target_pairs={{0,4},{2,6},{4,0},{6,2},{1,5},{3,7},{5,1},{7,3},{8,12},{10,14},{12... | collective-permute-start | bytes 393224 | tf_op jit(solution)/shard_map/ppermute | solution.py:693
  249.6 15.8 %collective-permute-start.18 = (bf16[1,128,512]{2,1,0:T(8,128)(2,1)S(1)}, bf16[1,128,512]{2,1,0:T(8,128)(2,1)}, u32[]{:S(2)}, u32[]{:S(2)}) collective-permute-start(bf16[1,128,512]{2,1,0:T(8,128)(2,1)S(1)} %get-tuple-element.160), channel_id=1, source_target_pairs={{0,6},{2,0},{4,2},{6,4},{1,7},{3,1},{5,3},{7,5},{8,14},{10,8},{12,... | collective-permute-start | bytes 393224 | tf_op jit(solution)/shard_map/ppermute | solution.py:693
  250.3 22.7 %collective-permute-start.19 = (bf16[1,384,768]{2,1,0:T(8,128)(2,1)S(1)}, bf16[1,384,768]{2,1,0:T(8,128)(2,1)}, u32[]{:S(2)}, u32[]{:S(2)}) collective-permute-start(bf16[1,384,768]{2,1,0:T(8,128)(2,1)S(1)} %get-tuple-element.167), channel_id=1, source_target_pairs={{0,16},{16,0},{1,17},{17,1},{2,18},{18,2},{3,19},{19,3},{4,20},{20... | collective-permute-start | bytes 1769480 | tf_op jit(solution)/shard_map/ppermute | solution.py:672
  251.8 21.2 %collective-permute-start.20 = (bf16[1,384,768]{2,1,0:T(8,128)(2,1)S(1)}, bf16[1,384,768]{2,1,0:T(8,128)(2,1)}, u32[]{:S(2)}, u32[]{:S(2)}) collective-permute-start(bf16[1,384,768]{2,1,0:T(8,128)(2,1)S(1)} %get-tuple-element.169), channel_id=1, source_target_pairs={{0,8},{8,0},{1,9},{9,1},{2,10},{10,2},{3,11},{11,3},{4,12},{12,4},... | collective-permute-start | bytes 1769480 | tf_op jit(solution)/shard_map/ppermute | solution.py:672
  277.0 23.1 %collective-permute-start.23 = (bf16[2,96,768]{2,1,0:T(8,128)(2,1)S(1)}, bf16[2,96,768]{2,1,0:T(8,128)(2,1)S(1)}, u32[]{:S(2)}, u32[]{:S(2)}) collective-permute-start(bf16[2,96,768]{2,1,0:T(8,128)(2,1)S(1)} %get-tuple-element.175), channel_id=1, source_target_pairs={{0,4},{2,6},{4,0},{6,2},{1,5},{3,7},{5,1},{7,3},{8,12},{10,14},{12... | collective-permute-start | bytes 884744 | tf_op jit(solution)/shard_map/ppermute | solution.py:693
  280.0 20.2 %collective-permute-start.24 = (bf16[2,96,768]{2,1,0:T(8,128)(2,1)S(1)}, bf16[2,96,768]{2,1,0:T(8,128)(2,1)S(1)}, u32[]{:S(2)}, u32[]{:S(2)}) collective-permute-start(bf16[2,96,768]{2,1,0:T(8,128)(2,1)S(1)} %get-tuple-element.176), channel_id=1, source_target_pairs={{0,6},{2,0},{4,2},{6,4},{1,7},{3,1},{5,3},{7,5},{8,14},{10,8},{12,... | collective-permute-start | bytes 884744 | tf_op jit(solution)/shard_map/ppermute | solution.py:693
  306.8 17.4 %collective-permute-start.25 = (bf16[2,224,768]{2,1,0:T(8,128)(2,1)S(1)}, bf16[2,224,768]{2,1,0:T(8,128)(2,1)S(1)}, u32[]{:S(2)}, u32[]{:S(2)}) collective-permute-start(bf16[2,224,768]{2,1,0:T(8,128)(2,1)S(1)} %get-tuple-element.178), channel_id=1, source_target_pairs={{0,8},{8,0},{1,9},{9,1},{2,10},{10,2},{3,11},{11,3},{4,12},{12,4},... | collective-permute-start | bytes 2064392 | tf_op jit(solution)/shard_map/ppermute | solution.py:672
  308.3 16.8 %collective-permute-start.26 = (bf16[2,224,768]{2,1,0:T(8,128)(2,1)S(1)}, bf16[2,224,768]{2,1,0:T(8,128)(2,1)S(1)}, u32[]{:S(2)}, u32[]{:S(2)}) collective-permute-start(bf16[2,224,768]{2,1,0:T(8,128)(2,1)S(1)} %get-tuple-element.180), channel_id=1, source_target_pairs={{0,16},{16,0},{1,17},{17,1},{2,18},{18,2},{3,19},{19,3},{4,20},{20... | collective-permute-start | bytes 2064392 | tf_op jit(solution)/shard_map/ppermute | solution.py:672
  309.4 20.4 %collective-permute-start.29 = (bf16[2,96,768]{2,1,0:T(8,128)(2,1)S(1)}, bf16[2,96,768]{2,1,0:T(8,128)(2,1)S(1)}, u32[]{:S(2)}, u32[]{:S(2)}) collective-permute-start(bf16[2,96,768]{2,1,0:T(8,128)(2,1)S(1)} %sum_third.6.refs_9_.refs_1_.refs_5_), channel_id=1, source_target_pairs={{0,2},{2,4},{4,6},{6,0},{1,3},{3,5},{5,7},{7,1},{8,10},{10,12},{12... | collective-permute-start | bytes 884744 | tf_op jit(solution)/shard_map/ppermute | solution.py:693
  316.3 19.2 %collective-permute-start.30 = (bf16[2,96,768]{2,1,0:T(8,128)(2,1)S(1)}, bf16[2,96,768]{2,1,0:T(8,128)(2,1)S(1)}, u32[]{:S(2)}, u32[]{:S(2)}) collective-permute-start(bf16[2,96,768]{2,1,0:T(8,128)(2,1)S(1)} %sum_third.6.refs_9_.refs_1_.refs_5_), channel_id=1, source_target_pairs={{0,4},{2,6},{4,0},{6,2},{1,5},{3,7},{5,1},{7,3},{8,12},{10,14},{12... | collective-permute-start | bytes 884744 | tf_op jit(solution)/shard_map/ppermute | solution.py:693
  317.7 17.9 %collective-permute-start.31 = (bf16[2,96,768]{2,1,0:T(8,128)(2,1)S(1)}, bf16[2,96,768]{2,1,0:T(8,128)(2,1)S(1)}, u32[]{:S(2)}, u32[]{:S(2)}) collective-permute-start(bf16[2,96,768]{2,1,0:T(8,128)(2,1)S(1)} %sum_third.6.refs_9_.refs_1_.refs_5_), channel_id=1, source_target_pairs={{0,6},{2,0},{4,2},{6,4},{1,7},{3,1},{5,3},{7,5},{8,14},{10,8},{12,... | collective-permute-start | bytes 884744 | tf_op jit(solution)/shard_map/ppermute | solution.py:693
  358.1 16.5 %collective-permute-start.37 = (bf16[4,96,768]{2,1,0:T(8,128)(2,1)S(1)}, bf16[4,96,768]{2,1,0:T(8,128)(2,1)S(1)}, u32[]{:S(2)}, u32[]{:S(2)}) collective-permute-start(bf16[4,96,768]{2,1,0:T(8,128)(2,1)S(1)} %get-tuple-element.194), channel_id=1, source_target_pairs={{0,8},{8,0},{1,9},{9,1},{2,10},{10,2},{3,11},{11,3},{4,12},{12,4},... | collective-permute-start | bytes 1769480 | tf_op jit(solution)/shard_map/ppermute | solution.py:672
  358.5 16.8 %collective-permute-start.35 = (bf16[4,96,768]{2,1,0:T(8,128)(2,1)S(1)}, bf16[4,96,768]{2,1,0:T(8,128)(2,1)S(1)}, u32[]{:S(2)}, u32[]{:S(2)}) collective-permute-start(bf16[4,96,768]{2,1,0:T(8,128)(2,1)S(1)} %get-tuple-element.185.refs_17_), channel_id=1, source_target_pairs={{0,16},{16,0},{1,17},{17,1},{2,18},{18,2},{3,19},{19,3},{4,20},{20... | collective-permute-start | bytes 1769480 | tf_op jit(solution)/shard_map/ppermute | solution.py:672
  375.9 18.4 %collective-permute-start.39 = (bf16[768,768]{1,0:T(8,128)(2,1)S(1)}, bf16[768,768]{1,0:T(8,128)(2,1)}, u32[]{:S(2)}, u32[]{:S(2)}) collective-permute-start(bf16[768,768]{1,0:T(8,128)(2,1)S(1)} %bitcast.113), channel_id=1, source_target_pairs={{0,1},{1,0},{2,3},{3,2},{4,5},{5,4},{6,7},{7,6},{8,9},{9,8},{10,11... | collective-permute-start | bytes 3538952 | tf_op jit(solution)/shard_map/ppermute | solution.py:672
  376.4 30.5 %collective-permute-start.38 = (bf16[768,768]{1,0:T(8,128)(2,1)S(1)}, bf16[768,768]{1,0:T(8,128)(2,1)}, u32[]{:S(2)}, u32[]{:S(2)}) collective-permute-start(bf16[768,768]{1,0:T(8,128)(2,1)S(1)} %bitcast.110), channel_id=1, source_target_pairs={{0,16},{16,0},{1,17},{17,1},{2,18},{18,2},{3,19},{19,3},{4,20},{20... | collective-permute-start | bytes 3538952 | tf_op jit(solution)/shard_map/ppermute | solution.py:672
  376.8 32.6 %collective-permute-start.36 = (bf16[768,768]{1,0:T(8,128)(2,1)S(1)}, bf16[768,768]{1,0:T(8,128)(2,1)S(1)}, u32[]{:S(2)}, u32[]{:S(2)}) collective-permute-start(bf16[768,768]{1,0:T(8,128)(2,1)S(1)} %bitcast.114), channel_id=1, source_target_pairs={{0,8},{8,0},{1,9},{9,1},{2,10},{10,2},{3,11},{11,3},{4,12},{12,4},... | collective-permute-start | bytes 3538952 | tf_op jit(solution)/shard_map/ppermute | solution.py:672
  (71 other events, 475.4 us)
Sparse Core Ops, SparseCore 0:
  182.4 101.3 all-gather.4
  358.2 73.0 all-gather.6

commit v4 on v3

--- a/solution.py
+++ b/solution.py
@@ -871,6 +871,39 @@
         up_ref[0, rows] = (in_ref[0, z, 1] if z_first else in_ref[0, 1, z]).astype(f32)
 
 
+def spread_turned_kernel(where_ref, in_ref, down_ref, up_ref):
+    unit = QUARTER // 4
+    for k in range(4):
+        rows = pl.ds(pl.multiple_of(lax.rem(where_ref[2] - k + 4, 4) * unit, 16), unit)
+        down_ref[0, rows] = in_ref[0, k, 0].astype(f32)
+        up_ref[0, rows] = in_ref[0, k, 1].astype(f32)
+
+
+def place_gathered(blocks, layer, where, deps=()):
+    unit, width = blocks.shape[-2:]
+    hidden = blocks.size // width // 2
+    return invoke(
+        spread_turned_kernel,
+        (blocks,),
+        deps,
+        scalars=(where,),
+        grid=(8,),
+        in_specs=[
+            pl.BlockSpec((1, 4, 2, unit, width), lambda i, w: (i % 4 * 2 + i // 4, 0, 0, 0, 0))
+        ],
+        out_specs=[
+            pl.BlockSpec((1, QUARTER, width), lambda i, w: (layer, i, 0)),
+            pl.BlockSpec((1, QUARTER, TILE), lambda i, w: (layer, i % 2, i // 2)),
+        ],
+        out_shape=[
+            jax.ShapeDtypeStruct((2, hidden, width), f32),
+            jax.ShapeDtypeStruct((2, width, hidden), f32),
+        ],
+        name="spread",
+        us=2,
+    )
+
+
 def place_ordered(rows, layer, before=None, z_first=False, deps=()):
     width = rows.shape[-1]
     hidden = rows.size // width // 2
@@ -1039,7 +1072,7 @@
     if direct:
         mlp2 = sum_third([parts[0]] + ahead, where, (dnm1,))
         wait = (mlp2,)
-        mlp2 = gather_blocks(mlp2)
+        ahead = turns(lambda k: mlp2)
     dnm1, keep, bup_keep = mlp_back_call(
         core_row, nm1, g1, w_up, w_down, 0, kept=(act1, slope1), before=(dnm1,), deps=wait
     )
@@ -1048,7 +1081,9 @@
     if direct:
         one_send, one, two_send, two = sum_cores(keep, got, where)
         one_got, two_got = swaps(one_send, two_send, ("b1", "b0"))
-        wait = (one,)
+        mlp2 = join([v[None] for v in (mlp2, *ahead)], (0,), where, (one,))[0]
+        wait = (mlp2,)
+        mlp2 = lax.all_gather(mlp2, B + (C,), axis=0, tiled=False)
     dq1, dkv1 = attend_back_call(
         first, q1, kv, att1, do1, lse1, tab, None, dkv2, deps=wait + (dnm1,)
     )
@@ -1117,7 +1152,7 @@
         )
         one_far, two_far = swaps(one_near, two_near, ("b1", "b0"))
         one_near_got, two_near_got = swap(one_near, C), swap(two_near, C)
-        grad_down, grad_up = place_ordered(mlp2, 1, z_first=True, deps=(one_near, two_near))
+        grad_down, grad_up = place_gathered(mlp2, 1, where, (one_near, two_near))
         mark = lambda c, v, u: c * 4 + v * 2 + u
         down_map = lambda w: (0, w, 0)
         up_map = lambda w: (0, w % 2, w // 2)

time: 454 us -> 450 us (level)
  waiting for transfers between devices: 127 us -> 114 us
  starting transfers between devices: 72 us -> 78.6 us
    ppermute x18 -> x21, waiting for transfers between devices: 37 us -> 21.4 us  [turns(): lax.ppermute(values_at(k), Z, [(i, (i + k) % size) for i in range(size)])]
    ppermute x18 -> x21, starting transfers between devices: 52.3 us -> 57 us  [turns(): lax.ppermute(values_at(k), Z, [(i, (i + k) % size) for i in range(size)])]
    pallas_call x42 -> x43, Pallas kernels: 204 us -> 206 us  [invoke(): pl.pallas_call(body, grid_spec=pltpu.PrefetchScalarGridSpec(num_scalar_pr...]
    unnamed x119 -> x115, local copies, waits for them, and re-layouts: 21 us -> 21.9 us
  transfers between devices with their start and end apart: 45 -> 48, of which waited for: 20 -> 20; matrix products, arithmetic and copies ran while one was open for 1% -> 1% of each run, Pallas kernels for 35% -> 35%
where the time goes in v4:
time: 450 us; the launch traced here: 445 us
  Pallas kernels  206 us (46%)
  waiting for transfers between devices  114 us (25%)
  starting transfers between devices  78.6 us (17%)
  local copies, waits for them, and re-layouts  24.2 us (5%)
  between operations  15 us (3%)
  other arithmetic  7.23 us (2%)
    pallas_call x43, Pallas kernels, invoke(): pl.pallas_call(body, grid_spec=pltpu.PrefetchScalarGridSpec(num_scalar_pr...  206 us
    ppermute x25, waiting for transfers between devices, swap(): return lax.ppermute(values, axis, PAIR)  84.7 us
    ppermute x21, starting transfers between devices, turns(): lax.ppermute(values_at(k), Z, [(i, (i + k) % size) for i in range(size)])  57 us
    unnamed x115, local copies, waits for them, and re-layouts  21.9 us
    ppermute x25, starting transfers between devices, swap(): return lax.ppermute(values, axis, PAIR)  21.5 us
    ppermute x21, waiting for transfers between devices, turns(): lax.ppermute(values_at(k), Z, [(i, (i + k) % size) for i in range(size)])  21.4 us
  transfers between devices with their start and end apart: 48, of which 20 were waited for; matrix products, arithmetic and copies ran while one was open for 1% of the time, Pallas kernels for 35%

profile of v4, /device:TPU:0, one launch (start us, length us, event | category | flops | bytes accessed | tf_op | source)
XLA Modules:
  0.0 444.8 jit_solution(16277320238157325955)
XLA Ops:
  22.7 11.7 %mlp_fwd.1 = (f32[512,768]{1,0:T(8,128)S(1)}, bf16[512,3072]{1,0:T(8,128)(2,1)}, bf16[512,3072]{1,0:T(8,128)(2,1)}) custom-call(bf16[512,768]{1,0:T(8,128)(2,1)S(1)} %get-tuple-element.108.refs_0_.refs_1_, bf16[2,768,3072]{2,1,0:T(8,128)(2,1)} %refs_3_.13, f32[1,3072]{1,0:T(1,128)S(1)} %get-tuple-element.210.refs_2_, bf16[2,3072,768]{2,1,0:T(8,128)(2,1)} %refs_4_.3), custom_call_target="tpu_custom_call" | custom-call | flops 6000000000 | bytes 10000000 | tf_op jit(solution)/shard_map/mlp_fwd/pallas_call | solution.py:48
  40.4 5.8 %attend.2 = (bf16[512,768]{1,0:T(8,128)(2,1)S(1)}, f32[4,2,8,768]{3,2,1,0:T(8,128)S(1)}) custom-call(s32[9]{0:T(128)S(1)} %pad_add_fusion.refs_0_, bf16[512,768]{1,0:T(8,128)(2,1)S(1)} %copy-done.33, bf16[4,128,512]{2,1,0:T(8,128)(2,1)S(1)} %join.5.refs_2_, bf16[4,128,512]{2,1,0:T(8,128)(2,1)S(1)} %collective-permute-done.3.refs_3_, ...), custom_call_target="tpu_custom_call" | custom-call | flops 35999997952 | bytes 60000000 | tf_op jit(solution)/shard_map/attend/pallas_call | solution.py:48
  46.3 5.5 %middle.1 = (bf16[512,768]{1,0:T(8,128)(2,1)S(1)}, bf16[512,768]{1,0:T(8,128)(2,1)S(1)}, bf16[512,768]{1,0:T(8,128)(2,1)S(1)}, bf16[512,768]{1,0:T(8,128)(2,1)S(1)}) custom-call(bf16[512,768]{1,0:T(8,128)(2,1)S(1)} %get-tuple-element.110.refs_0_.refs_3_.refs_4_, bf16[512,768]{1,0:T(8,128)(2,1)} %bitcast.129, f32[512,768]{1,0:T(8,128)} %copy-done.19, ...), custom_call_target="tpu_custom_call" | custom-call | flops 3000000000 | bytes 5000000 | tf_op jit(solution)/shard_map/middle/pallas_call | solution.py:48
  53.6 14.0 %mlp_both.2 = (f32[512,768]{1,0:T(8,128)S(1)}, f32[512,768]{1,0:T(8,128)}, bf16[2,1536,768]{2,1,0:T(8,128)(2,1)}, f32[1,1536]{1,0:T(1,128)S(1)}) custom-call(s32[1]{0:T(128)} %bitcast.11.refs_0_, bf16[512,768]{1,0:T(8,128)(2,1)S(1)} %get-tuple-element.112.refs_1_, bf16[512,768]{1,0:T(8,128)(2,1)S(1)} %bitcast.122, bf16[2,768,3072]{2,1,0:T(8,128)(2,1)} %refs_3_.13, ...), custom_call_target="tpu_custom_call" | custom-call | flops 24000000000 | bytes 40000000 | tf_op jit(solution)/shard_map/mlp_both/pallas_call | solution.py:48
  70.0 14.4 %mlp_both.3 = (f32[512,768]{1,0:T(8,128)S(1)}, f32[512,768]{1,0:T(8,128)}, bf16[2,1536,768]{2,1,0:T(8,128)(2,1)}, f32[1,1536]{1,0:T(1,128)S(1)}) custom-call(s32[1]{0:T(128)} %bitcast.11.refs_0_, bf16[512,768]{1,0:T(8,128)(2,1)S(1)} %copy-done.29, bf16[512,768]{1,0:T(8,128)(2,1)S(1)} %bitcast.123, bf16[2,768,3072]{2,1,0:T(8,128)(2,1)} %refs_3_.13, ...), custom_call_target="tpu_custom_call" | custom-call | flops 24000000000 | bytes 40000000 | tf_op jit(solution)/shard_map/mlp_both/pallas_call | solution.py:48
  85.7 6.0 %sum_cores.3 = (bf16[2,384,768]{2,1,0:T(8,128)(2,1)S(1)}, bf16[2,384,768]{2,1,0:T(8,128)(2,1)S(1)}, bf16[2,384,768]{2,1,0:T(8,128)(2,1)S(1)}, bf16[2,384,768]{2,1,0:T(8,128)(2,1)}) custom-call(s32[4]{0:T(128)S(1)} %pad_add_fusion.1.refs_0_, bf16[2,2,2,384,768]{4,3,2,1,0:T(8,128)(2,1)} %bitcast.184, ...), custom_call_target="tpu_custom_call" | custom-call | flops 12000000000 | bytes 20000000 | tf_op jit(solution)/shard_map/sum_cores/pallas_call | solution.py:48
  94.8 5.9 %attend.3 = (bf16[512,768]{1,0:T(8,128)(2,1)S(1)}, f32[4,2,8,768]{3,2,1,0:T(8,128)S(1)}) custom-call(s32[9]{0:T(128)S(1)} %pad_add_fusion.refs_0_, bf16[512,768]{1,0:T(8,128)(2,1)S(1)} %copy-done.27, bf16[4,128,512]{2,1,0:T(8,128)(2,1)S(1)} %join.5.refs_2_, bf16[4,128,512]{2,1,0:T(8,128)(2,1)S(1)} %copy-done.13, ...), custom_call_target="tpu_custom_call" | custom-call | flops 35999997952 | bytes 60000000 | tf_op jit(solution)/shard_map/attend/pallas_call | solution.py:48
  100.7 6.0 %attend_back.3 = (bf16[512,768]{1,0:T(8,128)(2,1)S(1)}, f32[1024,512]{1,0:T(8,128)}) custom-call(s32[9]{0:T(128)S(1)} %pad_add_fusion.refs_0_, bf16[512,768]{1,0:T(8,128)(2,1)S(1)} %copy-done.27, bf16[4,128,512]{2,1,0:T(8,128)(2,1)S(1)} %join.5.refs_2_, bf16[4,128,512]{2,1,0:T(8,128)(2,1)S(1)} %copy-done.13, ...), custom_call_target="tpu_custom_call" | custom-call | flops 27000000512 | bytes 45000000 | tf_op jit(solution)/shard_map/attend_back/pallas_call | solution.py:48
  106.6 13.4 %collective-permute-done.5.refs_2_.refs_4_ = bf16[2,384,768]{2,1,0:T(8,128)(2,1)S(1)} collective-permute-done((bf16[2,384,768]{2,1,0:T(8,128)(2,1)S(1)}, bf16[2,384,768]{2,1,0:T(8,128)(2,1)S(1)}, u32[]{:S(2)}, u32[]{:S(2)}) %collective-permute-start.5) | collective-permute-done | bytes 1179680 | tf_op jit(solution)/shard_map/ppermute | solution.py:672
  127.7 6.3 %attend_back.4 = (bf16[512,768]{1,0:T(8,128)(2,1)S(1)}, f32[1024,512]{1,0:T(8,128)}) custom-call(s32[9]{0:T(128)S(1)} %pad_add_fusion.refs_0_, bf16[512,768]{1,0:T(8,128)(2,1)S(1)} %copy-done.27, bf16[4,128,512]{2,1,0:T(8,128)(2,1)S(1)} %join.5.refs_2_, bf16[4,128,512]{2,1,0:T(8,128)(2,1)S(1)} %copy-done.13, ...), custom_call_target="tpu_custom_call", output_to_operand_aliasing={{0}: (8, {}), {1}: (9, {})} | custom-call | flops 27000000512 | bytes 45000000 | tf_op jit(solution)/shard_map/attend_back/pallas_call | solution.py:48
  134.9 5.1 %collective-permute-done.7 = bf16[1,384,768]{2,1,0:T(8,128)(2,1)S(1)} collective-permute-done((bf16[1,384,768]{2,1,0:T(8,128)(2,1)S(1)}, bf16[1,384,768]{2,1,0:T(8,128)(2,1)S(1)}, u32[]{:S(2)}, u32[]{:S(2)}) %collective-permute-start.7) | collective-permute-done | bytes 589856 | tf_op jit(solution)/shard_map/ppermute | solution.py:672
  142.1 7.9 %collective-permute-start.10 = (bf16[2,96,768]{2,1,0:T(8,128)(2,1)S(1)}, bf16[2,96,768]{2,1,0:T(8,128)(2,1)S(1)}, u32[]{:S(2)}, u32[]{:S(2)}) collective-permute-start(bf16[2,96,768]{2,1,0:T(8,128)(2,1)S(1)} %get-tuple-element.142), channel_id=1, source_target_pairs={{0,4},{2,6},{4,0},{6,2},{1,5},{3,7},{5,1},{7,3},{8,12},{10,14},{12... | collective-permute-start | bytes 884744 | tf_op jit(solution)/shard_map/ppermute | solution.py:693
  150.0 7.3 %collective-permute-start.11 = (bf16[2,96,768]{2,1,0:T(8,128)(2,1)S(1)}, bf16[2,96,768]{2,1,0:T(8,128)(2,1)S(1)}, u32[]{:S(2)}, u32[]{:S(2)}) collective-permute-start(bf16[2,96,768]{2,1,0:T(8,128)(2,1)S(1)} %get-tuple-element.143), channel_id=1, source_target_pairs={{0,6},{2,0},{4,2},{6,4},{1,7},{3,1},{5,3},{7,5},{8,14},{10,8},{12,... | collective-permute-start | bytes 884744 | tf_op jit(solution)/shard_map/ppermute | solution.py:693
  157.9 10.8 %turn.1 = (bf16[512,768]{1,0:T(8,128)(2,1)}, bf16[2304,768]{1,0:T(8,128)(2,1)}, bf16[512,768]{1,0:T(8,128)(2,1)S(1)}, bf16[512,768]{1,0:T(8,128)(2,1)S(1)}, f32[8,768]{1,0:T(8,128)S(1)}) custom-call(bf16[512,768]{1,0:T(8,128)(2,1)S(1)} %copy-done.24, f32[512,768]{1,0:T(8,128)} %copy-done.39, bf16[512,768]{1,0:T(8,128)(2,1)S(1)} %copy-done.44, ...), custom_call_target="tpu_custom_call" | custom-call | flops 35999997952 | bytes 60000000 | tf_op jit(solution)/shard_map/turn/pallas_call | solution.py:48
  168.7 11.1 %mlp_back.2 = (f32[512,768]{1,0:T(8,128)S(1)}, bf16[2,1536,768]{2,1,0:T(8,128)(2,1)}, f32[1,1536]{1,0:T(1,128)S(1)}) custom-call(s32[1]{0:T(128)} %bitcast.11.refs_0_, bf16[512,768]{1,0:T(8,128)(2,1)S(1)} %copy-done.3, bf16[512,768]{1,0:T(8,128)(2,1)S(1)} %get-tuple-element.136.refs_2_, bf16[2,768,3072]{2,1,0:T(8,128)(2,1)} %refs_3_.13, ...), custom_call_target="tpu_custom_call" | custom-call | flops 7200000000 | bytes 12000000 | tf_op jit(solution)/shard_map/mlp_back/pallas_call | solution.py:48
  185.3 12.1 %mlp_back.3 = (f32[512,768]{1,0:T(8,128)S(1)}, bf16[2,1536,768]{2,1,0:T(8,128)(2,1)}, f32[1,1536]{1,0:T(1,128)S(1)}) custom-call(s32[1]{0:T(128)} %bitcast.11.refs_0_, bf16[512,768]{1,0:T(8,128)(2,1)S(1)} %copy-done.3, bf16[512,768]{1,0:T(8,128)(2,1)S(1)} %get-tuple-element.136.refs_2_, bf16[2,768,3072]{2,1,0:T(8,128)(2,1)} %refs_3_.13, ...), custom_call_target="tpu_custom_call" | custom-call | flops 89999998976 | bytes 150000000 | tf_op jit(solution)/shard_map/mlp_back/pallas_call | solution.py:48
  198.6 6.3 %sum_cores.4 = (bf16[2,384,768]{2,1,0:T(8,128)(2,1)}, bf16[2,384,768]{2,1,0:T(8,128)(2,1)S(1)}, bf16[2,384,768]{2,1,0:T(8,128)(2,1)S(1)}, bf16[2,384,768]{2,1,0:T(8,128)(2,1)}) custom-call(s32[4]{0:T(128)S(1)} %pad_add_fusion.1.refs_0_, bf16[2,2,2,384,768]{4,3,2,1,0:T(8,128)(2,1)} %bitcast.188, ...), custom_call_target="tpu_custom_call" | custom-call | flops 12000000000 | bytes 20000000 | tf_op jit(solution)/shard_map/sum_cores/pallas_call | solution.py:48
  213.6 9.8 %attend_back.5 = (bf16[512,768]{1,0:T(8,128)(2,1)S(1)}, f32[1024,512]{1,0:T(8,128)}) custom-call(s32[9]{0:T(128)S(1)} %pad_add_fusion.refs_0_, bf16[512,768]{1,0:T(8,128)(2,1)S(1)} %copy-done.34, bf16[4,128,512]{2,1,0:T(8,128)(2,1)S(1)} %join.5.refs_2_, bf16[4,128,512]{2,1,0:T(8,128)(2,1)S(1)} %copy-done.14, bf16[512,768]{1,0:T(8,128)(2,1)S(1)} %copy-done.22, ...), custom_call_target="tpu_custom_call" | custom-call | flops 27000000512 | bytes 45000000 | tf_op jit(solution)/shard_map/attend_back/pallas_call | solution.py:48
  225.6 7.2 %collective-permute-done.17.refs_2_.refs_4_ = bf16[2,384,768]{2,1,0:T(8,128)(2,1)} collective-permute-done((bf16[2,384,768]{2,1,0:T(8,128)(2,1)}, bf16[2,384,768]{2,1,0:T(8,128)(2,1)}, u32[]{:S(2)}, u32[]{:S(2)}) %collective-permute-start.17) | collective-permute-done | bytes 1179680 | tf_op jit(solution)/shard_map/ppermute | solution.py:672
  239.4 9.0 %collective-permute-start.20 = (bf16[1,128,512]{2,1,0:T(8,128)(2,1)}, bf16[1,128,512]{2,1,0:T(8,128)(2,1)}, u32[]{:S(2)}, u32[]{:S(2)}) collective-permute-start(bf16[1,128,512]{2,1,0:T(8,128)(2,1)} %get-tuple-element.159), channel_id=1, source_target_pairs={{0,4},{2,6},{4,0},{6,2},{1,5},{3,7},{5,1},{7,3},{8,12},{10,14},{12... | collective-permute-start | bytes 393224 | tf_op jit(solution)/shard_map/ppermute | solution.py:693
  252.7 5.3 %collective-permute-done.20.refs_3_ = bf16[1,128,512]{2,1,0:T(8,128)(2,1)} collective-permute-done((bf16[1,128,512]{2,1,0:T(8,128)(2,1)}, bf16[1,128,512]{2,1,0:T(8,128)(2,1)}, u32[]{:S(2)}, u32[]{:S(2)}) %collective-permute-start.20) | collective-permute-done | bytes 131104 | tf_op jit(solution)/shard_map/ppermute | solution.py:693
  259.8 7.9 %collective-permute-done.22 = bf16[1,384,768]{2,1,0:T(8,128)(2,1)S(1)} collective-permute-done((bf16[1,384,768]{2,1,0:T(8,128)(2,1)S(1)}, bf16[1,384,768]{2,1,0:T(8,128)(2,1)S(1)}, u32[]{:S(2)}, u32[]{:S(2)}) %collective-permute-start.22) | collective-permute-done | bytes 589856 | tf_op jit(solution)/shard_map/ppermute | solution.py:672
  277.8 8.7 %last.1 = (f32[512,768]{1,0:T(8,128)}, bf16[1792,768]{1,0:T(8,128)(2,1)}, bf16[1792,768]{1,0:T(8,128)(2,1)}) custom-call(s32[1]{0:T(128)} %bitcast.11.refs_0_, bf16[512,768]{1,0:T(8,128)(2,1)S(1)} %bitcast.131, bf16[512,768]{1,0:T(8,128)(2,1)S(1)} %get-tuple-element.136.refs_2_, bf16[512,768]{1,0:T(8,128)(2,1)S(1)} %copy-done.31, ...), custom_call_target="tpu_custom_call" | custom-call | flops 6000000000 | bytes 10000000 | tf_op jit(solution)/shard_map/last/pallas_call | solution.py:48
  286.6 6.0 %collective-permute-done.26.refs_3_ = bf16[2,96,768]{2,1,0:T(8,128)(2,1)S(1)} collective-permute-done((bf16[2,96,768]{2,1,0:T(8,128)(2,1)S(1)}, bf16[2,96,768]{2,1,0:T(8,128)(2,1)S(1)}, u32[]{:S(2)}, u32[]{:S(2)}) %collective-permute-start.26) | collective-permute-done | bytes 294944 | tf_op jit(solution)/shard_map/ppermute | solution.py:693
  301.9 6.6 %collective-permute-start.32 = (bf16[2,96,768]{2,1,0:T(8,128)(2,1)S(1)}, bf16[2,96,768]{2,1,0:T(8,128)(2,1)S(1)}, u32[]{:S(2)}, u32[]{:S(2)}) collective-permute-start(bf16[2,96,768]{2,1,0:T(8,128)(2,1)S(1)} %sum_third.6.refs_9_.refs_1_.refs_5_), channel_id=1, source_target_pairs={{0,2},{2,4},{4,6},{6,0},{1,3},{3,5},{5,7},{7,1},{8,10},{10,12},{12... | collective-permute-start | bytes 884744 | tf_op jit(solution)/shard_map/ppermute | solution.py:693
  310.8 12.7 %collective-permute-done.28.refs_2_.refs_4_ = bf16[2,224,768]{2,1,0:T(8,128)(2,1)S(1)} collective-permute-done((bf16[2,224,768]{2,1,0:T(8,128)(2,1)S(1)}, bf16[2,224,768]{2,1,0:T(8,128)(2,1)S(1)}, u32[]{:S(2)}, u32[]{:S(2)}) %collective-permute-start.28) | collective-permute-done | bytes 688160 | tf_op jit(solution)/shard_map/ppermute | solution.py:672
  329.0 7.1 %collective-permute-done.30 = bf16[1,224,768]{2,1,0:T(8,128)(2,1)S(1)} collective-permute-done((bf16[1,224,768]{2,1,0:T(8,128)(2,1)S(1)}, bf16[1,224,768]{2,1,0:T(8,128)(2,1)S(1)}, u32[]{:S(2)}, u32[]{:S(2)}) %collective-permute-start.30) | collective-permute-done | bytes 344096 | tf_op jit(solution)/shard_map/ppermute | solution.py:672
  355.5 14.4 %collective-permute-done.40 = bf16[4,96,768]{2,1,0:T(8,128)(2,1)S(1)} collective-permute-done((bf16[4,96,768]{2,1,0:T(8,128)(2,1)S(1)}, bf16[4,96,768]{2,1,0:T(8,128)(2,1)S(1)}, u32[]{:S(2)}, u32[]{:S(2)}) %collective-permute-start.40) | collective-permute-done | bytes 589856 | tf_op jit(solution)/shard_map/ppermute | solution.py:672
  374.0 11.9 %spread.1 = (f32[2,3072,768]{2,1,0:T(8,128)}, f32[2,768,3072]{2,1,0:T(8,128)}) custom-call(s32[4]{0:T(128)S(1)} %pad_add_fusion.1.refs_0_, bf16[8,4,2,96,768]{4,3,2,1,0:T(8,128)(2,1)} %bitcast.175, bf16[768,768]{1,0:T(8,128)(2,1)S(1)} %bitcast.118, bf16[768,768]{1,0:T(8,128)(2,1)S(1)} %bitcast.114), custom_call_target="tpu_custom_call" | custom-call | flops 1200000000 | bytes 2000000 | tf_op jit(solution)/shard_map/spread/pallas_call | solution.py:48
  396.1 6.3 %collective-permute-done.41.refs_2_ = bf16[768,768]{1,0:T(8,128)(2,1)} collective-permute-done((bf16[768,768]{1,0:T(8,128)(2,1)S(1)}, bf16[768,768]{1,0:T(8,128)(2,1)}, u32[]{:S(2)}, u32[]{:S(2)}) %collective-permute-start.41) | collective-permute-done | bytes 1179680 | tf_op jit(solution)/shard_map/ppermute | solution.py:672
  419.7 7.7 %all-gather.7.cloned.1.call-done = bf16[64,56,768]{2,1,0:T(8,128)(2,1)} async-done(((bf16[2,56,768]{2,1,0:T(8,128)(2,1)}), bf16[64,56,768]{2,1,0:T(8,128)(2,1)}) %all-gather.7.cloned.1.call-update) | async-done | bytes 5505040 | tf_op jit(solution)/shard_map/all_gather | solution.py:817
  427.4 6.6 %finish.1 = (f32[2,768,768]{2,1,0:T(8,128)}, f32[768,768]{1,0:T(8,128)}, f32[768,896]{1,0:T(8,128)}, f32[128,768]{1,0:T(8,128)S(1)}) custom-call(bf16[32,2,56,768]{3,2,1,0:T(8,128)(2,1)} %bitcast.181), custom_call_target="tpu_custom_call" | custom-call | flops 3600000000 | bytes 6000000 | tf_op jit(solution)/shard_map/finish/pallas_call | solution.py:48
  (261 shorter events, 152.9 us)
Async XLA Ops:
  7.2 345.0 %all-gather.5.cloned.1.call-start = ((), (), s32[]{:S(2)}) async-start(), calls=%async_computation | async-start | bytes 10616832 | tf_op jit(solution)/shard_map/all_gather | solution.py:1086
  15.1 20.5 %collective-permute-start = (bf16[128,512]{1,0:T(8,128)(2,1)S(1)}, bf16[128,512]{1,0:T(8,128)(2,1)S(1)}, u32[]{:S(2)}, u32[]{:S(2)}) collective-permute-start(bf16[128,512]{1,0:T(8,128)(2,1)S(1)} %get-tuple-element.107), channel_id=1, source_target_pairs={{0,2},{2,4},{4,6},{6,0},{1,3},{3,5},{5,7},{7,1},{8,10},{10,12},{12... | collective-permute-start | bytes 393224 | tf_op jit(solution)/shard_map/ppermute | solution.py:693
  18.2 17.5 %collective-permute-start.1 = (bf16[128,512]{1,0:T(8,128)(2,1)S(1)}, bf16[128,512]{1,0:T(8,128)(2,1)S(1)}, u32[]{:S(2)}, u32[]{:S(2)}) collective-permute-start(bf16[128,512]{1,0:T(8,128)(2,1)S(1)} %get-tuple-element.107), channel_id=1, source_target_pairs={{0,4},{2,6},{4,0},{6,2},{1,5},{3,7},{5,1},{7,3},{8,12},{10,14},{12... | collective-permute-start | bytes 393224 | tf_op jit(solution)/shard_map/ppermute | solution.py:693
  68.8 16.9 %collective-permute-start.4 = (bf16[3072,768]{1,0:T(8,128)(2,1)}, bf16[3072,768]{1,0:T(8,128)(2,1)}, u32[]{:S(2)}, u32[]{:S(2)}) collective-permute-start(bf16[3072,768]{1,0:T(8,128)(2,1)} %bitcast.183), channel_id=1, source_target_pairs={{0,1},{1,0},{2,3},{3,2},{4,5},{5,4},{6,7},{7,6},{8,9},{9,8},{10,11... | collective-permute-start | bytes 14155784 | tf_op jit(solution)/shard_map/ppermute | solution.py:672
  91.7 28.3 %collective-permute-start.5 = (bf16[2,384,768]{2,1,0:T(8,128)(2,1)S(1)}, bf16[2,384,768]{2,1,0:T(8,128)(2,1)S(1)}, u32[]{:S(2)}, u32[]{:S(2)}) collective-permute-start(bf16[2,384,768]{2,1,0:T(8,128)(2,1)S(1)} %get-tuple-element.125), channel_id=1, source_target_pairs={{0,8},{8,0},{1,9},{9,1},{2,10},{10,2},{3,11},{11,3},{4,12},{12,4},... | collective-permute-start | bytes 3538952 | tf_op jit(solution)/shard_map/ppermute | solution.py:672
  93.3 28.0 %collective-permute-start.6 = (bf16[2,384,768]{2,1,0:T(8,128)(2,1)S(1)}, bf16[2,384,768]{2,1,0:T(8,128)(2,1)S(1)}, u32[]{:S(2)}, u32[]{:S(2)}) collective-permute-start(bf16[2,384,768]{2,1,0:T(8,128)(2,1)S(1)} %get-tuple-element.127), channel_id=1, source_target_pairs={{0,16},{16,0},{1,17},{17,1},{2,18},{18,2},{3,19},{19,3},{4,20},{20... | collective-permute-start | bytes 3538952 | tf_op jit(solution)/shard_map/ppermute | solution.py:672
  142.1 37.7 %collective-permute-start.10 = (bf16[2,96,768]{2,1,0:T(8,128)(2,1)S(1)}, bf16[2,96,768]{2,1,0:T(8,128)(2,1)S(1)}, u32[]{:S(2)}, u32[]{:S(2)}) collective-permute-start(bf16[2,96,768]{2,1,0:T(8,128)(2,1)S(1)} %get-tuple-element.142), channel_id=1, source_target_pairs={{0,4},{2,6},{4,0},{6,2},{1,5},{3,7},{5,1},{7,3},{8,12},{10,14},{12... | collective-permute-start | bytes 884744 | tf_op jit(solution)/shard_map/ppermute | solution.py:693
  150.0 29.8 %collective-permute-start.11 = (bf16[2,96,768]{2,1,0:T(8,128)(2,1)S(1)}, bf16[2,96,768]{2,1,0:T(8,128)(2,1)S(1)}, u32[]{:S(2)}, u32[]{:S(2)}) collective-permute-start(bf16[2,96,768]{2,1,0:T(8,128)(2,1)S(1)} %get-tuple-element.143), channel_id=1, source_target_pairs={{0,6},{2,0},{4,2},{6,4},{1,7},{3,1},{5,3},{7,5},{8,14},{10,8},{12,... | collective-permute-start | bytes 884744 | tf_op jit(solution)/shard_map/ppermute | solution.py:693
  157.4 22.5 %collective-permute-start.9 = (bf16[2,96,768]{2,1,0:T(8,128)(2,1)S(1)}, bf16[2,96,768]{2,1,0:T(8,128)(2,1)S(1)}, u32[]{:S(2)}, u32[]{:S(2)}) collective-permute-start(bf16[2,96,768]{2,1,0:T(8,128)(2,1)S(1)} %get-tuple-element.141), channel_id=1, source_target_pairs={{0,2},{2,4},{4,6},{6,0},{1,3},{3,5},{5,7},{7,1},{8,10},{10,12},{12... | collective-permute-start | bytes 884744 | tf_op jit(solution)/shard_map/ppermute | solution.py:693
  179.8 18.8 %collective-permute-start.15 = (bf16[3072,768]{1,0:T(8,128)(2,1)}, bf16[3072,768]{1,0:T(8,128)(2,1)}, u32[]{:S(2)}, u32[]{:S(2)}) collective-permute-start(bf16[3072,768]{1,0:T(8,128)(2,1)} %bitcast.182), channel_id=1, source_target_pairs={{0,1},{1,0},{2,3},{3,2},{4,5},{5,4},{6,7},{7,6},{8,9},{9,8},{10,11... | collective-permute-start | bytes 14155784 | tf_op jit(solution)/shard_map/ppermute | solution.py:672
  180.9 26.9 %collective-permute-start.12 = (bf16[2,96,768]{2,1,0:T(8,128)(2,1)S(1)}, bf16[2,96,768]{2,1,0:T(8,128)(2,1)S(1)}, u32[]{:S(2)}, u32[]{:S(2)}) collective-permute-start(bf16[2,96,768]{2,1,0:T(8,128)(2,1)S(1)} %sum_third.4.refs_8_), channel_id=1, source_target_pairs={{0,2},{2,4},{4,6},{6,0},{1,3},{3,5},{5,7},{7,1},{8,10},{10,12},{12... | collective-permute-start | bytes 884744 | tf_op jit(solution)/shard_map/ppermute | solution.py:693
  182.9 24.8 %collective-permute-start.13 = (bf16[2,96,768]{2,1,0:T(8,128)(2,1)S(1)}, bf16[2,96,768]{2,1,0:T(8,128)(2,1)S(1)}, u32[]{:S(2)}, u32[]{:S(2)}) collective-permute-start(bf16[2,96,768]{2,1,0:T(8,128)(2,1)S(1)} %sum_third.4.refs_8_), channel_id=1, source_target_pairs={{0,4},{2,6},{4,0},{6,2},{1,5},{3,7},{5,1},{7,3},{8,12},{10,14},{12... | collective-permute-start | bytes 884744 | tf_op jit(solution)/shard_map/ppermute | solution.py:693
  184.8 23.0 %collective-permute-start.14 = (bf16[2,96,768]{2,1,0:T(8,128)(2,1)S(1)}, bf16[2,96,768]{2,1,0:T(8,128)(2,1)S(1)}, u32[]{:S(2)}, u32[]{:S(2)}) collective-permute-start(bf16[2,96,768]{2,1,0:T(8,128)(2,1)S(1)} %sum_third.4.refs_8_), channel_id=1, source_target_pairs={{0,6},{2,0},{4,2},{6,4},{1,7},{3,1},{5,3},{7,5},{8,14},{10,8},{12,... | collective-permute-start | bytes 884744 | tf_op jit(solution)/shard_map/ppermute | solution.py:693
  204.9 27.9 %collective-permute-start.17 = (bf16[2,384,768]{2,1,0:T(8,128)(2,1)}, bf16[2,384,768]{2,1,0:T(8,128)(2,1)}, u32[]{:S(2)}, u32[]{:S(2)}) collective-permute-start(bf16[2,384,768]{2,1,0:T(8,128)(2,1)} %get-tuple-element.153), channel_id=1, source_target_pairs={{0,8},{8,0},{1,9},{9,1},{2,10},{10,2},{3,11},{11,3},{4,12},{12,4},... | collective-permute-start | bytes 3538952 | tf_op jit(solution)/shard_map/ppermute | solution.py:672
  206.2 27.4 %collective-permute-start.18 = (bf16[2,384,768]{2,1,0:T(8,128)(2,1)S(1)}, bf16[2,384,768]{2,1,0:T(8,128)(2,1)}, u32[]{:S(2)}, u32[]{:S(2)}) collective-permute-start(bf16[2,384,768]{2,1,0:T(8,128)(2,1)S(1)} %get-tuple-element.155), channel_id=1, source_target_pairs={{0,16},{16,0},{1,17},{17,1},{2,18},{18,2},{3,19},{19,3},{4,20},{20... | collective-permute-start | bytes 3538952 | tf_op jit(solution)/shard_map/ppermute | solution.py:672
  239.4 18.6 %collective-permute-start.20 = (bf16[1,128,512]{2,1,0:T(8,128)(2,1)}, bf16[1,128,512]{2,1,0:T(8,128)(2,1)}, u32[]{:S(2)}, u32[]{:S(2)}) collective-permute-start(bf16[1,128,512]{2,1,0:T(8,128)(2,1)} %get-tuple-element.159), channel_id=1, source_target_pairs={{0,4},{2,6},{4,0},{6,2},{1,5},{3,7},{5,1},{7,3},{8,12},{10,14},{12... | collective-permute-start | bytes 393224 | tf_op jit(solution)/shard_map/ppermute | solution.py:693
  248.5 19.2 %collective-permute-start.22 = (bf16[1,384,768]{2,1,0:T(8,128)(2,1)S(1)}, bf16[1,384,768]{2,1,0:T(8,128)(2,1)S(1)}, u32[]{:S(2)}, u32[]{:S(2)}) collective-permute-start(bf16[1,384,768]{2,1,0:T(8,128)(2,1)S(1)} %get-tuple-element.167), channel_id=1, source_target_pairs={{0,16},{16,0},{1,17},{17,1},{2,18},{18,2},{3,19},{19,3},{4,20},{20... | collective-permute-start | bytes 1769480 | tf_op jit(solution)/shard_map/ppermute | solution.py:672
  249.9 21.0 %collective-permute-start.23 = (bf16[1,384,768]{2,1,0:T(8,128)(2,1)S(1)}, bf16[1,384,768]{2,1,0:T(8,128)(2,1)}, u32[]{:S(2)}, u32[]{:S(2)}) collective-permute-start(bf16[1,384,768]{2,1,0:T(8,128)(2,1)S(1)} %get-tuple-element.169), channel_id=1, source_target_pairs={{0,8},{8,0},{1,9},{9,1},{2,10},{10,2},{3,11},{11,3},{4,12},{12,4},... | collective-permute-start | bytes 1769480 | tf_op jit(solution)/shard_map/ppermute | solution.py:672
  251.4 176.0 %all-gather.7.cloned.1.call-start = ((), (), s32[]{:S(2)}) async-start(), calls=%async_computation.1 | async-start | bytes 5677056 | tf_op jit(solution)/shard_map/all_gather | solution.py:817
  275.4 17.2 %collective-permute-start.26 = (bf16[2,96,768]{2,1,0:T(8,128)(2,1)S(1)}, bf16[2,96,768]{2,1,0:T(8,128)(2,1)S(1)}, u32[]{:S(2)}, u32[]{:S(2)}) collective-permute-start(bf16[2,96,768]{2,1,0:T(8,128)(2,1)S(1)} %get-tuple-element.175), channel_id=1, source_target_pairs={{0,4},{2,6},{4,0},{6,2},{1,5},{3,7},{5,1},{7,3},{8,12},{10,14},{12... | collective-permute-start | bytes 884744 | tf_op jit(solution)/shard_map/ppermute | solution.py:693
  275.4 17.2 %collective-permute-start.27 = (bf16[2,96,768]{2,1,0:T(8,128)(2,1)S(1)}, bf16[2,96,768]{2,1,0:T(8,128)(2,1)S(1)}, u32[]{:S(2)}, u32[]{:S(2)}) collective-permute-start(bf16[2,96,768]{2,1,0:T(8,128)(2,1)S(1)} %get-tuple-element.176), channel_id=1, source_target_pairs={{0,6},{2,0},{4,2},{6,4},{1,7},{3,1},{5,3},{7,5},{8,14},{10,8},{12,... | collective-permute-start | bytes 884744 | tf_op jit(solution)/shard_map/ppermute | solution.py:693
  299.2 24.3 %collective-permute-start.28 = (bf16[2,224,768]{2,1,0:T(8,128)(2,1)S(1)}, bf16[2,224,768]{2,1,0:T(8,128)(2,1)S(1)}, u32[]{:S(2)}, u32[]{:S(2)}) collective-permute-start(bf16[2,224,768]{2,1,0:T(8,128)(2,1)S(1)} %get-tuple-element.178), channel_id=1, source_target_pairs={{0,8},{8,0},{1,9},{9,1},{2,10},{10,2},{3,11},{11,3},{4,12},{12,4},... | collective-permute-start | bytes 2064392 | tf_op jit(solution)/shard_map/ppermute | solution.py:672
  301.9 21.6 %collective-permute-start.29 = (bf16[2,224,768]{2,1,0:T(8,128)(2,1)S(1)}, bf16[2,224,768]{2,1,0:T(8,128)(2,1)S(1)}, u32[]{:S(2)}, u32[]{:S(2)}) collective-permute-start(bf16[2,224,768]{2,1,0:T(8,128)(2,1)S(1)} %get-tuple-element.180), channel_id=1, source_target_pairs={{0,16},{16,0},{1,17},{17,1},{2,18},{18,2},{3,19},{19,3},{4,20},{20... | collective-permute-start | bytes 2064392 | tf_op jit(solution)/shard_map/ppermute | solution.py:672
  301.9 26.5 %collective-permute-start.32 = (bf16[2,96,768]{2,1,0:T(8,128)(2,1)S(1)}, bf16[2,96,768]{2,1,0:T(8,128)(2,1)S(1)}, u32[]{:S(2)}, u32[]{:S(2)}) collective-permute-start(bf16[2,96,768]{2,1,0:T(8,128)(2,1)S(1)} %sum_third.6.refs_9_.refs_1_.refs_5_), channel_id=1, source_target_pairs={{0,2},{2,4},{4,6},{6,0},{1,3},{3,5},{5,7},{7,1},{8,10},{10,12},{12... | collective-permute-start | bytes 884744 | tf_op jit(solution)/shard_map/ppermute | solution.py:693
  308.5 19.9 %collective-permute-start.33 = (bf16[2,96,768]{2,1,0:T(8,128)(2,1)S(1)}, bf16[2,96,768]{2,1,0:T(8,128)(2,1)S(1)}, u32[]{:S(2)}, u32[]{:S(2)}) collective-permute-start(bf16[2,96,768]{2,1,0:T(8,128)(2,1)S(1)} %sum_third.6.refs_9_.refs_1_.refs_5_), channel_id=1, source_target_pairs={{0,4},{2,6},{4,0},{6,2},{1,5},{3,7},{5,1},{7,3},{8,12},{10,14},{12... | collective-permute-start | bytes 884744 | tf_op jit(solution)/shard_map/ppermute | solution.py:693
  308.6 19.8 %collective-permute-start.34 = (bf16[2,96,768]{2,1,0:T(8,128)(2,1)S(1)}, bf16[2,96,768]{2,1,0:T(8,128)(2,1)S(1)}, u32[]{:S(2)}, u32[]{:S(2)}) collective-permute-start(bf16[2,96,768]{2,1,0:T(8,128)(2,1)S(1)} %sum_third.6.refs_9_.refs_1_.refs_5_), channel_id=1, source_target_pairs={{0,6},{2,0},{4,2},{6,4},{1,7},{3,1},{5,3},{7,5},{8,14},{10,8},{12,... | collective-permute-start | bytes 884744 | tf_op jit(solution)/shard_map/ppermute | solution.py:693
  353.5 16.5 %collective-permute-start.40 = (bf16[4,96,768]{2,1,0:T(8,128)(2,1)S(1)}, bf16[4,96,768]{2,1,0:T(8,128)(2,1)S(1)}, u32[]{:S(2)}, u32[]{:S(2)}) collective-permute-start(bf16[4,96,768]{2,1,0:T(8,128)(2,1)S(1)} %get-tuple-element.194), channel_id=1, source_target_pairs={{0,8},{8,0},{1,9},{9,1},{2,10},{10,2},{3,11},{11,3},{4,12},{12,4},... | collective-permute-start | bytes 1769480 | tf_op jit(solution)/shard_map/ppermute | solution.py:672
  354.2 16.4 %collective-permute-start.38 = (bf16[4,96,768]{2,1,0:T(8,128)(2,1)S(1)}, bf16[4,96,768]{2,1,0:T(8,128)(2,1)S(1)}, u32[]{:S(2)}, u32[]{:S(2)}) collective-permute-start(bf16[4,96,768]{2,1,0:T(8,128)(2,1)S(1)} %get-tuple-element.185.refs_17_), channel_id=1, source_target_pairs={{0,16},{16,0},{1,17},{17,1},{2,18},{18,2},{3,19},{19,3},{4,20},{20... | collective-permute-start | bytes 1769480 | tf_op jit(solution)/shard_map/ppermute | solution.py:672
  370.5 15.3 %collective-permute-start.43 = (bf16[768,768]{1,0:T(8,128)(2,1)S(1)}, bf16[768,768]{1,0:T(8,128)(2,1)}, u32[]{:S(2)}, u32[]{:S(2)}) collective-permute-start(bf16[768,768]{1,0:T(8,128)(2,1)S(1)} %bitcast.112), channel_id=1, source_target_pairs={{0,1},{1,0},{2,3},{3,2},{4,5},{5,4},{6,7},{7,6},{8,9},{9,8},{10,11... | collective-permute-start | bytes 3538952 | tf_op jit(solution)/shard_map/ppermute | solution.py:672
  371.3 19.7 %collective-permute-start.42 = (bf16[768,768]{1,0:T(8,128)(2,1)S(1)}, bf16[768,768]{1,0:T(8,128)(2,1)}, u32[]{:S(2)}, u32[]{:S(2)}) collective-permute-start(bf16[768,768]{1,0:T(8,128)(2,1)S(1)} %bitcast.116), channel_id=1, source_target_pairs={{0,1},{1,0},{2,3},{3,2},{4,5},{5,4},{6,7},{7,6},{8,9},{9,8},{10,11... | collective-permute-start | bytes 3538952 | tf_op jit(solution)/shard_map/ppermute | solution.py:672
  371.8 30.5 %collective-permute-start.41 = (bf16[768,768]{1,0:T(8,128)(2,1)S(1)}, bf16[768,768]{1,0:T(8,128)(2,1)}, u32[]{:S(2)}, u32[]{:S(2)}) collective-permute-start(bf16[768,768]{1,0:T(8,128)(2,1)S(1)} %bitcast.113), channel_id=1, source_target_pairs={{0,16},{16,0},{1,17},{17,1},{2,18},{18,2},{3,19},{19,3},{4,20},{20... | collective-permute-start | bytes 3538952 | tf_op jit(solution)/shard_map/ppermute | solution.py:672
  372.5 32.8 %collective-permute-start.39 = (bf16[768,768]{1,0:T(8,128)(2,1)S(1)}, bf16[768,768]{1,0:T(8,128)(2,1)S(1)}, u32[]{:S(2)}, u32[]{:S(2)}) collective-permute-start(bf16[768,768]{1,0:T(8,128)(2,1)S(1)} %bitcast.117), channel_id=1, source_target_pairs={{0,8},{8,0},{1,9},{9,1},{2,10},{10,2},{3,11},{11,3},{4,12},{12,4},... | collective-permute-start | bytes 3538952 | tf_op jit(solution)/shard_map/ppermute | solution.py:672
  (72 other events, 464.3 us)
Sparse Core Ops, SparseCore 0:
  251.5 65.0 all-gather.4
  353.6 73.7 all-gather.6

commit v5 on v4

--- a/solution.py
+++ b/solution.py
@@ -384,7 +384,7 @@
     ins = 5 if has_start else 4
     refs = refs[:ins] + refs[ins + unread :]
     if has_start:
-        o_ref, do_ref, lse_ref, tab_ref, start_ref, dq_out, dkv_ref, k0, k1, v0, v1, t0, t1, dq_ref = refs
+        o_ref, do_ref, lse_ref, tab_ref, start_ref, dq_out, low_ref, k0, k1, v0, v1, t0, t1, dq_ref, dkv_ref = refs
         dkv_ref[...] = start_ref[...]
     else:
         o_ref, do_ref, lse_ref, tab_ref, dq_out, dkv_ref, k0, k1, v0, v1, t0, t1, dq_ref = refs
@@ -428,6 +428,8 @@
         return carry
 
     lax.fori_loop(0, full, step, 0)
+    if has_start:
+        low_ref[...] = dkv_ref[...].astype(bf16)
     cos_tab, sin_low, sin_high = tab_ref[0], -tab_ref[1], -tab_ref[2]
     dq = dq_ref[...].T * SCALE
     for p in range(q_ref.shape[1] // 128):
@@ -467,10 +469,11 @@
         out_specs=[tok_spec, len_spec],
         scratch=[pltpu.VMEM((length, 128), bf16)] * 4
         + [pltpu.VMEM((length // 128, 128, 128), bf16)] * 2
-        + [pltpu.VMEM((128, rows), f32)],
+        + [pltpu.VMEM((128, rows), f32)]
+        + ([] if start is None else [pltpu.VMEM((length, 128), f32)]),
         out_shape=[
             jax.ShapeDtypeStruct((tokens, width), bf16),
-            jax.ShapeDtypeStruct((length, seqs * 128), f32),
+            jax.ShapeDtypeStruct((length, seqs * 128), f32 if start is None else bf16),
         ],
         aliases={1 + len(operands) + i: i for i in range(len(before))},
         name="attend_back",

time: 450 us -> 449 us (level)
    unnamed x115 -> x117, local copies, waits for them, and re-layouts: 21.9 us -> 21.9 us
  transfers between devices with their start and end apart: 48 -> 48, of which waited for: 20 -> 20; matrix products, arithmetic and copies ran while one was open for 1% -> 0% of each run, Pallas kernels for 35% -> 35%
where the time goes in v5:
time: 449 us; the launch traced here: 444 us
  Pallas kernels  206 us (46%)
  waiting for transfers between devices  114 us (25%)
  starting transfers between devices  78 us (17%)
  local copies, waits for them, and re-layouts  25.5 us (6%)
  between operations  15 us (3%)
  other arithmetic  5.23 us (1%)
    pallas_call x43, Pallas kernels, invoke(): pl.pallas_call(body, grid_spec=pltpu.PrefetchScalarGridSpec(num_scalar_pr...  206 us
    ppermute x25, waiting for transfers between devices, swap(): return lax.ppermute(values, axis, PAIR)  85.4 us
    ppermute x21, starting transfers between devices, turns(): lax.ppermute(values_at(k), Z, [(i, (i + k) % size) for i in range(size)])  56.5 us
    unnamed x117, local copies, waits for them, and re-layouts  21.9 us
    ppermute x25, starting transfers between devices, swap(): return lax.ppermute(values, axis, PAIR)  21.5 us
    ppermute x21, waiting for transfers between devices, turns(): lax.ppermute(values_at(k), Z, [(i, (i + k) % size) for i in range(size)])  21.3 us
  transfers between devices with their start and end apart: 48, of which 20 were waited for; matrix products, arithmetic and copies ran while one was open for 0% of the time, Pallas kernels for 35%

profile of v5, /device:TPU:0, one launch (start us, length us, event | category | flops | bytes accessed | tf_op | source)
XLA Modules:
  0.0 443.9 jit_solution(4583852435403056392)
XLA Ops:
  22.7 11.6 %mlp_fwd.1 = (f32[512,768]{1,0:T(8,128)S(1)}, bf16[512,3072]{1,0:T(8,128)(2,1)}, bf16[512,3072]{1,0:T(8,128)(2,1)}) custom-call(bf16[512,768]{1,0:T(8,128)(2,1)S(1)} %get-tuple-element.108.refs_0_.refs_1_, bf16[2,768,3072]{2,1,0:T(8,128)(2,1)} %refs_3_.13, f32[1,3072]{1,0:T(1,128)S(1)} %get-tuple-element.210.refs_2_, bf16[2,3072,768]{2,1,0:T(8,128)(2,1)} %refs_4_.3), custom_call_target="tpu_custom_call" | custom-call | flops 6000000000 | bytes 10000000 | tf_op jit(solution)/shard_map/mlp_fwd/pallas_call | solution.py:48
  40.2 5.8 %attend.2 = (bf16[512,768]{1,0:T(8,128)(2,1)S(1)}, f32[4,2,8,768]{3,2,1,0:T(8,128)S(1)}) custom-call(s32[9]{0:T(128)S(1)} %pad_add_fusion.refs_0_, bf16[512,768]{1,0:T(8,128)(2,1)S(1)} %copy-done.34, bf16[4,128,512]{2,1,0:T(8,128)(2,1)S(1)} %join.5.refs_2_, bf16[4,128,512]{2,1,0:T(8,128)(2,1)S(1)} %collective-permute-done.3.refs_3_, ...), custom_call_target="tpu_custom_call" | custom-call | flops 35999997952 | bytes 60000000 | tf_op jit(solution)/shard_map/attend/pallas_call | solution.py:48
  46.1 5.5 %middle.1 = (bf16[512,768]{1,0:T(8,128)(2,1)S(1)}, bf16[512,768]{1,0:T(8,128)(2,1)S(1)}, bf16[512,768]{1,0:T(8,128)(2,1)S(1)}, bf16[512,768]{1,0:T(8,128)(2,1)S(1)}) custom-call(bf16[512,768]{1,0:T(8,128)(2,1)S(1)} %get-tuple-element.110.refs_0_.refs_3_.refs_4_, bf16[512,768]{1,0:T(8,128)(2,1)} %bitcast.129, f32[512,768]{1,0:T(8,128)} %copy-done.20, ...), custom_call_target="tpu_custom_call" | custom-call | flops 3000000000 | bytes 5000000 | tf_op jit(solution)/shard_map/middle/pallas_call | solution.py:48
  53.5 14.0 %mlp_both.2 = (f32[512,768]{1,0:T(8,128)S(1)}, f32[512,768]{1,0:T(8,128)}, bf16[2,1536,768]{2,1,0:T(8,128)(2,1)}, f32[1,1536]{1,0:T(1,128)S(1)}) custom-call(s32[1]{0:T(128)} %bitcast.11.refs_0_, bf16[512,768]{1,0:T(8,128)(2,1)S(1)} %get-tuple-element.112.refs_1_, bf16[512,768]{1,0:T(8,128)(2,1)S(1)} %bitcast.122, bf16[2,768,3072]{2,1,0:T(8,128)(2,1)} %refs_3_.13, ...), custom_call_target="tpu_custom_call" | custom-call | flops 24000000000 | bytes 40000000 | tf_op jit(solution)/shard_map/mlp_both/pallas_call | solution.py:48
  69.8 14.4 %mlp_both.3 = (f32[512,768]{1,0:T(8,128)S(1)}, f32[512,768]{1,0:T(8,128)}, bf16[2,1536,768]{2,1,0:T(8,128)(2,1)}, f32[1,1536]{1,0:T(1,128)S(1)}) custom-call(s32[1]{0:T(128)} %bitcast.11.refs_0_, bf16[512,768]{1,0:T(8,128)(2,1)S(1)} %copy-done.30, bf16[512,768]{1,0:T(8,128)(2,1)S(1)} %bitcast.123, bf16[2,768,3072]{2,1,0:T(8,128)(2,1)} %refs_3_.13, ...), custom_call_target="tpu_custom_call" | custom-call | flops 24000000000 | bytes 40000000 | tf_op jit(solution)/shard_map/mlp_both/pallas_call | solution.py:48
  85.5 6.0 %sum_cores.3 = (bf16[2,384,768]{2,1,0:T(8,128)(2,1)S(1)}, bf16[2,384,768]{2,1,0:T(8,128)(2,1)S(1)}, bf16[2,384,768]{2,1,0:T(8,128)(2,1)S(1)}, bf16[2,384,768]{2,1,0:T(8,128)(2,1)}) custom-call(s32[4]{0:T(128)S(1)} %pad_add_fusion.1.refs_0_, bf16[2,2,2,384,768]{4,3,2,1,0:T(8,128)(2,1)} %bitcast.184, ...), custom_call_target="tpu_custom_call" | custom-call | flops 12000000000 | bytes 20000000 | tf_op jit(solution)/shard_map/sum_cores/pallas_call | solution.py:48
  94.6 5.9 %attend.3 = (bf16[512,768]{1,0:T(8,128)(2,1)S(1)}, f32[4,2,8,768]{3,2,1,0:T(8,128)S(1)}) custom-call(s32[9]{0:T(128)S(1)} %pad_add_fusion.refs_0_, bf16[512,768]{1,0:T(8,128)(2,1)S(1)} %copy-done.28, bf16[4,128,512]{2,1,0:T(8,128)(2,1)S(1)} %join.5.refs_2_, bf16[4,128,512]{2,1,0:T(8,128)(2,1)S(1)} %copy-done.14, ...), custom_call_target="tpu_custom_call" | custom-call | flops 35999997952 | bytes 60000000 | tf_op jit(solution)/shard_map/attend/pallas_call | solution.py:48
  100.5 6.0 %attend_back.3 = (bf16[512,768]{1,0:T(8,128)(2,1)S(1)}, f32[1024,512]{1,0:T(8,128)}) custom-call(s32[9]{0:T(128)S(1)} %pad_add_fusion.refs_0_, bf16[512,768]{1,0:T(8,128)(2,1)S(1)} %copy-done.28, bf16[4,128,512]{2,1,0:T(8,128)(2,1)S(1)} %join.5.refs_2_, bf16[4,128,512]{2,1,0:T(8,128)(2,1)S(1)} %copy-done.14, ...), custom_call_target="tpu_custom_call" | custom-call | flops 27000000512 | bytes 45000000 | tf_op jit(solution)/shard_map/attend_back/pallas_call | solution.py:48
  106.5 13.4 %collective-permute-done.5.refs_2_.refs_4_ = bf16[2,384,768]{2,1,0:T(8,128)(2,1)S(1)} collective-permute-done((bf16[2,384,768]{2,1,0:T(8,128)(2,1)S(1)}, bf16[2,384,768]{2,1,0:T(8,128)(2,1)S(1)}, u32[]{:S(2)}, u32[]{:S(2)}) %collective-permute-start.5) | collective-permute-done | bytes 1179680 | tf_op jit(solution)/shard_map/ppermute | solution.py:675
  127.5 6.3 %attend_back.4 = (bf16[512,768]{1,0:T(8,128)(2,1)S(1)}, f32[1024,512]{1,0:T(8,128)}) custom-call(s32[9]{0:T(128)S(1)} %pad_add_fusion.refs_0_, bf16[512,768]{1,0:T(8,128)(2,1)S(1)} %copy-done.28, bf16[4,128,512]{2,1,0:T(8,128)(2,1)S(1)} %join.5.refs_2_, bf16[4,128,512]{2,1,0:T(8,128)(2,1)S(1)} %copy-done.14, ...), custom_call_target="tpu_custom_call", output_to_operand_aliasing={{0}: (8, {}), {1}: (9, {})} | custom-call | flops 27000000512 | bytes 45000000 | tf_op jit(solution)/shard_map/attend_back/pallas_call | solution.py:48
  134.7 5.2 %collective-permute-done.7 = bf16[1,384,768]{2,1,0:T(8,128)(2,1)S(1)} collective-permute-done((bf16[1,384,768]{2,1,0:T(8,128)(2,1)S(1)}, bf16[1,384,768]{2,1,0:T(8,128)(2,1)S(1)}, u32[]{:S(2)}, u32[]{:S(2)}) %collective-permute-start.7) | collective-permute-done | bytes 589856 | tf_op jit(solution)/shard_map/ppermute | solution.py:675
  141.9 7.9 %collective-permute-start.10 = (bf16[2,96,768]{2,1,0:T(8,128)(2,1)S(1)}, bf16[2,96,768]{2,1,0:T(8,128)(2,1)S(1)}, u32[]{:S(2)}, u32[]{:S(2)}) collective-permute-start(bf16[2,96,768]{2,1,0:T(8,128)(2,1)S(1)} %get-tuple-element.142), channel_id=1, source_target_pairs={{0,4},{2,6},{4,0},{6,2},{1,5},{3,7},{5,1},{7,3},{8,12},{10,14},{12... | collective-permute-start | bytes 884744 | tf_op jit(solution)/shard_map/ppermute | solution.py:696
  149.8 7.3 %collective-permute-start.11 = (bf16[2,96,768]{2,1,0:T(8,128)(2,1)S(1)}, bf16[2,96,768]{2,1,0:T(8,128)(2,1)S(1)}, u32[]{:S(2)}, u32[]{:S(2)}) collective-permute-start(bf16[2,96,768]{2,1,0:T(8,128)(2,1)S(1)} %get-tuple-element.143), channel_id=1, source_target_pairs={{0,6},{2,0},{4,2},{6,4},{1,7},{3,1},{5,3},{7,5},{8,14},{10,8},{12,... | collective-permute-start | bytes 884744 | tf_op jit(solution)/shard_map/ppermute | solution.py:696
  157.7 10.8 %turn.1 = (bf16[512,768]{1,0:T(8,128)(2,1)}, bf16[2304,768]{1,0:T(8,128)(2,1)}, bf16[512,768]{1,0:T(8,128)(2,1)S(1)}, bf16[512,768]{1,0:T(8,128)(2,1)S(1)}, f32[8,768]{1,0:T(8,128)S(1)}) custom-call(bf16[512,768]{1,0:T(8,128)(2,1)S(1)} %copy-done.25, f32[512,768]{1,0:T(8,128)} %copy-done.40, bf16[512,768]{1,0:T(8,128)(2,1)S(1)} %copy-done.45, ...), custom_call_target="tpu_custom_call" | custom-call | flops 35999997952 | bytes 60000000 | tf_op jit(solution)/shard_map/turn/pallas_call | solution.py:48
  168.5 11.1 %mlp_back.2 = (f32[512,768]{1,0:T(8,128)S(1)}, bf16[2,1536,768]{2,1,0:T(8,128)(2,1)}, f32[1,1536]{1,0:T(1,128)S(1)}) custom-call(s32[1]{0:T(128)} %bitcast.11.refs_0_, bf16[512,768]{1,0:T(8,128)(2,1)S(1)} %copy-done.4, bf16[512,768]{1,0:T(8,128)(2,1)S(1)} %get-tuple-element.136.refs_2_, bf16[2,768,3072]{2,1,0:T(8,128)(2,1)} %refs_3_.13, ...), custom_call_target="tpu_custom_call" | custom-call | flops 7200000000 | bytes 12000000 | tf_op jit(solution)/shard_map/mlp_back/pallas_call | solution.py:48
  185.1 12.1 %mlp_back.3 = (f32[512,768]{1,0:T(8,128)S(1)}, bf16[2,1536,768]{2,1,0:T(8,128)(2,1)}, f32[1,1536]{1,0:T(1,128)S(1)}) custom-call(s32[1]{0:T(128)} %bitcast.11.refs_0_, bf16[512,768]{1,0:T(8,128)(2,1)S(1)} %copy-done.4, bf16[512,768]{1,0:T(8,128)(2,1)S(1)} %get-tuple-element.136.refs_2_, bf16[2,768,3072]{2,1,0:T(8,128)(2,1)} %refs_3_.13, ...), custom_call_target="tpu_custom_call" | custom-call | flops 89999998976 | bytes 150000000 | tf_op jit(solution)/shard_map/mlp_back/pallas_call | solution.py:48
  198.4 6.3 %sum_cores.4 = (bf16[2,384,768]{2,1,0:T(8,128)(2,1)}, bf16[2,384,768]{2,1,0:T(8,128)(2,1)S(1)}, bf16[2,384,768]{2,1,0:T(8,128)(2,1)S(1)}, bf16[2,384,768]{2,1,0:T(8,128)(2,1)}) custom-call(s32[4]{0:T(128)S(1)} %pad_add_fusion.1.refs_0_, bf16[2,2,2,384,768]{4,3,2,1,0:T(8,128)(2,1)} %bitcast.188, ...), custom_call_target="tpu_custom_call" | custom-call | flops 12000000000 | bytes 20000000 | tf_op jit(solution)/shard_map/sum_cores/pallas_call | solution.py:48
  213.4 9.9 %attend_back.5 = (bf16[512,768]{1,0:T(8,128)(2,1)S(1)}, bf16[1024,512]{1,0:T(8,128)(2,1)}) custom-call(s32[9]{0:T(128)S(1)} %pad_add_fusion.refs_0_, bf16[512,768]{1,0:T(8,128)(2,1)S(1)} %copy-done.35, bf16[4,128,512]{2,1,0:T(8,128)(2,1)S(1)} %join.5.refs_2_, bf16[4,128,512]{2,1,0:T(8,128)(2,1)S(1)} %copy-done.15, bf16[512,768]{1,0:T(8,128)(2,1)S(1)} %copy-done.23, ...), custom_call_target="tpu_custom_call" | custom-call | flops 27000000512 | bytes 45000000 | tf_op jit(solution)/shard_map/attend_back/pallas_call | solution.py:48
  224.8 7.8 %collective-permute-done.17.refs_2_.refs_4_ = bf16[2,384,768]{2,1,0:T(8,128)(2,1)} collective-permute-done((bf16[2,384,768]{2,1,0:T(8,128)(2,1)}, bf16[2,384,768]{2,1,0:T(8,128)(2,1)}, u32[]{:S(2)}, u32[]{:S(2)}) %collective-permute-start.17) | collective-permute-done | bytes 1179680 | tf_op jit(solution)/shard_map/ppermute | solution.py:675
  239.2 8.4 %collective-permute-start.20 = (bf16[1,128,512]{2,1,0:T(8,128)(2,1)}, bf16[1,128,512]{2,1,0:T(8,128)(2,1)}, u32[]{:S(2)}, u32[]{:S(2)}) collective-permute-start(bf16[1,128,512]{2,1,0:T(8,128)(2,1)} %get-tuple-element.159), channel_id=1, source_target_pairs={{0,4},{2,6},{4,0},{6,2},{1,5},{3,7},{5,1},{7,3},{8,12},{10,14},{12... | collective-permute-start | bytes 393224 | tf_op jit(solution)/shard_map/ppermute | solution.py:696
  251.8 5.3 %collective-permute-done.20.refs_3_ = bf16[1,128,512]{2,1,0:T(8,128)(2,1)} collective-permute-done((bf16[1,128,512]{2,1,0:T(8,128)(2,1)}, bf16[1,128,512]{2,1,0:T(8,128)(2,1)}, u32[]{:S(2)}, u32[]{:S(2)}) %collective-permute-start.20) | collective-permute-done | bytes 131104 | tf_op jit(solution)/shard_map/ppermute | solution.py:696
  258.9 7.9 %collective-permute-done.22 = bf16[1,384,768]{2,1,0:T(8,128)(2,1)S(1)} collective-permute-done((bf16[1,384,768]{2,1,0:T(8,128)(2,1)S(1)}, bf16[1,384,768]{2,1,0:T(8,128)(2,1)S(1)}, u32[]{:S(2)}, u32[]{:S(2)}) %collective-permute-start.22) | collective-permute-done | bytes 589856 | tf_op jit(solution)/shard_map/ppermute | solution.py:675
  277.0 8.7 %last.1 = (f32[512,768]{1,0:T(8,128)}, bf16[1792,768]{1,0:T(8,128)(2,1)}, bf16[1792,768]{1,0:T(8,128)(2,1)}) custom-call(s32[1]{0:T(128)} %bitcast.11.refs_0_, bf16[512,768]{1,0:T(8,128)(2,1)S(1)} %bitcast.131, bf16[512,768]{1,0:T(8,128)(2,1)S(1)} %get-tuple-element.136.refs_2_, bf16[512,768]{1,0:T(8,128)(2,1)S(1)} %copy-done.32, ...), custom_call_target="tpu_custom_call" | custom-call | flops 6000000000 | bytes 10000000 | tf_op jit(solution)/shard_map/last/pallas_call | solution.py:48
  285.7 6.0 %collective-permute-done.26.refs_3_ = bf16[2,96,768]{2,1,0:T(8,128)(2,1)S(1)} collective-permute-done((bf16[2,96,768]{2,1,0:T(8,128)(2,1)S(1)}, bf16[2,96,768]{2,1,0:T(8,128)(2,1)S(1)}, u32[]{:S(2)}, u32[]{:S(2)}) %collective-permute-start.26) | collective-permute-done | bytes 294944 | tf_op jit(solution)/shard_map/ppermute | solution.py:696
  301.1 6.6 %collective-permute-start.32 = (bf16[2,96,768]{2,1,0:T(8,128)(2,1)S(1)}, bf16[2,96,768]{2,1,0:T(8,128)(2,1)S(1)}, u32[]{:S(2)}, u32[]{:S(2)}) collective-permute-start(bf16[2,96,768]{2,1,0:T(8,128)(2,1)S(1)} %sum_third.6.refs_9_.refs_1_.refs_5_), channel_id=1, source_target_pairs={{0,2},{2,4},{4,6},{6,0},{1,3},{3,5},{5,7},{7,1},{8,10},{10,12},{12... | collective-permute-start | bytes 884744 | tf_op jit(solution)/shard_map/ppermute | solution.py:696
  310.0 12.7 %collective-permute-done.28.refs_2_.refs_4_ = bf16[2,224,768]{2,1,0:T(8,128)(2,1)S(1)} collective-permute-done((bf16[2,224,768]{2,1,0:T(8,128)(2,1)S(1)}, bf16[2,224,768]{2,1,0:T(8,128)(2,1)S(1)}, u32[]{:S(2)}, u32[]{:S(2)}) %collective-permute-start.28) | collective-permute-done | bytes 688160 | tf_op jit(solution)/shard_map/ppermute | solution.py:675
  328.2 7.1 %collective-permute-done.30 = bf16[1,224,768]{2,1,0:T(8,128)(2,1)S(1)} collective-permute-done((bf16[1,224,768]{2,1,0:T(8,128)(2,1)S(1)}, bf16[1,224,768]{2,1,0:T(8,128)(2,1)S(1)}, u32[]{:S(2)}, u32[]{:S(2)}) %collective-permute-start.30) | collective-permute-done | bytes 344096 | tf_op jit(solution)/shard_map/ppermute | solution.py:675
  354.7 14.4 %collective-permute-done.40 = bf16[4,96,768]{2,1,0:T(8,128)(2,1)S(1)} collective-permute-done((bf16[4,96,768]{2,1,0:T(8,128)(2,1)S(1)}, bf16[4,96,768]{2,1,0:T(8,128)(2,1)S(1)}, u32[]{:S(2)}, u32[]{:S(2)}) %collective-permute-start.40) | collective-permute-done | bytes 589856 | tf_op jit(solution)/shard_map/ppermute | solution.py:675
  373.1 11.9 %spread.1 = (f32[2,3072,768]{2,1,0:T(8,128)}, f32[2,768,3072]{2,1,0:T(8,128)}) custom-call(s32[4]{0:T(128)S(1)} %pad_add_fusion.1.refs_0_, bf16[8,4,2,96,768]{4,3,2,1,0:T(8,128)(2,1)} %bitcast.175, bf16[768,768]{1,0:T(8,128)(2,1)S(1)} %bitcast.118, bf16[768,768]{1,0:T(8,128)(2,1)S(1)} %bitcast.114), custom_call_target="tpu_custom_call" | custom-call | flops 1200000000 | bytes 2000000 | tf_op jit(solution)/shard_map/spread/pallas_call | solution.py:48
  395.2 6.2 %collective-permute-done.41.refs_2_ = bf16[768,768]{1,0:T(8,128)(2,1)} collective-permute-done((bf16[768,768]{1,0:T(8,128)(2,1)S(1)}, bf16[768,768]{1,0:T(8,128)(2,1)}, u32[]{:S(2)}, u32[]{:S(2)}) %collective-permute-start.41) | collective-permute-done | bytes 1179680 | tf_op jit(solution)/shard_map/ppermute | solution.py:675
  418.9 7.7 %all-gather.7.cloned.1.call-done = bf16[64,56,768]{2,1,0:T(8,128)(2,1)} async-done(((bf16[2,56,768]{2,1,0:T(8,128)(2,1)}), bf16[64,56,768]{2,1,0:T(8,128)(2,1)}) %all-gather.7.cloned.1.call-update) | async-done | bytes 5505040 | tf_op jit(solution)/shard_map/all_gather | solution.py:820
  426.6 6.6 %finish.1 = (f32[2,768,768]{2,1,0:T(8,128)}, f32[768,768]{1,0:T(8,128)}, f32[768,896]{1,0:T(8,128)}, f32[128,768]{1,0:T(8,128)S(1)}) custom-call(bf16[32,2,56,768]{3,2,1,0:T(8,128)(2,1)} %bitcast.181), custom_call_target="tpu_custom_call" | custom-call | flops 3600000000 | bytes 6000000 | tf_op jit(solution)/shard_map/finish/pallas_call | solution.py:48
  (262 shorter events, 152.1 us)
Async XLA Ops:
  7.2 344.1 %all-gather.5.cloned.1.call-start = ((), (), s32[]{:S(2)}) async-start(), calls=%async_computation | async-start | bytes 10616832 | tf_op jit(solution)/shard_map/all_gather | solution.py:1089
  15.1 20.3 %collective-permute-start = (bf16[128,512]{1,0:T(8,128)(2,1)S(1)}, bf16[128,512]{1,0:T(8,128)(2,1)S(1)}, u32[]{:S(2)}, u32[]{:S(2)}) collective-permute-start(bf16[128,512]{1,0:T(8,128)(2,1)S(1)} %get-tuple-element.107), channel_id=1, source_target_pairs={{0,2},{2,4},{4,6},{6,0},{1,3},{3,5},{5,7},{7,1},{8,10},{10,12},{12... | collective-permute-start | bytes 393224 | tf_op jit(solution)/shard_map/ppermute | solution.py:696
  18.2 17.3 %collective-permute-start.1 = (bf16[128,512]{1,0:T(8,128)(2,1)S(1)}, bf16[128,512]{1,0:T(8,128)(2,1)S(1)}, u32[]{:S(2)}, u32[]{:S(2)}) collective-permute-start(bf16[128,512]{1,0:T(8,128)(2,1)S(1)} %get-tuple-element.107), channel_id=1, source_target_pairs={{0,4},{2,6},{4,0},{6,2},{1,5},{3,7},{5,1},{7,3},{8,12},{10,14},{12... | collective-permute-start | bytes 393224 | tf_op jit(solution)/shard_map/ppermute | solution.py:696
  68.6 16.9 %collective-permute-start.4 = (bf16[3072,768]{1,0:T(8,128)(2,1)}, bf16[3072,768]{1,0:T(8,128)(2,1)}, u32[]{:S(2)}, u32[]{:S(2)}) collective-permute-start(bf16[3072,768]{1,0:T(8,128)(2,1)} %bitcast.183), channel_id=1, source_target_pairs={{0,1},{1,0},{2,3},{3,2},{4,5},{5,4},{6,7},{7,6},{8,9},{9,8},{10,11... | collective-permute-start | bytes 14155784 | tf_op jit(solution)/shard_map/ppermute | solution.py:675
  91.5 28.3 %collective-permute-start.5 = (bf16[2,384,768]{2,1,0:T(8,128)(2,1)S(1)}, bf16[2,384,768]{2,1,0:T(8,128)(2,1)S(1)}, u32[]{:S(2)}, u32[]{:S(2)}) collective-permute-start(bf16[2,384,768]{2,1,0:T(8,128)(2,1)S(1)} %get-tuple-element.125), channel_id=1, source_target_pairs={{0,8},{8,0},{1,9},{9,1},{2,10},{10,2},{3,11},{11,3},{4,12},{12,4},... | collective-permute-start | bytes 3538952 | tf_op jit(solution)/shard_map/ppermute | solution.py:675
  93.1 28.0 %collective-permute-start.6 = (bf16[2,384,768]{2,1,0:T(8,128)(2,1)S(1)}, bf16[2,384,768]{2,1,0:T(8,128)(2,1)S(1)}, u32[]{:S(2)}, u32[]{:S(2)}) collective-permute-start(bf16[2,384,768]{2,1,0:T(8,128)(2,1)S(1)} %get-tuple-element.127), channel_id=1, source_target_pairs={{0,16},{16,0},{1,17},{17,1},{2,18},{18,2},{3,19},{19,3},{4,20},{20... | collective-permute-start | bytes 3538952 | tf_op jit(solution)/shard_map/ppermute | solution.py:675
  141.9 37.7 %collective-permute-start.10 = (bf16[2,96,768]{2,1,0:T(8,128)(2,1)S(1)}, bf16[2,96,768]{2,1,0:T(8,128)(2,1)S(1)}, u32[]{:S(2)}, u32[]{:S(2)}) collective-permute-start(bf16[2,96,768]{2,1,0:T(8,128)(2,1)S(1)} %get-tuple-element.142), channel_id=1, source_target_pairs={{0,4},{2,6},{4,0},{6,2},{1,5},{3,7},{5,1},{7,3},{8,12},{10,14},{12... | collective-permute-start | bytes 884744 | tf_op jit(solution)/shard_map/ppermute | solution.py:696
  149.8 29.8 %collective-permute-start.11 = (bf16[2,96,768]{2,1,0:T(8,128)(2,1)S(1)}, bf16[2,96,768]{2,1,0:T(8,128)(2,1)S(1)}, u32[]{:S(2)}, u32[]{:S(2)}) collective-permute-start(bf16[2,96,768]{2,1,0:T(8,128)(2,1)S(1)} %get-tuple-element.143), channel_id=1, source_target_pairs={{0,6},{2,0},{4,2},{6,4},{1,7},{3,1},{5,3},{7,5},{8,14},{10,8},{12,... | collective-permute-start | bytes 884744 | tf_op jit(solution)/shard_map/ppermute | solution.py:696
  157.2 22.5 %collective-permute-start.9 = (bf16[2,96,768]{2,1,0:T(8,128)(2,1)S(1)}, bf16[2,96,768]{2,1,0:T(8,128)(2,1)S(1)}, u32[]{:S(2)}, u32[]{:S(2)}) collective-permute-start(bf16[2,96,768]{2,1,0:T(8,128)(2,1)S(1)} %get-tuple-element.141), channel_id=1, source_target_pairs={{0,2},{2,4},{4,6},{6,0},{1,3},{3,5},{5,7},{7,1},{8,10},{10,12},{12... | collective-permute-start | bytes 884744 | tf_op jit(solution)/shard_map/ppermute | solution.py:696
  179.6 18.8 %collective-permute-start.15 = (bf16[3072,768]{1,0:T(8,128)(2,1)}, bf16[3072,768]{1,0:T(8,128)(2,1)}, u32[]{:S(2)}, u32[]{:S(2)}) collective-permute-start(bf16[3072,768]{1,0:T(8,128)(2,1)} %bitcast.182), channel_id=1, source_target_pairs={{0,1},{1,0},{2,3},{3,2},{4,5},{5,4},{6,7},{7,6},{8,9},{9,8},{10,11... | collective-permute-start | bytes 14155784 | tf_op jit(solution)/shard_map/ppermute | solution.py:675
  180.7 26.8 %collective-permute-start.12 = (bf16[2,96,768]{2,1,0:T(8,128)(2,1)S(1)}, bf16[2,96,768]{2,1,0:T(8,128)(2,1)S(1)}, u32[]{:S(2)}, u32[]{:S(2)}) collective-permute-start(bf16[2,96,768]{2,1,0:T(8,128)(2,1)S(1)} %sum_third.4.refs_8_), channel_id=1, source_target_pairs={{0,2},{2,4},{4,6},{6,0},{1,3},{3,5},{5,7},{7,1},{8,10},{10,12},{12... | collective-permute-start | bytes 884744 | tf_op jit(solution)/shard_map/ppermute | solution.py:696
  182.7 24.8 %collective-permute-start.13 = (bf16[2,96,768]{2,1,0:T(8,128)(2,1)S(1)}, bf16[2,96,768]{2,1,0:T(8,128)(2,1)S(1)}, u32[]{:S(2)}, u32[]{:S(2)}) collective-permute-start(bf16[2,96,768]{2,1,0:T(8,128)(2,1)S(1)} %sum_third.4.refs_8_), channel_id=1, source_target_pairs={{0,4},{2,6},{4,0},{6,2},{1,5},{3,7},{5,1},{7,3},{8,12},{10,14},{12... | collective-permute-start | bytes 884744 | tf_op jit(solution)/shard_map/ppermute | solution.py:696
  184.6 23.0 %collective-permute-start.14 = (bf16[2,96,768]{2,1,0:T(8,128)(2,1)S(1)}, bf16[2,96,768]{2,1,0:T(8,128)(2,1)S(1)}, u32[]{:S(2)}, u32[]{:S(2)}) collective-permute-start(bf16[2,96,768]{2,1,0:T(8,128)(2,1)S(1)} %sum_third.4.refs_8_), channel_id=1, source_target_pairs={{0,6},{2,0},{4,2},{6,4},{1,7},{3,1},{5,3},{7,5},{8,14},{10,8},{12,... | collective-permute-start | bytes 884744 | tf_op jit(solution)/shard_map/ppermute | solution.py:696
  204.7 27.9 %collective-permute-start.17 = (bf16[2,384,768]{2,1,0:T(8,128)(2,1)}, bf16[2,384,768]{2,1,0:T(8,128)(2,1)}, u32[]{:S(2)}, u32[]{:S(2)}) collective-permute-start(bf16[2,384,768]{2,1,0:T(8,128)(2,1)} %get-tuple-element.153), channel_id=1, source_target_pairs={{0,8},{8,0},{1,9},{9,1},{2,10},{10,2},{3,11},{11,3},{4,12},{12,4},... | collective-permute-start | bytes 3538952 | tf_op jit(solution)/shard_map/ppermute | solution.py:675
  206.0 27.4 %collective-permute-start.18 = (bf16[2,384,768]{2,1,0:T(8,128)(2,1)S(1)}, bf16[2,384,768]{2,1,0:T(8,128)(2,1)}, u32[]{:S(2)}, u32[]{:S(2)}) collective-permute-start(bf16[2,384,768]{2,1,0:T(8,128)(2,1)S(1)} %get-tuple-element.155), channel_id=1, source_target_pairs={{0,16},{16,0},{1,17},{17,1},{2,18},{18,2},{3,19},{19,3},{4,20},{20... | collective-permute-start | bytes 3538952 | tf_op jit(solution)/shard_map/ppermute | solution.py:675
  239.2 18.0 %collective-permute-start.20 = (bf16[1,128,512]{2,1,0:T(8,128)(2,1)}, bf16[1,128,512]{2,1,0:T(8,128)(2,1)}, u32[]{:S(2)}, u32[]{:S(2)}) collective-permute-start(bf16[1,128,512]{2,1,0:T(8,128)(2,1)} %get-tuple-element.159), channel_id=1, source_target_pairs={{0,4},{2,6},{4,0},{6,2},{1,5},{3,7},{5,1},{7,3},{8,12},{10,14},{12... | collective-permute-start | bytes 393224 | tf_op jit(solution)/shard_map/ppermute | solution.py:696
  247.6 19.3 %collective-permute-start.22 = (bf16[1,384,768]{2,1,0:T(8,128)(2,1)S(1)}, bf16[1,384,768]{2,1,0:T(8,128)(2,1)S(1)}, u32[]{:S(2)}, u32[]{:S(2)}) collective-permute-start(bf16[1,384,768]{2,1,0:T(8,128)(2,1)S(1)} %get-tuple-element.167), channel_id=1, source_target_pairs={{0,16},{16,0},{1,17},{17,1},{2,18},{18,2},{3,19},{19,3},{4,20},{20... | collective-permute-start | bytes 1769480 | tf_op jit(solution)/shard_map/ppermute | solution.py:675
  249.1 21.0 %collective-permute-start.23 = (bf16[1,384,768]{2,1,0:T(8,128)(2,1)S(1)}, bf16[1,384,768]{2,1,0:T(8,128)(2,1)}, u32[]{:S(2)}, u32[]{:S(2)}) collective-permute-start(bf16[1,384,768]{2,1,0:T(8,128)(2,1)S(1)} %get-tuple-element.169), channel_id=1, source_target_pairs={{0,8},{8,0},{1,9},{9,1},{2,10},{10,2},{3,11},{11,3},{4,12},{12,4},... | collective-permute-start | bytes 1769480 | tf_op jit(solution)/shard_map/ppermute | solution.py:675
  250.6 176.0 %all-gather.7.cloned.1.call-start = ((), (), s32[]{:S(2)}) async-start(), calls=%async_computation.1 | async-start | bytes 5677056 | tf_op jit(solution)/shard_map/all_gather | solution.py:820
  274.6 17.2 %collective-permute-start.26 = (bf16[2,96,768]{2,1,0:T(8,128)(2,1)S(1)}, bf16[2,96,768]{2,1,0:T(8,128)(2,1)S(1)}, u32[]{:S(2)}, u32[]{:S(2)}) collective-permute-start(bf16[2,96,768]{2,1,0:T(8,128)(2,1)S(1)} %get-tuple-element.175), channel_id=1, source_target_pairs={{0,4},{2,6},{4,0},{6,2},{1,5},{3,7},{5,1},{7,3},{8,12},{10,14},{12... | collective-permute-start | bytes 884744 | tf_op jit(solution)/shard_map/ppermute | solution.py:696
  274.6 17.2 %collective-permute-start.27 = (bf16[2,96,768]{2,1,0:T(8,128)(2,1)S(1)}, bf16[2,96,768]{2,1,0:T(8,128)(2,1)S(1)}, u32[]{:S(2)}, u32[]{:S(2)}) collective-permute-start(bf16[2,96,768]{2,1,0:T(8,128)(2,1)S(1)} %get-tuple-element.176), channel_id=1, source_target_pairs={{0,6},{2,0},{4,2},{6,4},{1,7},{3,1},{5,3},{7,5},{8,14},{10,8},{12,... | collective-permute-start | bytes 884744 | tf_op jit(solution)/shard_map/ppermute | solution.py:696
  298.3 24.3 %collective-permute-start.28 = (bf16[2,224,768]{2,1,0:T(8,128)(2,1)S(1)}, bf16[2,224,768]{2,1,0:T(8,128)(2,1)S(1)}, u32[]{:S(2)}, u32[]{:S(2)}) collective-permute-start(bf16[2,224,768]{2,1,0:T(8,128)(2,1)S(1)} %get-tuple-element.178), channel_id=1, source_target_pairs={{0,8},{8,0},{1,9},{9,1},{2,10},{10,2},{3,11},{11,3},{4,12},{12,4},... | collective-permute-start | bytes 2064392 | tf_op jit(solution)/shard_map/ppermute | solution.py:675
  301.1 21.6 %collective-permute-start.29 = (bf16[2,224,768]{2,1,0:T(8,128)(2,1)S(1)}, bf16[2,224,768]{2,1,0:T(8,128)(2,1)S(1)}, u32[]{:S(2)}, u32[]{:S(2)}) collective-permute-start(bf16[2,224,768]{2,1,0:T(8,128)(2,1)S(1)} %get-tuple-element.180), channel_id=1, source_target_pairs={{0,16},{16,0},{1,17},{17,1},{2,18},{18,2},{3,19},{19,3},{4,20},{20... | collective-permute-start | bytes 2064392 | tf_op jit(solution)/shard_map/ppermute | solution.py:675
  301.1 26.5 %collective-permute-start.32 = (bf16[2,96,768]{2,1,0:T(8,128)(2,1)S(1)}, bf16[2,96,768]{2,1,0:T(8,128)(2,1)S(1)}, u32[]{:S(2)}, u32[]{:S(2)}) collective-permute-start(bf16[2,96,768]{2,1,0:T(8,128)(2,1)S(1)} %sum_third.6.refs_9_.refs_1_.refs_5_), channel_id=1, source_target_pairs={{0,2},{2,4},{4,6},{6,0},{1,3},{3,5},{5,7},{7,1},{8,10},{10,12},{12... | collective-permute-start | bytes 884744 | tf_op jit(solution)/shard_map/ppermute | solution.py:696
  307.6 19.9 %collective-permute-start.33 = (bf16[2,96,768]{2,1,0:T(8,128)(2,1)S(1)}, bf16[2,96,768]{2,1,0:T(8,128)(2,1)S(1)}, u32[]{:S(2)}, u32[]{:S(2)}) collective-permute-start(bf16[2,96,768]{2,1,0:T(8,128)(2,1)S(1)} %sum_third.6.refs_9_.refs_1_.refs_5_), channel_id=1, source_target_pairs={{0,4},{2,6},{4,0},{6,2},{1,5},{3,7},{5,1},{7,3},{8,12},{10,14},{12... | collective-permute-start | bytes 884744 | tf_op jit(solution)/shard_map/ppermute | solution.py:696
  307.8 19.8 %collective-permute-start.34 = (bf16[2,96,768]{2,1,0:T(8,128)(2,1)S(1)}, bf16[2,96,768]{2,1,0:T(8,128)(2,1)S(1)}, u32[]{:S(2)}, u32[]{:S(2)}) collective-permute-start(bf16[2,96,768]{2,1,0:T(8,128)(2,1)S(1)} %sum_third.6.refs_9_.refs_1_.refs_5_), channel_id=1, source_target_pairs={{0,6},{2,0},{4,2},{6,4},{1,7},{3,1},{5,3},{7,5},{8,14},{10,8},{12,... | collective-permute-start | bytes 884744 | tf_op jit(solution)/shard_map/ppermute | solution.py:696
  352.6 16.5 %collective-permute-start.40 = (bf16[4,96,768]{2,1,0:T(8,128)(2,1)S(1)}, bf16[4,96,768]{2,1,0:T(8,128)(2,1)S(1)}, u32[]{:S(2)}, u32[]{:S(2)}) collective-permute-start(bf16[4,96,768]{2,1,0:T(8,128)(2,1)S(1)} %get-tuple-element.194), channel_id=1, source_target_pairs={{0,8},{8,0},{1,9},{9,1},{2,10},{10,2},{3,11},{11,3},{4,12},{12,4},... | collective-permute-start | bytes 1769480 | tf_op jit(solution)/shard_map/ppermute | solution.py:675
  353.4 16.4 %collective-permute-start.38 = (bf16[4,96,768]{2,1,0:T(8,128)(2,1)S(1)}, bf16[4,96,768]{2,1,0:T(8,128)(2,1)S(1)}, u32[]{:S(2)}, u32[]{:S(2)}) collective-permute-start(bf16[4,96,768]{2,1,0:T(8,128)(2,1)S(1)} %get-tuple-element.185.refs_17_), channel_id=1, source_target_pairs={{0,16},{16,0},{1,17},{17,1},{2,18},{18,2},{3,19},{19,3},{4,20},{20... | collective-permute-start | bytes 1769480 | tf_op jit(solution)/shard_map/ppermute | solution.py:675
  369.7 15.3 %collective-permute-start.43 = (bf16[768,768]{1,0:T(8,128)(2,1)S(1)}, bf16[768,768]{1,0:T(8,128)(2,1)}, u32[]{:S(2)}, u32[]{:S(2)}) collective-permute-start(bf16[768,768]{1,0:T(8,128)(2,1)S(1)} %bitcast.112), channel_id=1, source_target_pairs={{0,1},{1,0},{2,3},{3,2},{4,5},{5,4},{6,7},{7,6},{8,9},{9,8},{10,11... | collective-permute-start | bytes 3538952 | tf_op jit(solution)/shard_map/ppermute | solution.py:675
  370.4 19.7 %collective-permute-start.42 = (bf16[768,768]{1,0:T(8,128)(2,1)S(1)}, bf16[768,768]{1,0:T(8,128)(2,1)}, u32[]{:S(2)}, u32[]{:S(2)}) collective-permute-start(bf16[768,768]{1,0:T(8,128)(2,1)S(1)} %bitcast.116), channel_id=1, source_target_pairs={{0,1},{1,0},{2,3},{3,2},{4,5},{5,4},{6,7},{7,6},{8,9},{9,8},{10,11... | collective-permute-start | bytes 3538952 | tf_op jit(solution)/shard_map/ppermute | solution.py:675
  371.0 30.5 %collective-permute-start.41 = (bf16[768,768]{1,0:T(8,128)(2,1)S(1)}, bf16[768,768]{1,0:T(8,128)(2,1)}, u32[]{:S(2)}, u32[]{:S(2)}) collective-permute-start(bf16[768,768]{1,0:T(8,128)(2,1)S(1)} %bitcast.113), channel_id=1, source_target_pairs={{0,16},{16,0},{1,17},{17,1},{2,18},{18,2},{3,19},{19,3},{4,20},{20... | collective-permute-start | bytes 3538952 | tf_op jit(solution)/shard_map/ppermute | solution.py:675
  371.7 32.8 %collective-permute-start.39 = (bf16[768,768]{1,0:T(8,128)(2,1)S(1)}, bf16[768,768]{1,0:T(8,128)(2,1)S(1)}, u32[]{:S(2)}, u32[]{:S(2)}) collective-permute-start(bf16[768,768]{1,0:T(8,128)(2,1)S(1)} %bitcast.117), channel_id=1, source_target_pairs={{0,8},{8,0},{1,9},{9,1},{2,10},{10,2},{3,11},{11,3},{4,12},{12,4},... | collective-permute-start | bytes 3538952 | tf_op jit(solution)/shard_map/ppermute | solution.py:675
  (73 other events, 470.0 us)
Sparse Core Ops, SparseCore 0:
  250.7 65.0 all-gather.4
  352.7 73.7 all-gather.6
